TPU v7x, 32 devices: a whole 2x2x4 slice. The times are simulated.
32 devices in a mesh: dp: 8 (over y, x, core), text: 4 (over z).
Axes of the slice: x: 2, y: 2, z: 4, core: 2. Of those that a mesh axis runs over, the one named last changes fastest.
Arguments:
- latents: float32 [16, 1024, 64], P('dp', 'text'), may hold values from -6 to 6
- noise_field: float32 [16, 1024, 64], P('dp', 'text'), may hold values from -6 to 6
- timesteps: int32 [16], P('dp'), may hold values from 0 to 255
- text_tokens: bfloat16 [16, 128, 768], P('dp', 'text'), may hold values from -6 to 6
- text_lengths: int32 [16], P('dp'), may hold values from 4 to 128, as said below
- negatives: int32 [16, 15], P('dp'), may hold values from 0 to 15, as said below
- assignment: int32 [256], replicated, may hold values from 0 to 255, as said below
- end_weights: float32 [1536, 2, 64], P(('dp', 'text')), as said below
- time_table: float32 [256, 1536], P(('dp', 'text')), may hold values from -0.375 to 0.375
- square_slots: float32 [256, 192, 192], P(('dp', 'text')), as said below
- cross_weights: float32 [1536, 2, 1536], P(('dp', 'text')), as said below
- key_value: float32 [768, 3072], P(('dp', 'text')), may hold values from -0.21875 to 0.21875
- gate_up: float32 [1536, 12288], P(('dp', 'text')), may hold values from -0.15625 to 0.15625
- down_weight: float32 [6144, 1536], P(('dp', 'text')), may hold values from -0.078125 to 0.078125
- norm_gains: float32 [1536, 3], P(('dp', 'text')), as said below
- first_ends: float32 [1536, 2, 64], P(('dp', 'text')), may hold values from -4.7683716e-07 to 4.7683716e-07
- second_ends: float32 [1536, 2, 64], P(('dp', 'text')), may hold values from 5.504055e-16 to 2.201622e-15
- first_table: float32 [256, 1536], P(('dp', 'text')), may hold values from -2.2351742e-08 to 2.2351742e-08
- second_table: float32 [256, 1536], P(('dp', 'text')), may hold values from 1.100811e-18 to 4.403244e-18
- first_cross: float32 [1536, 2, 1536], P(('dp', 'text')), may hold values from -1.7881393e-07 to 1.7881393e-07
- second_cross: float32 [1536, 2, 1536], P(('dp', 'text')), may hold values from 6.6048665e-17 to 2.6419466e-16
- first_key_value: float32 [768, 3072], P(('dp', 'text')), may hold values from -4.7683716e-07 to 4.7683716e-07
- second_key_value: float32 [768, 3072], P(('dp', 'text')), may hold values from 5.504055e-16 to 2.201622e-15
- first_gate_up: float32 [1536, 12288], P(('dp', 'text')), may hold values from -8.940697e-08 to 8.940697e-08
- second_gate_up: float32 [1536, 12288], P(('dp', 'text')), may hold values from 1.6512166e-17 to 6.6048665e-17
- first_down: float32 [6144, 1536], P(('dp', 'text')), may hold values from -1.4901161e-07 to 1.4901161e-07
- second_down: float32 [6144, 1536], P(('dp', 'text')), may hold values from 4.4032442e-17 to 1.7612977e-16
- first_gains: float32 [1536, 3], P(('dp', 'text')), may hold values from -1.9073486e-06 to 1.9073486e-06
- second_gains: float32 [1536, 3], P(('dp', 'text')), may hold values from 8.806488e-15 to 3.5225952e-14
- left_stats: float32 [256, 192, 192], P(('dp', 'text')), as said below
- right_stats: float32 [256, 192, 192], P(('dp', 'text')), as said below
- left_roots: float32 [256, 192, 192], P(('dp', 'text')), as said below
- right_roots: float32 [256, 192, 192], P(('dp', 'text')), as said below
Outputs:
- loss_sum: float32 [], replicated
- gradient_norm: float32 [], replicated
- new_first_ends: float32 [1536, 2, 64], P(('dp', 'text'))
- new_second_ends: float32 [1536, 2, 64], P(('dp', 'text'))
- new_end_weights: float32 [1536, 2, 64], P(('dp', 'text'))
- new_first_table: float32 [256, 1536], P(('dp', 'text'))
- new_second_table: float32 [256, 1536], P(('dp', 'text'))
- new_time_table: float32 [256, 1536], P(('dp', 'text'))
- new_first_cross: float32 [1536, 2, 1536], P(('dp', 'text'))
- renewed_cross_moment: float32 [1536, 2, 1536], P(('dp', 'text'))
- new_cross_weights: float32 [1536, 2, 1536], P(('dp', 'text'))
- new_first_key_value: float32 [768, 3072], P(('dp', 'text'))
- new_second_key_value: float32 [768, 3072], P(('dp', 'text'))
- new_key_value: float32 [768, 3072], P(('dp', 'text'))
- new_first_gate_up: float32 [1536, 12288], P(('dp', 'text'))
- new_second_gate_up: float32 [1536, 12288], P(('dp', 'text'))
- new_gate_up: float32 [1536, 12288], P(('dp', 'text'))
- new_first_down: float32 [6144, 1536], P(('dp', 'text'))
- new_second_down: float32 [6144, 1536], P(('dp', 'text'))
- new_down_weight: float32 [6144, 1536], P(('dp', 'text'))
- new_first_gains: float32 [1536, 3], P(('dp', 'text'))
- new_second_gains: float32 [1536, 3], P(('dp', 'text'))
- new_norm_gains: float32 [1536, 3], P(('dp', 'text'))
- clipped_slots: float32 [256, 192, 192], P(('dp', 'text'))
- new_left_stats: float32 [256, 192, 192], P(('dp', 'text'))
- new_right_stats: float32 [256, 192, 192], P(('dp', 'text'))
- new_square_slots: float32 [256, 192, 192], P(('dp', 'text'))
Inputs may be any that keep to these rules, and one draw needn't show every extreme that they name: `text_lengths`: in each aligned block of 2 items one item's prompt reaches the last text shard; some item has length 128. negatives[i, :] never holds i; repeats may occur. `assignment`: A permutation of the block numbers. `end_weights`: normal entries, fan-in scaled. `square_slots`: normal entries. `cross_weights`: normal entries. `norm_gains`: Positive. `left_stats`: Diagonal, positive on the diagonal. `right_stats`: Diagonal, positive on the diagonal. `left_roots`: Symmetric. `right_roots`: Symmetric.
All inputs are finite; a program needn't handle non-finite values.
Results may differ from a plain program's by a relative error of at most 0.02.
The roundings to bfloat16 on the way count: a program that leaves them out, or rounds other values in their place, can miss the bound.
Values may be sent and summed in bfloat16 or wider, within the bound.
A program may use at most 448 MiB of HBM per device.

v0:
```python
from functools import partial
import math

import jax
import jax.numpy as jnp
from jax import lax
from jax.sharding import PartitionSpec as P

D = 1536
HEADS = 24
HD = 64
FF = 6144
DIN = 64
DT = 768
FRAMES = 1024
NTIME = 256
STEP = 10
BLK = 192


BEST_PRECISION = lax.Precision.HIGHEST
NORM_EPS = 1e-05
POOL_EPS = 1e-06
SCORE_SCALE = 0.125
CONTRAST_TEMP = 0.02
CONTRAST_WEIGHT = 0.1
CLIP_NORM = 0.005
BETA_FIRST = 0.9
BETA_SECOND = 0.999
ADAM_EPS = 1e-08
WEIGHT_DECAY = 0.01
ADAM_RATES = (0.02, 0.05, 0.0, 0.1, 0.02, 0.02, 0.02, 1.0)
STAT_DECAY = 0.999
SHAMPOO_RATE = 0.01
MASK_VALUE = -1000000000.0


def layer_stats(inputs):
    center = inputs - jnp.mean(inputs, -1, keepdims=True)
    inverse = lax.rsqrt(jnp.mean(center * center, -1, keepdims=True) + NORM_EPS)
    return (center * inverse, inverse)


def layer_back(grad_out, normed, inverse, gain_row):
    scaled = grad_out * gain_row
    grad_in = inverse * (
        scaled
        - jnp.mean(scaled, -1, keepdims=True)
        - normed * jnp.mean(scaled * normed, -1, keepdims=True)
    )
    return (grad_in, jnp.sum(grad_out * normed, 0))


def time_features(timesteps):
    halfway = NTIME // 2
    frequency = jnp.exp(jnp.arange(halfway, dtype=jnp.float32) * (math.log(64.0) / halfway))
    moment = (timesteps.astype(jnp.float32) + 0.5) / NTIME
    phase = 2.0 * math.pi * moment[:, None] * frequency[None, :]
    return jnp.concatenate([jnp.cos(phase), jnp.sin(phase)], 1)


def rope_tables(positions_count, offset):
    halfway = HD // 2
    frequency = jnp.exp(jnp.arange(halfway, dtype=jnp.float32) * (-2.0 * math.log(10000.0) / HD))
    positions = (jnp.arange(positions_count, dtype=jnp.int32) + offset).astype(jnp.float32)
    angles = positions[:, None] * frequency[None, :]
    return (jnp.concatenate([jnp.cos(angles)] * 2, -1), jnp.concatenate([jnp.sin(angles)] * 2, -1))


def rotate(values, cosine_table, sine_table):
    halfway = HD // 2
    turned = jnp.concatenate([-values[..., halfway:], values[..., :halfway]], -1)
    return values * cosine_table[:, None, :] + turned * sine_table[:, None, :]


def rotate_back(gradient, cosine_table, sine_table):
    halfway = HD // 2
    product = gradient * sine_table[:, None, :]
    return gradient * cosine_table[:, None, :] + jnp.concatenate(
        [product[..., halfway:], -product[..., :halfway]], -1
    )


def to_matrices(blocks):
    per_side = D // BLK
    return blocks.reshape(4, per_side, per_side, BLK, BLK).transpose(0, 1, 3, 2, 4).reshape(4, D, D)


def to_blocks(matrices):
    per_side = D // BLK
    return (
        matrices.reshape(4, per_side, BLK, per_side, BLK)
        .transpose(0, 1, 3, 2, 4)
        .reshape(4 * per_side * per_side, BLK, BLK)
    )


def normalize(vectors):
    return vectors * lax.rsqrt(jnp.sum(vectors * vectors, -1, keepdims=True) + POOL_EPS)


def contrast_loss(pooled_audio, pooled_text, negatives):
    audio_unit_vectors = normalize(pooled_audio)
    text_unit_vectors = normalize(pooled_text)
    positive_pairs = jnp.sum(audio_unit_vectors * text_unit_vectors, -1) / CONTRAST_TEMP
    negative_pairs = (
        jnp.einsum(
            "ux,uax->ua", audio_unit_vectors, text_unit_vectors[negatives], precision=BEST_PRECISION
        )
        / CONTRAST_TEMP
    )
    scores = jnp.concatenate([positive_pairs[:, None], negative_pairs], 1)
    peak_score = jnp.max(scores, -1, keepdims=True)
    logsum = peak_score[:, 0] + jnp.log(jnp.sum(jnp.exp(scores - peak_score), -1))
    return jnp.sum(logsum - positive_pairs)


def item_scores(one_query, one_key, one_bias):
    scores = jnp.einsum("fhd,khd->hfk", one_query, one_key, preferred_element_type=jnp.float32)
    return scores * SCORE_SCALE + one_bias


def attend_forward(queries, all_keys, values, key_bias):

    def single(pieces):
        one_query, one_key, one_value, one_bias = pieces
        scores = item_scores(one_query, one_key, one_bias)
        peak_score = jnp.max(scores, -1, keepdims=True)
        weights = jnp.exp(scores - peak_score)
        row_total = jnp.sum(weights, -1, keepdims=True)
        mixture = jnp.einsum(
            "hfk,khd->fhd",
            (weights / row_total).astype(jnp.bfloat16),
            one_value,
            preferred_element_type=jnp.float32,
        )
        return (mixture.astype(jnp.bfloat16), peak_score + jnp.log(row_total))

    return lax.map(single, (queries, all_keys, values, key_bias))


def attend_backward(queries, all_keys, values, key_bias, logsums, grad_mixture):

    def single(pieces):
        one_query, one_key, one_value, one_bias, one_logsum, grad_rows = pieces
        attention = jnp.exp(item_scores(one_query, one_key, one_bias) - one_logsum)
        grad_attention = jnp.einsum(
            "fhd,khd->hfk", grad_rows, one_value, preferred_element_type=jnp.float32
        )
        grad_value = jnp.einsum(
            "hfk,fhd->khd",
            attention.astype(jnp.bfloat16),
            grad_rows,
            preferred_element_type=jnp.float32,
        )
        grad_scores = attention * (
            grad_attention - jnp.sum(attention * grad_attention, -1, keepdims=True)
        )
        grad_scores = grad_scores.astype(jnp.bfloat16)
        grad_query = (
            jnp.einsum("hfk,khd->fhd", grad_scores, one_key, preferred_element_type=jnp.float32)
            * SCORE_SCALE
        )
        grad_key = (
            jnp.einsum("hfk,fhd->khd", grad_scores, one_query, preferred_element_type=jnp.float32)
            * SCORE_SCALE
        )
        return (grad_query, grad_key, grad_value)

    return lax.map(single, (queries, all_keys, values, key_bias, logsums, grad_mixture))


def feed_forward(rows_in, gate_matrix, down_matrix):
    width = down_matrix.shape[0]
    gate_values = jnp.dot(rows_in, gate_matrix, preferred_element_type=jnp.float32)
    gate_part = gate_values[:, :width]
    up_part = gate_values[:, width:]
    sigmoid = jax.nn.sigmoid(gate_part)
    silu_value = gate_part * sigmoid
    hidden = (silu_value * up_part).astype(jnp.bfloat16)
    partial_out = jnp.dot(hidden, down_matrix, preferred_element_type=jnp.float32)
    return (partial_out, (hidden, gate_part, up_part, sigmoid, silu_value))


def feed_back(rows_in, gate_matrix, down_matrix, kept, grad_low):
    hidden, gate_part, up_part, sigmoid, silu_value = kept
    grad_down = jnp.einsum("rf,rd->fd", hidden, grad_low, preferred_element_type=jnp.float32)
    grad_hidden = jnp.einsum("rd,fd->rf", grad_low, down_matrix, preferred_element_type=jnp.float32)
    grad_gate = grad_hidden * up_part * sigmoid * (1.0 + gate_part * (1.0 - sigmoid))
    grad_pair = jnp.concatenate([grad_gate, grad_hidden * silu_value], 1).astype(jnp.bfloat16)
    grad_gate_up = jnp.einsum("rd,rg->dg", rows_in, grad_pair, preferred_element_type=jnp.float32)
    grad_rows = jnp.einsum("rg,dg->rd", grad_pair, gate_matrix, preferred_element_type=jnp.float32)
    return (grad_rows, grad_gate_up, grad_down)


def adam_update(weight, first_moment, second_moment, gradient, rate):
    first_moment = BETA_FIRST * first_moment + (1.0 - BETA_FIRST) * gradient
    second_moment = BETA_SECOND * second_moment + (1.0 - BETA_SECOND) * gradient * gradient
    corrected = first_moment / (1.0 - BETA_FIRST**STEP)
    scaled = second_moment / (1.0 - BETA_SECOND**STEP)
    weight = weight - rate * (corrected / (jnp.sqrt(scaled) + ADAM_EPS) + WEIGHT_DECAY * weight)
    return (first_moment, second_moment, weight)


def shampoo_update(slots_now, gradient, left_stat, right_stat, left_root, right_root):
    left_stat = STAT_DECAY * left_stat + (1.0 - STAT_DECAY) * jnp.einsum(
        "sij,skj->sik", gradient, gradient, precision=BEST_PRECISION
    )
    right_stat = STAT_DECAY * right_stat + (1.0 - STAT_DECAY) * jnp.einsum(
        "sji,sjk->sik", gradient, gradient, precision=BEST_PRECISION
    )
    inner = jnp.einsum("sij,sjk->sik", gradient, right_root, precision=BEST_PRECISION)
    direction = jnp.einsum("sij,sjk->sik", left_root, inner, precision=BEST_PRECISION)
    return (
        left_stat,
        right_stat,
        slots_now - SHAMPOO_RATE * (direction + WEIGHT_DECAY * slots_now),
    )


def shards(
    latents,
    noise_field,
    timesteps,
    text_tokens,
    text_lengths,
    negatives,
    assignment,
    end_weights,
    time_table,
    square_slots,
    cross_weights,
    key_value,
    gate_up,
    down_weight,
    norm_gains,
    first_ends,
    second_ends,
    first_table,
    second_table,
    first_cross,
    second_cross,
    first_key_value,
    second_key_value,
    first_gate_up,
    second_gate_up,
    first_down,
    second_down,
    first_gains,
    second_gains,
    left_stats,
    right_stats,
    left_roots,
    right_roots,
):
    text_index = lax.axis_index("text")
    group_index = lax.axis_index("dp")
    group_count = lax.axis_size("dp")
    text_count_axis = lax.axis_size("text")
    piece_width = FF // (group_count * text_count_axis)
    low_ends = end_weights.astype(jnp.bfloat16)
    low_table = time_table.astype(jnp.bfloat16)
    low_slots = square_slots.astype(jnp.bfloat16)
    low_cross = cross_weights.astype(jnp.bfloat16)
    low_pairs = key_value.astype(jnp.bfloat16)
    low_gains = norm_gains.astype(jnp.bfloat16)
    low_gate = gate_up.astype(jnp.bfloat16)
    low_down = down_weight.astype(jnp.bfloat16)
    group_set = (
        lax.all_gather(low_ends, "text", axis=0, tiled=True),
        lax.all_gather(low_table, "text", axis=0, tiled=True),
        lax.all_gather(low_slots, "text", axis=0, tiled=True),
        lax.all_gather(low_cross, "text", axis=0, tiled=True),
        lax.all_gather(low_pairs, "text", axis=0, tiled=True),
        lax.all_gather(low_gains, "text", axis=0, tiled=True),
        lax.all_gather(low_gate, "text", axis=0, tiled=True),
    )
    gate_group = group_set[6].reshape(
        group_set[6].shape[0], 2, group_count, text_count_axis, piece_width
    )
    gate_columns = lax.dynamic_index_in_dim(gate_group, text_index, 3, keepdims=False)
    full_set = (
        lax.all_gather(group_set[0], "dp", axis=0, tiled=True),
        lax.all_gather(group_set[1], "dp", axis=0, tiled=True),
        lax.all_gather(group_set[2], "dp", axis=0, tiled=True),
        lax.all_gather(group_set[3], "dp", axis=0, tiled=True),
        lax.all_gather(group_set[4], "dp", axis=0, tiled=True),
        lax.all_gather(group_set[5], "dp", axis=0, tiled=True),
        lax.all_gather(gate_columns, "dp", axis=0, tiled=True),
        lax.all_gather(low_down, "dp", axis=0, tiled=True),
    )
    ends_full, table_full, slots_full, cross_full, pairs_full, gains_full = full_set[:6]
    gate_full = full_set[6].reshape(D, 2 * group_count * piece_width)
    down_full = full_set[7]
    item_count = latents.shape[0]
    frames_dev = latents.shape[1]
    tokens_dev = text_tokens.shape[1]
    row_count = item_count * frames_dev
    items_total = item_count * group_count
    mse_scale = 1.0 / (items_total * FRAMES * DIN)
    weight_in = ends_full[:, 0, :]
    weight_out = ends_full[:, 1, :]
    gain_values = gains_full.astype(jnp.float32)
    inverse_order = (
        jnp.zeros_like(assignment)
        .at[assignment]
        .set(jnp.arange(assignment.shape[0], dtype=jnp.int32))
    )
    squares = to_matrices(slots_full[inverse_order])
    projection = jnp.concatenate([squares[0], squares[1], squares[2]], 1)
    cosine_table, sine_table = rope_tables(frames_dev, 1 + text_index * frames_dev)
    angles = (timesteps.astype(jnp.float32) + 0.5) * (0.5 * math.pi / NTIME)
    signal = jnp.cos(angles)[:, None, None]
    spread = jnp.sin(angles)[:, None, None]
    noised = (signal * latents + spread * noise_field).astype(jnp.bfloat16).reshape(row_count, DIN)
    residual = jnp.einsum("rc,dc->rd", noised, weight_in, preferred_element_type=jnp.float32)
    normed_one, inverse_one = layer_stats(residual)
    input_one = (normed_one * gain_values[:, 0]).astype(jnp.bfloat16)
    features = time_features(timesteps).astype(jnp.bfloat16)
    embeds = jnp.dot(features, table_full, preferred_element_type=jnp.float32)
    normed_time, inverse_time = layer_stats(embeds)
    input_time = (normed_time * gain_values[:, 0]).astype(jnp.bfloat16)
    joined_rows = jnp.dot(input_one, projection, preferred_element_type=jnp.float32)
    head_shape = (item_count, frames_dev, HEADS, HD)
    rot_queries = rotate(joined_rows[:, :D].reshape(head_shape), cosine_table, sine_table).astype(
        jnp.bfloat16
    )
    rot_keys = rotate(
        joined_rows[:, D : 2 * D].reshape(head_shape), cosine_table, sine_table
    ).astype(jnp.bfloat16)
    value_rows = joined_rows[:, 2 * D :].astype(jnp.bfloat16).reshape(item_count, frames_dev, D)
    time_pair = jnp.dot(input_time, projection[:, D:], preferred_element_type=jnp.float32).astype(
        jnp.bfloat16
    )
    keys_all, values_all = (
        lax.all_gather(rot_keys.reshape(item_count, frames_dev, D), "text", axis=1, tiled=True),
        lax.all_gather(value_rows, "text", axis=1, tiled=True),
    )
    key_count = keys_all.shape[1] + 1
    all_keys = jnp.concatenate([time_pair[:, None, :D], keys_all], 1).reshape(
        item_count, key_count, HEADS, HD
    )
    all_values = jnp.concatenate([time_pair[:, None, D:], values_all], 1).reshape(
        item_count, key_count, HEADS, HD
    )
    self_bias = jnp.zeros((item_count, key_count), jnp.float32)
    mixed_self, logsum_self = attend_forward(rot_queries, all_keys, all_values, self_bias)
    mixed_flat = mixed_self.reshape(row_count, D)
    after_self = residual + jnp.dot(mixed_flat, squares[3], preferred_element_type=jnp.float32)
    normed_two, inverse_two = layer_stats(after_self)
    input_two = (normed_two * gain_values[:, 1]).astype(jnp.bfloat16)
    cross_queries = jnp.dot(
        input_two, cross_full[:, 0, :], preferred_element_type=jnp.float32
    ).astype(jnp.bfloat16)
    cross_heads = cross_queries.reshape(head_shape)
    projected = jnp.dot(
        text_tokens.reshape(item_count * tokens_dev, DT),
        pairs_full,
        preferred_element_type=jnp.float32,
    )
    projected = projected.astype(jnp.bfloat16).reshape(item_count, tokens_dev, 2 * D)
    text_all = lax.all_gather(projected, "text", axis=1, tiled=True)
    text_count = text_all.shape[1]
    valid_keys = jnp.arange(text_count, dtype=jnp.int32)[None, :] < text_lengths[:, None]
    cross_bias = jnp.where(valid_keys, 0.0, MASK_VALUE).astype(jnp.float32)
    text_keys = text_all[:, :, :D].reshape(item_count, text_count, HEADS, HD)
    text_values = text_all[:, :, D:].reshape(item_count, text_count, HEADS, HD)
    mixed_cross, logsum_cross = attend_forward(cross_heads, text_keys, text_values, cross_bias)
    cross_flat = mixed_cross.reshape(row_count, D)
    after_cross = after_self + jnp.dot(
        cross_flat, cross_full[:, 1, :], preferred_element_type=jnp.float32
    )
    normed_three, inverse_three = layer_stats(after_cross)
    input_three = (normed_three * gain_values[:, 2]).astype(jnp.bfloat16)
    feed_rows = lax.all_gather(
        input_three.reshape(item_count, frames_dev, D), "text", axis=1, tiled=True
    ).reshape(-1, D)
    feed_out, feed_kept = feed_forward(feed_rows, gate_full, down_full)
    down_out = (
        lax.psum_scatter(
            feed_out.reshape(item_count, -1, D).astype(jnp.bfloat16),
            "text",
            scatter_dimension=1,
            tiled=True,
        )
        .astype(jnp.float32)
        .reshape(row_count, D)
    )
    output_rows = after_cross + down_out
    output_low = output_rows.astype(jnp.bfloat16)
    predicted = jnp.dot(output_low, weight_out, preferred_element_type=jnp.float32).reshape(
        latents.shape
    )
    errors = predicted - (signal * noise_field - spread * latents)
    lengths_float = text_lengths.astype(jnp.float32)
    own_valid = (text_index * tokens_dev + jnp.arange(tokens_dev, dtype=jnp.int32))[
        None, :
    ] < text_lengths[:, None]
    own_mask = own_valid.astype(jnp.float32)
    audio_part = jnp.sum(output_rows.reshape(item_count, frames_dev, D), 1)
    text_part = (
        jnp.sum(projected[:, :, :D].astype(jnp.float32) * own_mask[:, :, None], 1)
        / lengths_float[:, None]
    )
    pooled_set = (
        lax.all_gather(audio_part, ("dp", "text"), axis=0, tiled=True),
        lax.all_gather(text_part, ("dp", "text"), axis=0, tiled=True),
        lax.all_gather(negatives.astype(jnp.float32), ("dp", "text"), axis=0, tiled=True),
    )
    audio_pooled = (
        jnp.sum(pooled_set[0].reshape(group_count, text_count_axis, item_count, D), 1).reshape(
            -1, D
        )
        / FRAMES
    )
    text_pooled = jnp.sum(
        pooled_set[1].reshape(group_count, text_count_axis, item_count, D), 1
    ).reshape(-1, D)
    negative_rows = pooled_set[2].reshape(group_count, text_count_axis, item_count, -1)[:, 0]
    negative_rows = negative_rows.reshape(items_total, -1).astype(jnp.int32)
    contrast_value, contrast_back = jax.vjp(
        partial(contrast_loss, negatives=negative_rows), audio_pooled, text_pooled
    )
    grad_audio_all, grad_text_all = contrast_back(jnp.float32(CONTRAST_WEIGHT / items_total))
    grad_audio = lax.dynamic_slice_in_dim(grad_audio_all, group_index * item_count, item_count, 0)
    grad_text = lax.dynamic_slice_in_dim(grad_text_all, group_index * item_count, item_count, 0)
    grad_predicted = (2.0 * mse_scale * errors).astype(jnp.bfloat16).reshape(row_count, DIN)
    grad_out_weight = jnp.einsum(
        "rd,rc->dc", output_low, grad_predicted, preferred_element_type=jnp.float32
    )
    grad_output = jnp.einsum(
        "rc,dc->rd", grad_predicted, weight_out, preferred_element_type=jnp.float32
    )
    grad_output = (
        grad_output.reshape(item_count, frames_dev, D) + grad_audio[:, None, :] / FRAMES
    ).reshape(row_count, D)
    grad_down_in = grad_output.astype(jnp.bfloat16)
    grad_feed_rows = lax.all_gather(
        grad_down_in.reshape(item_count, frames_dev, D), "text", axis=1, tiled=True
    ).reshape(-1, D)
    grad_feed_in, grad_gate_up, grad_down = feed_back(
        feed_rows, gate_full, down_full, feed_kept, grad_feed_rows
    )
    grad_input_three = (
        lax.psum_scatter(
            grad_feed_in.reshape(item_count, -1, D).astype(jnp.bfloat16),
            "text",
            scatter_dimension=1,
            tiled=True,
        )
        .astype(jnp.float32)
        .reshape(row_count, D)
    )
    grad_after_cross, gain_three = layer_back(
        grad_input_three, normed_three, inverse_three, gain_values[:, 2]
    )
    grad_after_cross = grad_after_cross + grad_output
    grad_cross_in = grad_after_cross.astype(jnp.bfloat16)
    grad_cross_out = jnp.einsum(
        "rd,re->de", cross_flat, grad_cross_in, preferred_element_type=jnp.float32
    )
    grad_mixed_cross = jnp.einsum(
        "re,de->rd", grad_cross_in, cross_full[:, 1, :], preferred_element_type=jnp.float32
    )
    grad_mixed_cross = grad_mixed_cross.astype(jnp.bfloat16).reshape(head_shape)
    grad_cq, grad_text_keys, grad_text_values = attend_backward(
        cross_heads, text_keys, text_values, cross_bias, logsum_cross, grad_mixed_cross
    )
    grad_cq_low = grad_cq.reshape(row_count, D).astype(jnp.bfloat16)
    grad_cross_query = jnp.einsum(
        "rd,re->de", input_two, grad_cq_low, preferred_element_type=jnp.float32
    )
    grad_input_two = jnp.einsum(
        "re,de->rd", grad_cq_low, cross_full[:, 0, :], preferred_element_type=jnp.float32
    )
    grad_pairs = jnp.concatenate(
        [
            grad_text_keys.reshape(item_count, text_count, D),
            grad_text_values.reshape(item_count, text_count, D),
        ],
        2,
    )
    grad_own_pairs = lax.psum_scatter(
        grad_pairs.astype(jnp.bfloat16), "text", scatter_dimension=1, tiled=True
    ).astype(jnp.float32)
    pooled_grad = own_mask[:, :, None] * (grad_text[:, None, :] / lengths_float[:, None, None])
    grad_own_pairs = grad_own_pairs + jnp.concatenate([pooled_grad, jnp.zeros_like(pooled_grad)], 2)
    grad_own_pairs = grad_own_pairs.astype(jnp.bfloat16).reshape(item_count * tokens_dev, 2 * D)
    grad_textside = jnp.einsum(
        "tc,tk->ck",
        text_tokens.reshape(item_count * tokens_dev, DT),
        grad_own_pairs,
        preferred_element_type=jnp.float32,
    )
    grad_after_self, gain_two = layer_back(
        grad_input_two, normed_two, inverse_two, gain_values[:, 1]
    )
    grad_after_self = grad_after_self + grad_after_cross
    grad_self_in = grad_after_self.astype(jnp.bfloat16)
    grad_attn_out = jnp.einsum(
        "rd,re->de", mixed_flat, grad_self_in, preferred_element_type=jnp.float32
    )
    grad_mixed_self = jnp.einsum(
        "re,de->rd", grad_self_in, squares[3], preferred_element_type=jnp.float32
    )
    grad_mixed_self = grad_mixed_self.astype(jnp.bfloat16).reshape(head_shape)
    grad_rot_queries, grad_keys, value_gradients = attend_backward(
        rot_queries, all_keys, all_values, self_bias, logsum_self, grad_mixed_self
    )
    grad_keys_own, grad_values_own = (
        lax.psum_scatter(
            grad_keys[:, 1:].reshape(item_count, key_count - 1, D).astype(jnp.bfloat16),
            "text",
            scatter_dimension=1,
            tiled=True,
        ).astype(jnp.float32),
        lax.psum_scatter(
            value_gradients[:, 1:].reshape(item_count, key_count - 1, D).astype(jnp.bfloat16),
            "text",
            scatter_dimension=1,
            tiled=True,
        ).astype(jnp.float32),
    )
    grad_queries = (
        rotate_back(grad_rot_queries, cosine_table, sine_table)
        .astype(jnp.bfloat16)
        .reshape(row_count, D)
    )
    grad_key_rows = rotate_back(grad_keys_own.reshape(head_shape), cosine_table, sine_table)
    grad_key_rows = grad_key_rows.astype(jnp.bfloat16).reshape(row_count, D)
    grad_joined = jnp.concatenate(
        [grad_queries, grad_key_rows, grad_values_own.astype(jnp.bfloat16).reshape(row_count, D)], 1
    )
    grad_projection = jnp.einsum(
        "rd,rk->dk", input_one, grad_joined, preferred_element_type=jnp.float32
    )
    grad_input_one = jnp.einsum(
        "rk,dk->rd", grad_joined, projection, preferred_element_type=jnp.float32
    )
    grad_time_pair = jnp.concatenate(
        [grad_keys[:, 0].reshape(item_count, D), value_gradients[:, 0].reshape(item_count, D)], 1
    )
    time_rows = jnp.dot(input_time.astype(jnp.float32).T, grad_time_pair, precision=BEST_PRECISION)
    grad_projection = grad_projection + jnp.concatenate(
        [jnp.zeros((D, D), jnp.float32), time_rows], 1
    )
    grad_input_time = jnp.einsum(
        "ik,dk->id", grad_time_pair, projection[:, D:].astype(jnp.float32), precision=BEST_PRECISION
    )
    grad_residual, gain_one = layer_back(grad_input_one, normed_one, inverse_one, gain_values[:, 0])
    grad_residual = (grad_residual + grad_after_self).astype(jnp.bfloat16)
    grad_embeds, gain_time = layer_back(
        grad_input_time, normed_time, inverse_time, gain_values[:, 0]
    )
    grad_in_weight = jnp.einsum(
        "rd,rc->dc", grad_residual, noised, preferred_element_type=jnp.float32
    )
    grad_table = jnp.dot(features.astype(jnp.float32).T, grad_embeds, precision=BEST_PRECISION)
    grad_gains = jnp.stack([gain_one + gain_time, gain_two, gain_three], 1)
    grad_ends = jnp.stack([grad_in_weight, grad_out_weight], 1)
    grad_cross = jnp.stack([grad_cross_query, grad_cross_out], 1)
    grad_squares = jnp.stack(
        [
            grad_projection[:, :D],
            grad_projection[:, D : 2 * D],
            grad_projection[:, 2 * D :],
            grad_attn_out,
        ],
        0,
    )
    grad_slots = jnp.take(to_blocks(grad_squares), assignment, axis=0)
    gate_pieces = grad_gate_up.reshape(D, 2, group_count, piece_width)
    group_grads = (
        lax.psum_scatter(
            grad_ends.astype(jnp.bfloat16), "dp", scatter_dimension=0, tiled=True
        ).astype(jnp.float32),
        lax.psum_scatter(
            grad_table.astype(jnp.bfloat16), "dp", scatter_dimension=0, tiled=True
        ).astype(jnp.float32),
        lax.psum_scatter(
            grad_slots.astype(jnp.bfloat16), "dp", scatter_dimension=0, tiled=True
        ).astype(jnp.float32),
        lax.psum_scatter(
            grad_cross.astype(jnp.bfloat16), "dp", scatter_dimension=0, tiled=True
        ).astype(jnp.float32),
        lax.psum_scatter(
            grad_textside.astype(jnp.bfloat16), "dp", scatter_dimension=0, tiled=True
        ).astype(jnp.float32),
        lax.psum_scatter(
            grad_gains.astype(jnp.bfloat16), "dp", scatter_dimension=0, tiled=True
        ).astype(jnp.float32),
        lax.psum_scatter(
            gate_pieces.astype(jnp.bfloat16), "dp", scatter_dimension=0, tiled=True
        ).astype(jnp.float32),
        lax.psum_scatter(
            grad_down.astype(jnp.bfloat16), "dp", scatter_dimension=0, tiled=True
        ).astype(jnp.float32),
    )
    placing = (jnp.arange(text_count_axis, dtype=jnp.int32) == text_index).astype(jnp.float32)
    spread_gate = group_grads[6][:, :, :, None, :] * placing[None, None, None, :, None]
    spread_gate = spread_gate.reshape(spread_gate.shape[0], 2 * FF)
    owned = (
        lax.psum_scatter(
            group_grads[0].astype(jnp.bfloat16), "text", scatter_dimension=0, tiled=True
        ).astype(jnp.float32),
        lax.psum_scatter(
            group_grads[1].astype(jnp.bfloat16), "text", scatter_dimension=0, tiled=True
        ).astype(jnp.float32),
        lax.psum_scatter(
            group_grads[2].astype(jnp.bfloat16), "text", scatter_dimension=0, tiled=True
        ).astype(jnp.float32),
        lax.psum_scatter(
            group_grads[3].astype(jnp.bfloat16), "text", scatter_dimension=0, tiled=True
        ).astype(jnp.float32),
        lax.psum_scatter(
            group_grads[4].astype(jnp.bfloat16), "text", scatter_dimension=0, tiled=True
        ).astype(jnp.float32),
        lax.psum_scatter(
            group_grads[5].astype(jnp.bfloat16), "text", scatter_dimension=0, tiled=True
        ).astype(jnp.float32),
        lax.psum_scatter(
            spread_gate.astype(jnp.bfloat16), "text", scatter_dimension=0, tiled=True
        ).astype(jnp.float32),
    )
    reduced = (owned[0], owned[1], owned[2], owned[3], owned[4], owned[6], group_grads[7], owned[5])
    square_sum = jnp.zeros((), jnp.float32)
    for member in reduced:
        square_sum = square_sum + jnp.sum(member * member)
    loss_part = jnp.sum(errors * errors) * mse_scale
    totals = lax.psum((square_sum, loss_part), ("dp", "text"))
    loss_total = totals[1] + CONTRAST_WEIGHT * contrast_value / items_total
    gradient_norm = jnp.sqrt(totals[0])
    factor = CLIP_NORM / jnp.maximum(gradient_norm, CLIP_NORM)
    masters = (
        end_weights,
        time_table,
        square_slots,
        cross_weights,
        key_value,
        gate_up,
        down_weight,
        norm_gains,
    )
    firsts = (
        first_ends,
        first_table,
        None,
        first_cross,
        first_key_value,
        first_gate_up,
        first_down,
        first_gains,
    )
    seconds = (
        second_ends,
        second_table,
        None,
        second_cross,
        second_key_value,
        second_gate_up,
        second_down,
        second_gains,
    )
    results = [loss_total, gradient_norm]
    for index_value in (0, 1, 3, 4, 5, 6, 7):
        results.extend(
            adam_update(
                masters[index_value],
                firsts[index_value],
                seconds[index_value],
                factor * reduced[index_value],
                ADAM_RATES[index_value],
            )
        )
    clipped_slots = factor * reduced[2]
    left_new, right_new, slots_new = shampoo_update(
        square_slots, clipped_slots, left_stats, right_stats, left_roots, right_roots
    )
    results.extend([clipped_slots, left_new, right_new, slots_new])
    return tuple(results)


def solution(mesh):
    in_specs = (
        P("dp", "text", None),
        P("dp", "text", None),
        P("dp"),
        P("dp", "text", None),
        P("dp"),
        P("dp", None),
        P(),
        P(("dp", "text"), None, None),
        P(("dp", "text"), None),
        P(("dp", "text"), None, None),
        P(("dp", "text"), None, None),
        P(("dp", "text"), None),
        P(("dp", "text"), None),
        P(("dp", "text"), None),
        P(("dp", "text"), None),
        P(("dp", "text"), None, None),
        P(("dp", "text"), None, None),
        P(("dp", "text"), None),
        P(("dp", "text"), None),
        P(("dp", "text"), None, None),
        P(("dp", "text"), None, None),
        P(("dp", "text"), None),
        P(("dp", "text"), None),
        P(("dp", "text"), None),
        P(("dp", "text"), None),
        P(("dp", "text"), None),
        P(("dp", "text"), None),
        P(("dp", "text"), None),
        P(("dp", "text"), None),
        P(("dp", "text"), None, None),
        P(("dp", "text"), None, None),
        P(("dp", "text"), None, None),
        P(("dp", "text"), None, None),
    )
    out_specs = (
        P(),
        P(),
        P(("dp", "text"), None, None),
        P(("dp", "text"), None, None),
        P(("dp", "text"), None, None),
        P(("dp", "text"), None),
        P(("dp", "text"), None),
        P(("dp", "text"), None),
        P(("dp", "text"), None, None),
        P(("dp", "text"), None, None),
        P(("dp", "text"), None, None),
        P(("dp", "text"), None),
        P(("dp", "text"), None),
        P(("dp", "text"), None),
        P(("dp", "text"), None),
        P(("dp", "text"), None),
        P(("dp", "text"), None),
        P(("dp", "text"), None),
        P(("dp", "text"), None),
        P(("dp", "text"), None),
        P(("dp", "text"), None),
        P(("dp", "text"), None),
        P(("dp", "text"), None),
        P(("dp", "text"), None, None),
        P(("dp", "text"), None, None),
        P(("dp", "text"), None, None),
        P(("dp", "text"), None, None),
    )
    return jax.shard_map(shards, mesh=mesh, in_specs=in_specs, out_specs=out_specs, check_vma=False)
```

profile of v0, /device:TPU:0, one launch (start us, length us, event | category | flops | bytes accessed | tf_op | source)
XLA Modules:
  0.0 2922.5 jit_solution(9708316410496861712)
XLA Ops:
  9.9 22.7 all_gather.79
  32.7 46.4 %all-gather.20.cloned.1.call-done = bf16[32,192,192]{2,1,0:T(8,128)(2,1)} async-done(((bf16[8,192,192]{2,1,0:T(8,128)(2,1)}), bf16[32,192,192]{2,1,0:T(8,128)(2,1)}) %all-gather.20.cloned.1.call-update) | async-done | bytes 2359312 | tf_op jit(solution)/shard_map/all_gather | solution.py:272
  137.6 109.8 %all-gather.22.cloned.1.call-done = bf16[256,192,192]{2,1,0:T(8,128)(2,1)} async-done(((bf16[32,192,192]{2,1,0:T(8,128)(2,1)}), bf16[256,192,192]{2,1,0:T(8,128)(2,1)}) %all-gather.22.cloned.1.call-update) | async-done | bytes 18874384 | tf_op jit(solution)/shard_map/all_gather | solution.py:285
  268.2 25.9 copy.608
  491.9 32.5 %all-gather.24.cloned.1.call-done = bf16[2,1024,1536]{2,1,0:T(8,128)(2,1)} async-done(((bf16[2,256,1536]{2,1,0:T(8,128)(2,1)}), bf16[2,1024,1536]{2,1,0:T(8,128)(2,1)}) %all-gather.24.cloned.1.call-update) | async-done | bytes 6291472 | tf_op jit(solution)/shard_map/all_gather | solution.py:337
  543.7 96.1 %all-gather.26.cloned.1.call-done = bf16[2,1024,1536]{1,2,0:T(8,128)(2,1)} async-done(((bf16[2,256,1536]{1,2,0:T(8,128)(2,1)}), bf16[2,1024,1536]{1,2,0:T(8,128)(2,1)}) %all-gather.26.cloned.1.call-update) | async-done | bytes 6291472 | tf_op jit(solution)/shard_map/all_gather | solution.py:336
  650.1 74.9 %while.52 = (s32[]{:T(128)}, bf16[2,256,24,64]{1,3,2,0:T(8,128)(2,1)S(1)}, f32[2,24,256,1]{2,1,3,0:T(8,128)S(1)}, bf16[2,1025,24,64]{1,3,2,0:T(8,128)(2,1)}, bf1...) while((s32[]{:T(128)}, bf16[2,256,24,64]{1,3,2,0:T(8,128)(2,1)S(1)}, ...), condition=%wide.region_8.9_spmd, body=%wide.region_5.8_spmd.sunk | while | flops 1669251072 | bytes 109611120 | solution.py:139
  790.4 100.4 %all-gather.36.cloned.1.call-done = bf16[2,1024,1536]{2,1,0:T(8,128)(2,1)} async-done(((bf16[2,256,1536]{2,1,0:T(8,128)(2,1)}), bf16[2,1024,1536]{2,1,0:T(8,128)(2,1)}) %all-gather.36.cloned.1.call-update) | async-done | bytes 6291472 | tf_op jit(solution)/shard_map/all_gather | solution.py:375
  890.8 24.0 fusion.234
  946.0 69.9 %all-gather.5 = f32[32,2,15]{2,1,0:T(2,128)S(1)} all-gather(f32[1,2,15]{2,1,0:T(2,128)S(1)} %convert_bitcast_fusion.1), channel_id=1, replica_groups=mesh['dp'=8,'text'=4] {'dp','text'}, dimensions={0}, use_global_device_ids=true | all-gather | bytes 3960 | tf_op jit(solution)/shard_map/all_gather | solution.py:408
  1018.1 73.0 %all-gather.4 = f32[32,2,1536]{2,1,0:T(2,128)S(1)} all-gather(f32[1,2,1536]{2,1,0:T(2,128)S(1)} %divide_bitcast_fusion), channel_id=1, replica_groups=mesh['dp'=8,'text'=4] {'dp','text'}, dimensions={0}, use_global_device_ids=true | all-gather | bytes 405504 | tf_op jit(solution)/shard_map/all_gather | solution.py:407
  1099.1 67.9 %all-gather.3 = f32[32,2,1536]{2,1,0:T(2,128)S(1)} all-gather(f32[1,2,1536]{2,1,0:T(2,128)S(1)} %bitcast.548), channel_id=1, replica_groups=mesh['dp'=8,'text'=4] {'dp','text'}, dimensions={0}, use_global_device_ids=true | all-gather | bytes 405504 | tf_op jit(solution)/shard_map/all_gather | solution.py:406
  1189.7 114.5 %all-gather.42.cloned.1.call-done = bf16[2,1024,1536]{2,1,0:T(8,128)(2,1)} async-done(((bf16[2,256,1536]{2,1,0:T(8,128)(2,1)}), bf16[2,1024,1536]{2,1,0:T(8,128)(2,1)}) %all-gather.42.cloned.1.call-update) | async-done | bytes 6291472 | tf_op jit(solution)/shard_map/all_gather | solution.py:438
  1304.2 25.9 multiply_convert_fusion.3
  1330.0 26.0 fusion.103
  1356.7 108.5 %reduce-scatter.32.cloned.1.call-done = bf16[2,256,1536]{2,1,0:T(8,128)(2,1)} async-done(((bf16[2,1024,1536]{2,1,0:T(8,128)(2,1)}), bf16[2,256,1536]{2,1,0:T(8,128)(2,1)}) %reduce-scatter.32.cloned.1.call-update) | async-done | bytes 1572880 | tf_op jit(solution)/shard_map/reduce_scatter | solution.py:445
  1534.8 244.1 %while.55 = (s32[]{:T(128)}, f32[2,256,24,64]{1,0,3,2:T(2,128)}, f32[2,1025,24,64]{1,3,2,0:T(8,128)}, f32[2,1025,24,64]{1,3,2,0:T(8,128)}, bf16[2,1025,24,64]{1,...) while((s32[]{:T(128)}, f32[2,256,24,64]{1,0,3,2:T(2,128)}, ...), condition=%wide.region_43.44_spmd, body=%wide.region_41.43_spmd.sunk | while | flops 4082806272 | bytes 225353872 | solution.py:170
  1566.6 21.3 multiply_convert_fusion.19
  1624.6 32.2 %dynamic_update_slice.63 = f32[2,256,24,64]{1,0,3,2:T(2,128)} dynamic-update-slice(f32[2,256,24,64]{1,0,3,2:T(2,128)} %get-tuple-element.1048, f32[1,256,24,64]{1,0,3,2:T(1,128)S(1)} %copy.610, s32[]{:T(128)S(6)} %copy.658, s32[]{:T(128)} %constant.106.clone.1..sunk, s32[]{:T(128)} %constant.106.clone.1..sunk, s32[]{:T(128)} %constant.106.clone.1..sunk) | dynamic-update-slice | bytes 3145732 | tf_op jit(solution)/shard_map/while/body/jit(dynamic_update_index_in_dim)/dynamic_update_slice | solution.py:170
  1746.4 32.2 %dynamic_update_slice.63 = f32[2,256,24,64]{1,0,3,2:T(2,128)} dynamic-update-slice(f32[2,256,24,64]{1,0,3,2:T(2,128)} %get-tuple-element.1048, f32[1,256,24,64]{1,0,3,2:T(1,128)S(1)} %copy.610, s32[]{:T(128)S(6)} %copy.658, s32[]{:T(128)} %constant.106.clone.1..sunk, s32[]{:T(128)} %constant.106.clone.1..sunk, s32[]{:T(128)} %constant.106.clone.1..sunk) | dynamic-update-slice | bytes 3145732 | tf_op jit(solution)/shard_map/while/body/jit(dynamic_update_index_in_dim)/dynamic_update_slice | solution.py:170
  1842.3 32.7 %convolution_convert_fusion = bf16[1536,2,8,192]{3,0,2,1:T(8,128)(2,1)} fusion(bf16[2048,1536,1,1]{1,0,3,2:T(8,128)(2,1)} %bitcast.554, bf16[2,8,192,2048]{3,2,1,0:T(8,128)(2,1)} %bitcast.505), kind=kOutput, calls=%fused_computation.126 | convolution fusion | flops 19332071424 | bytes 28311552 | tf_op jit(solution)/shard_map/rd,rg->dg/dot_general | solution.py:191
  1912.8 101.1 %reduce-scatter.34.cloned.1.call-done = bf16[2,256,1536]{1,2,0:T(8,128)(2,1)} async-done(((bf16[2,1024,1536]{1,2,0:T(8,128)(2,1)}), bf16[2,256,1536]{1,2,0:T(8,128)(2,1)}) %reduce-scatter.34.cloned.1.call-update) | async-done | bytes 1572880 | tf_op jit(solution)/shard_map/reduce_scatter | solution.py:511
  2218.8 22.4 select_convert_fusion
  2300.2 24.3 reduce-scatter.46.cloned.1.call-done
  2324.5 160.7 %reduce-scatter.42.cloned.1.call-done = bf16[32,192,192]{2,1,0:T(8,128)(2,1)} async-done(((bf16[256,192,192]{2,1,0:T(8,128)(2,1)}), bf16[32,192,192]{2,1,0:T(8,128)(2,1)}) %reduce-scatter.42.cloned.1.call-update) | async-done | bytes 2359312 | tf_op jit(solution)/shard_map/reduce_scatter | solution.py:580
  2488.9 54.1 %reduce-scatter.56.cloned.1.call-done = bf16[192,1536]{1,0:T(8,128)(2,1)} async-done(((bf16[1536,1536]{1,0:T(8,128)(2,1)}), bf16[192,1536]{1,0:T(8,128)(2,1)}) %reduce-scatter.56.cloned.1.call-update) | async-done | bytes 589840 | tf_op jit(solution)/shard_map/reduce_scatter | solution.py:595
  2565.6 84.4 %reduce-scatter.54.cloned.1.call-done = bf16[48,12288]{1,0:T(8,128)(2,1)} async-done(((bf16[192,12288]{1,0:T(8,128)(2,1)}), bf16[48,12288]{1,0:T(8,128)(2,1)}) %reduce-scatter.54.cloned.1.call-update) | async-done | bytes 1179664 | tf_op jit(solution)/shard_map/reduce_scatter | solution.py:621
  2652.5 22.4 reduce-scatter.62.cloned.1.call-done
  2696.0 34.1 %reduce-scatter.58.cloned.1.call-done = bf16[192,128]{1,0:T(8,128)(2,1)} async-done(((bf16[1536,128]{1,0:T(8,128)(2,1)}), bf16[192,128]{1,0:T(8,128)(2,1)}) %reduce-scatter.58.cloned.1.call-update) | async-done | bytes 49168
  2731.2 22.8 all-reduce.2
  2764.8 60.0 %reduce-scatter.44.cloned.1.call-done = bf16[8,192,192]{2,1,0:T(8,128)(2,1)} async-done(((bf16[32,192,192]{2,1,0:T(8,128)(2,1)}), bf16[8,192,192]{2,1,0:T(8,128)(2,1)}) %reduce-scatter.44.cloned.1.call-update) | async-done | bytes 589840 | tf_op jit(solution)/shard_map/reduce_scatter | solution.py:609
  2831.4 40.4 %all-reduce.3 = (f32[]{:T(128)}, f32[]{:T(128)}) all-reduce(f32[]{:T(128)S(6)} %mul.997, f32[]{:T(128)S(6)} %add.499), channel_id=1, replica_groups=mesh['dp'=8,'text'=4] {'dp','text'}, use_global_device_ids=true, to_apply=%region_19.20 | all-reduce | flops 2 | bytes 16 | tf_op jit(solution)/shard_map/psum | solution.py:630
  (805 shorter events, 1232.5 us)
Async XLA Ops:
  7.2 71.8 %all-gather.20.cloned.1.call-start = ((), (), s32[]{:S(2)}) async-start(), calls=%async_computation.19 | async-start | bytes 3932160 | tf_op jit(solution)/shard_map/all_gather | solution.py:272
  9.8 122.5 %all-gather.28.cloned.1.call-start = ((), (), s32[]{:S(2)}) async-start(), calls=%async_computation.23 | async-start | bytes 5308416 | tf_op jit(solution)/shard_map/all_gather | solution.py:287
  32.6 214.8 %all-gather.22.cloned.1.call-start = ((), (), s32[]{:S(2)}) async-start(), calls=%async_computation.20 | async-start | bytes 28311552 | tf_op jit(solution)/shard_map/all_gather | solution.py:285
  79.1 327.5 %all-gather.32.cloned.1.call-start = ((), (), s32[]{:S(2)}) async-start(), calls=%async_computation.25 | async-start | bytes 1474560 | tf_op jit(solution)/shard_map/all_gather | solution.py:273
  80.0 353.2 %all-gather.38.cloned.1.call-start = ((), (), s32[]{:S(2)}) async-start(), calls=%async_computation.28 | async-start | bytes 5898240 | tf_op jit(solution)/shard_map/all_gather | solution.py:276
  82.9 369.4 %all-gather.30.cloned.1.call-start = ((), (), s32[]{:S(2)}) async-start(), calls=%async_computation.24 | async-start | bytes 1966080 | tf_op jit(solution)/shard_map/all_gather | solution.py:362
  137.1 387.4 %all-gather.24.cloned.1.call-start = ((), (), s32[]{:S(2)}) async-start(), calls=%async_computation.21 | async-start | bytes 7864320 | tf_op jit(solution)/shard_map/all_gather | solution.py:337
  377.9 261.9 %all-gather.26.cloned.1.call-start = ((), (), s32[]{:S(2)}) async-start(), calls=%async_computation.22 | async-start | bytes 7864320 | tf_op jit(solution)/shard_map/all_gather | solution.py:336
  406.5 328.4 %all-gather.34.cloned.1.call-start = ((), (), s32[]{:S(2)}) async-start(), calls=%async_computation.26 | async-start | bytes 10616832 | tf_op jit(solution)/shard_map/all_gather | solution.py:286
  407.3 366.2 %all-gather.44.cloned.1.call-start = ((), (), s32[]{:S(2)}) async-start(), calls=%async_computation.45 | async-start | bytes 14155776 | tf_op jit(solution)/shard_map/all_gather | solution.py:289
  452.0 438.7 %all-gather.36.cloned.1.call-start = ((), (), s32[]{:S(2)}) async-start(), calls=%async_computation.27 | async-start | bytes 7864320 | tf_op jit(solution)/shard_map/all_gather | solution.py:375
  772.1 158.2 %all-gather.40.cloned.1.call-start = ((), (), s32[]{:S(2)}) async-start(), calls=%async_computation.29 | async-start | bytes 5308416 | tf_op jit(solution)/shard_map/all_gather | solution.py:290
  773.5 322.8 %reduce-scatter.30.cloned.1.call-start = ((), (), s32[]{:S(2)}) async-start(), calls=%async_computation.30 | async-start | bytes 7864320 | tf_op jit(solution)/shard_map/reduce_scatter | solution.py:380
  945.4 358.7 %all-gather.42.cloned.1.call-start = ((), (), s32[]{:S(2)}) async-start(), calls=%async_computation.31 | async-start | bytes 7864320 | tf_op jit(solution)/shard_map/all_gather | solution.py:438
  1189.4 275.8 %reduce-scatter.32.cloned.1.call-start = ((), (), s32[]{:S(2)}) async-start(), calls=%async_computation.32 | async-start | bytes 7864320 | tf_op jit(solution)/shard_map/reduce_scatter | solution.py:445
  1356.1 526.4 %reduce-scatter.50.cloned.1.call-start = ((), (), s32[]{:S(2)}) async-start(), calls=%async_computation.41 | async-start | bytes 1966080 | tf_op jit(solution)/shard_map/reduce_scatter | solution.py:483
  1510.2 398.9 %reduce-scatter.36.cloned.1.call-start = ((), (), s32[]{:S(2)}) async-start(), calls=%async_computation.34 | async-start | bytes 7864320 | tf_op jit(solution)/shard_map/reduce_scatter | solution.py:517
  1789.0 224.8 %reduce-scatter.34.cloned.1.call-start = ((), (), s32[]{:S(2)}) async-start(), calls=%async_computation.33 | async-start | bytes 7864320 | tf_op jit(solution)/shard_map/reduce_scatter | solution.py:511
  1799.2 458.0 %reduce-scatter.38.cloned.1.call-start = ((), (), s32[]{:S(2)}) async-start(), calls=%async_computation.35 | async-start | bytes 884736 | tf_op jit(solution)/shard_map/reduce_scatter | solution.py:577
  1842.2 415.8 %reduce-scatter.52.cloned.1.call-start = ((), (), s32[]{:S(2)}) async-start(), calls=%async_computation.42 | async-start | bytes 14155776 | tf_op jit(solution)/shard_map/reduce_scatter | solution.py:592
  1875.1 414.5 %reduce-scatter.60.cloned.1.call-start = ((), (), s32[]{:S(2)}) async-start(), calls=%async_computation.47 | async-start | bytes 5308416
  1893.8 404.2 %reduce-scatter.64.cloned.1.call-start = ((), (), s32[]{:S(2)}) async-start(), calls=%async_computation.49 | async-start | bytes 442368
  2067.3 257.2 %reduce-scatter.46.cloned.1.call-start = ((), (), s32[]{:S(2)}) async-start(), calls=%async_computation.39 | async-start | bytes 10616832 | tf_op jit(solution)/shard_map/reduce_scatter | solution.py:583
  2078.0 407.3 %reduce-scatter.42.cloned.1.call-start = ((), (), s32[]{:S(2)}) async-start(), calls=%async_computation.37 | async-start | bytes 28311552 | tf_op jit(solution)/shard_map/reduce_scatter | solution.py:580
  2241.3 301.8 %reduce-scatter.56.cloned.1.call-start = ((), (), s32[]{:S(2)}) async-start(), calls=%async_computation.44 | async-start | bytes 5308416 | tf_op jit(solution)/shard_map/reduce_scatter | solution.py:595
  2257.0 307.3 %reduce-scatter.40.cloned.1.call-start = ((), (), s32[]{:S(2)}) async-start(), calls=%async_computation.36 | async-start | bytes 122880 | tf_op jit(solution)/shard_map/reduce_scatter | solution.py:606
  2257.5 392.4 %reduce-scatter.54.cloned.1.call-start = ((), (), s32[]{:S(2)}) async-start(), calls=%async_computation.43 | async-start | bytes 5898240 | tf_op jit(solution)/shard_map/reduce_scatter | solution.py:621
  2289.5 385.4 %reduce-scatter.62.cloned.1.call-start = ((), (), s32[]{:S(2)}) async-start(), calls=%async_computation.48 | async-start | bytes 737280 | tf_op jit(solution)/shard_map/reduce_scatter | solution.py:615
  2290.3 404.3 %reduce-scatter.66.cloned.1.call-start = ((), (), s32[]{:S(2)}) async-start(), calls=%async_computation.50 | async-start | bytes 61440
  2298.0 432.1 %reduce-scatter.58.cloned.1.call-start = ((), (), s32[]{:S(2)}) async-start(), calls=%async_computation.46 | async-start | bytes 442368
  2300.2 462.9 %reduce-scatter.48.cloned.1.call-start = ((), (), s32[]{:S(2)}) async-start(), calls=%async_computation.40 | async-start | bytes 1474560 | tf_op jit(solution)/shard_map/reduce_scatter | solution.py:612
  2324.5 500.3 %reduce-scatter.44.cloned.1.call-start = ((), (), s32[]{:S(2)}) async-start(), calls=%async_computation.38 | async-start | bytes 3932160 | tf_op jit(solution)/shard_map/reduce_scatter | solution.py:609
  (184 other events, 7465.3 us)
Sparse Core Ops, SparseCore 0:
  10.2 68.7 all-gather.19
  80.9 38.1 all-gather.27
  121.0 126.3 all-gather.21
  249.4 30.4 all-gather.31
  281.9 88.5 all-gather.37
  372.5 35.5 all-gather.29
  410.2 114.1 all-gather.23
  526.6 113.2 all-gather.25
  641.7 57.0 all-gather.33
  701.1 72.1 all-gather.43
  775.4 115.3 all-gather.35
  893.1 37.0 all-gather.39
  945.5 115.8 reduce-scatter.29
  1189.5 114.5 all-gather.41
  1356.2 108.9 reduce-scatter.31
  1510.3 35.8 reduce-scatter.49
  1789.2 111.2 reduce-scatter.35
  1902.6 111.2 reduce-scatter.33
  2017.6 35.5 reduce-scatter.37
  2056.5 92.4 reduce-scatter.51
  2152.4 53.8 reduce-scatter.59
  2210.2 33.7 reduce-scatter.63
  2248.0 76.4 reduce-scatter.45
  2328.4 156.8 reduce-scatter.41
  2489.1 53.8 reduce-scatter.55
  2545.1 19.0 reduce-scatter.39
  2566.5 83.4 reduce-scatter.53
  2652.4 22.4 reduce-scatter.61
  2677.2 17.3 reduce-scatter.65
  2698.1 32.0 reduce-scatter.57
  2732.4 30.5 reduce-scatter.47
  2765.4 59.3 reduce-scatter.43
where the time goes:
time: 2940 us; the launch traced here: 2920 us
  waiting for transfers between devices  1200 us (41%)
  local copies, waits for them, and re-layouts  557 us (19%)
  matrix products  506 us (17%)
  blocking collectives  362 us (12%)
  other arithmetic  268 us (9%)
    reduce_scatter x1, waiting for transfers between devices, shards(): lax.psum_scatter(grad_slots.astype(jnp.bfloat16), 'dp', scatter_dimension...  161 us
    all_gather x1, waiting for transfers between devices, shards(): lax.all_gather(grad_down_in.reshape(item_count, frames_dev, D), 'text', a...  114 us
    all_gather x1, waiting for transfers between devices, shards(): lax.all_gather(group_set[2], 'dp', axis=0, tiled=True)  110 us
    reduce_scatter x1, waiting for transfers between devices, shards(): lax.psum_scatter(grad_feed_in.reshape(item_count, -1, D).astype(jnp.bfloa...  109 us
    reduce_scatter x1, waiting for transfers between devices, shards(): lax.psum_scatter(grad_keys[:, 1:].reshape(item_count, key_count - 1, D).a...  101 us
    all_gather x1, waiting for transfers between devices, shards(): lax.all_gather(input_three.reshape(item_count, frames_dev, D), 'text', ax...  100 us
    all_gather x1, waiting for transfers between devices, shards(): lax.all_gather(rot_keys.reshape(item_count, frames_dev, D), 'text', axis=...  96.1 us
    reduce_scatter x1, waiting for transfers between devices, shards(): lax.psum_scatter(spread_gate.astype(jnp.bfloat16), 'text', scatter_dimens...  84.4 us
  transfers between devices with their start and end apart: 32, of which 19 were waited for; matrix products, arithmetic and copies ran while one was open for 38% of the time, Pallas kernels for 0%

commit v1 on v0

--- a/solution.py
+++ b/solution.py
@@ -4,7 +4,9 @@
 import jax
 import jax.numpy as jnp
 from jax import lax
-from jax.sharding import PartitionSpec as P
+from jax.experimental import pallas as pl
+from jax.experimental.pallas import tpu as pltpu
+from jax.sharding import Mesh, PartitionSpec as P
 
 D = 1536
 HEADS = 24
@@ -630,7 +632,6 @@
     totals = lax.psum((square_sum, loss_part), ("dp", "text"))
     loss_total = totals[1] + CONTRAST_WEIGHT * contrast_value / items_total
     gradient_norm = jnp.sqrt(totals[0])
-    factor = CLIP_NORM / jnp.maximum(gradient_norm, CLIP_NORM)
     masters = (
         end_weights,
         time_table,
@@ -661,6 +662,775 @@
         second_down,
         second_gains,
     )
+    return finish(
+        loss_total,
+        gradient_norm,
+        reduced,
+        masters,
+        firsts,
+        seconds,
+        (left_stats, right_stats, left_roots, right_roots),
+    )
+
+
+def swap(values, axis, bit=1):
+    return lax.ppermute(values, axis, [(i, i ^ bit) for i in range(lax.axis_size(axis))])
+
+
+def pick(values, position, axis=0):
+    return lax.dynamic_index_in_dim(values, position, axis, keepdims=False)
+
+
+def grow(values, axis):
+    bit = 1
+    while bit < lax.axis_size(axis):
+        values = jnp.concatenate([values, swap(values, axis, bit)], 0)
+        bit *= 2
+    return values
+
+
+def own_quarters(values, core, line):
+    pair = jnp.concatenate([values, swap(values, "c")], 0)
+    pieces = []
+    for offset in range(4):
+        target = line ^ offset
+        piece = pick(pair, ((target // 2) ^ core) * 2 + target % 2)
+        pieces.append(swap(piece, "z", offset) if offset else piece)
+    return jnp.concatenate(pieces, 0)
+
+
+def gather_pieces(block, first, second):
+    base = grow(block[None], "z")
+    near = swap(base, first)
+    across = swap(base, second)
+    far = swap(near, second)
+    return (base, near, across, far) if first == "x" else (base, across, near, far)
+
+
+def place_kernel(spot, *refs):
+    sources, target = refs[:4], refs[4]
+    quadrant = pl.program_id(0)
+    pair = target.shape[1] == 2
+    for index_value, source in enumerate(sources):
+
+        @pl.when(quadrant == index_value)
+        def store():
+            if pair:
+                target[0, spot[2], 0] = source[0, 0]
+                target[0, 1 - spot[2], 0] = source[0, 1]
+            else:
+                target[0, 0, 0] = source[0, 0]
+
+
+def place(pieces, spot):
+    lines, cores, height, width = pieces[0].shape
+
+    def source_map(index_value):
+        def at(quadrant, line, where):
+            return (jnp.clip((quadrant - index_value) * lines + line, 0, lines - 1), 0, 0, 0)
+
+        return at
+
+    placed = pl.pallas_call(
+        place_kernel,
+        grid_spec=pltpu.PrefetchScalarGridSpec(
+            num_scalar_prefetch=1,
+            grid=(4, lines),
+            in_specs=[
+                pl.BlockSpec((1, cores, height, width), source_map(index_value))
+                for index_value in range(4)
+            ],
+            out_specs=pl.BlockSpec(
+                (1, cores, 1, height, width),
+                lambda quadrant, line, where: (where[0] ^ quadrant, 0, where[1] ^ line, 0, 0),
+            ),
+        ),
+        out_shape=jax.ShapeDtypeStruct((4, cores, lines, height, width), pieces[0].dtype),
+        cost_estimate=pl.CostEstimate(
+            flops=0, bytes_accessed=16 * lines * cores * height * width, transcendentals=0
+        ),
+    )(spot, *pieces)
+    return placed.reshape(4 * cores * lines * height, width)
+
+
+def half_block(tile, is_right, to_right):
+    wide = tile.astype(jnp.float32)
+    turned = pltpu.roll(wide, BLK, 1)
+    return jnp.where(is_right == to_right, wide, turned)
+
+
+def assemble_kernel(left_at, right_at, left_half, right_half, left, right, target):
+    step = pl.program_id(0)
+    left_tile = half_block(left[0], left_half[step], 0)
+    right_tile = half_block(right[0], right_half[step], 1)
+    lane = lax.broadcasted_iota(jnp.int32, left_tile.shape, 1)
+    target[...] = jnp.where(lane < BLK, left_tile, right_tile).astype(target.dtype)
+
+
+def assemble(pairs, places, rights, rows, columns):
+    steps = places.shape[0] // 2
+    across = columns // (2 * BLK)
+    return pl.pallas_call(
+        assemble_kernel,
+        grid_spec=pltpu.PrefetchScalarGridSpec(
+            num_scalar_prefetch=4,
+            grid=(steps,),
+            in_specs=[
+                pl.BlockSpec((1, BLK, 2 * BLK), lambda step, a, b, c, d: (a[step], 0, 0)),
+                pl.BlockSpec((1, BLK, 2 * BLK), lambda step, a, b, c, d: (b[step], 0, 0)),
+            ],
+            out_specs=pl.BlockSpec(
+                (BLK, 2 * BLK), lambda step, a, b, c, d: (step // across, step % across)
+            ),
+        ),
+        out_shape=jax.ShapeDtypeStruct((rows, columns), pairs.dtype),
+        cost_estimate=pl.CostEstimate(flops=0, bytes_accessed=6 * rows * columns, transcendentals=0),
+    )(places[0::2], places[1::2], rights[0::2], rights[1::2], pairs, pairs)
+
+
+def collect_kernel(left_at, right_at, left_half, right_half, left, right, target):
+    step = pl.program_id(0)
+    left_tile = half_block(left[...], left_half[step] % 2, 0)
+    right_tile = half_block(right[...], right_half[step] % 2, 1)
+    left_tile = jnp.where(left_half[step] < 2, left_tile, 0.0)
+    right_tile = jnp.where(right_half[step] < 2, right_tile, 0.0)
+    lane = lax.broadcasted_iota(jnp.int32, left_tile.shape, 1)
+    target[0] = jnp.where(lane < BLK, left_tile, right_tile).astype(target.dtype)
+
+
+def collect(matrix, places, halves):
+    steps = places.shape[0] // 2
+    across = matrix.shape[1] // (2 * BLK)
+    return pl.pallas_call(
+        collect_kernel,
+        grid_spec=pltpu.PrefetchScalarGridSpec(
+            num_scalar_prefetch=4,
+            grid=(steps,),
+            in_specs=[
+                pl.BlockSpec(
+                    (BLK, 2 * BLK), lambda step, a, b, c, d: (a[step] // across, a[step] % across)
+                ),
+                pl.BlockSpec(
+                    (BLK, 2 * BLK), lambda step, a, b, c, d: (b[step] // across, b[step] % across)
+                ),
+            ],
+            out_specs=pl.BlockSpec((1, BLK, 2 * BLK), lambda step, a, b, c, d: (step, 0, 0)),
+        ),
+        out_shape=jax.ShapeDtypeStruct((steps, BLK, 2 * BLK), matrix.dtype),
+        cost_estimate=pl.CostEstimate(
+            flops=0, bytes_accessed=6 * matrix.size, transcendentals=0
+        ),
+    )(places[0::2], places[1::2], halves[0::2], halves[1::2], matrix, matrix)
+
+
+def low_sum(*terms):
+    total = terms[0].astype(jnp.float32)
+    for term in terms[1:]:
+        total = total + term.astype(jnp.float32)
+    return total
+
+
+def reduce_quads(quads, first, line, line_axis):
+    mine, near_x, near_y, far = quads
+    if first == "y":
+        from_far = swap(far, "y")
+        from_side = swap(near_y, "y")
+        onward = low_sum(near_x, from_far).astype(jnp.bfloat16)
+        from_onward = swap(onward, "x")
+    else:
+        from_far = swap(far, "x")
+        from_side = swap(near_x, "x")
+        onward = low_sum(near_y, from_far).astype(jnp.bfloat16)
+        from_onward = swap(onward, "y")
+    return reduce_line((mine, from_side, from_onward), line, line_axis)
+
+
+def reduce_line(terms, line, line_axis):
+    def part(index_value):
+        return low_sum(*[pick(term, index_value, line_axis) for term in terms])
+
+    far_send = jnp.stack(
+        [part((line ^ 2) & 2), part(((line ^ 2) & 2) + 1)], 0
+    ).astype(jnp.bfloat16)
+    received = swap(far_send, "z", 2)
+    near_send = part(line ^ 1) + pick(received, (line ^ 1) % 2).astype(jnp.float32)
+    last = swap(near_send.astype(jnp.bfloat16), "z", 1)
+    return part(line) + low_sum(pick(received, line % 2), last)
+
+
+def reduce_small(values, row, column, line):
+    for axis, me in (("y", row), ("x", column)):
+        received = swap(pick(values, 1 - me).astype(jnp.bfloat16), axis)
+        values = pick(values, me) + received.astype(jnp.float32)
+    return reduce_line((values,), line, 0)
+
+
+def on_both(partial_sum):
+    low = partial_sum.astype(jnp.bfloat16)
+    return low_sum(low, swap(low, "c"))
+
+
+def tdot(left, right):
+    return lax.dot_general(left, right, (((0,), (0,)), ((), ())), preferred_element_type=jnp.float32)
+
+
+def dot_back(left, right):
+    return lax.dot_general(left, right, (((1,), (1,)), ((), ())), preferred_element_type=jnp.float32)
+
+
+def item_per_chip(
+    latents,
+    noise_field,
+    timesteps,
+    text_tokens,
+    text_lengths,
+    negatives,
+    assignment,
+    end_weights,
+    time_table,
+    square_slots,
+    cross_weights,
+    key_value,
+    gate_up,
+    down_weight,
+    norm_gains,
+    first_ends,
+    second_ends,
+    first_table,
+    second_table,
+    first_cross,
+    second_cross,
+    first_key_value,
+    second_key_value,
+    first_gate_up,
+    second_gate_up,
+    first_down,
+    second_down,
+    first_gains,
+    second_gains,
+    left_stats,
+    right_stats,
+    left_roots,
+    right_roots,
+):
+    bf16, f32 = jnp.bfloat16, jnp.float32
+    row, column = lax.axis_index("y"), lax.axis_index("x")
+    core, line = lax.axis_index("c"), lax.axis_index("z")
+    plane = 2 * row + column
+    item = 4 * plane + line
+    spot = jnp.stack([plane, line, core]).astype(jnp.int32)
+    quads = range(4)
+    half = D // 2
+    heads = HEADS // 2
+    items_total = 16
+    mse_scale = 1.0 / (items_total * FRAMES * DIN)
+
+    pack = jnp.concatenate(
+        [
+            end_weights.reshape(4, D),
+            time_table,
+            jnp.pad(norm_gains.reshape(1, 144), ((0, 3), (0, D - 144))),
+        ],
+        0,
+    ).astype(bf16)
+    packs = pack[None]
+    for axis in ("c", "z", "x", "y"):
+        packs = grow(packs, axis)
+    owner = jnp.arange(32, dtype=jnp.int32)
+    packs = packs[
+        ((owner // 4) % 2 ^ core) + 2 * (owner % 4 ^ line) + 8 * (owner // 8 ^ plane)
+    ]
+    ends_full = packs[:, :4].reshape(D, 2, DIN)
+    table_full = packs[:, 4:12].reshape(NTIME, D)
+    gain_values = packs[:, 12, :144].reshape(D, 3).astype(f32)
+    weight_in, weight_out = ends_full[:, 0, :], ends_full[:, 1, :]
+
+    low_slots = square_slots.astype(bf16).reshape(4, 2, BLK, BLK)
+    low_pairs = jnp.concatenate([low_slots[:, 0], low_slots[:, 1]], 2)
+    slot_pieces = []
+    for color, (first, second) in enumerate((("x", "y"), ("y", "x"))):
+        pieces = gather_pieces(low_pairs[2 * color : 2 * color + 2], first, second)
+        slot_pieces.append(jnp.concatenate(pieces, 0))
+    own_pairs = jnp.concatenate(slot_pieces, 0).reshape(64, BLK, 2 * BLK)
+    all_pairs = jnp.concatenate([own_pairs, swap(own_pairs, "c")], 0)
+    inverse_order = (
+        jnp.zeros_like(assignment)
+        .at[assignment]
+        .set(jnp.arange(assignment.shape[0], dtype=jnp.int32))
+    )
+
+    def pair_place(slot):
+        device, inner = slot // 8, slot % 8
+        place_value = ((device // 4) % 2 ^ core) * 2 + inner // 4
+        place_value = (place_value * 4 + (device // 8 ^ plane)) * 4 + (device % 4 ^ line)
+        return place_value * 2 + (inner // 2) % 2, inner % 2
+
+    def grid_blocks(matrix, rows, columns):
+        return (matrix * 64 + rows * 8 + columns).reshape(-1)
+
+    eight, four = jnp.arange(8, dtype=jnp.int32), jnp.arange(4, dtype=jnp.int32)
+    joined_blocks = grid_blocks(
+        jnp.arange(3, dtype=jnp.int32)[None, :, None],
+        eight[:, None, None],
+        (4 * core + four)[None, None, :],
+    )
+    out_blocks = grid_blocks(3, (4 * core + four)[:, None], eight[None, :])
+    places, rights = pair_place(inverse_order[joined_blocks])
+    projection = assemble(all_pairs, places, rights, D, 3 * half)
+    places, rights = pair_place(inverse_order[out_blocks])
+    weight_mix = assemble(all_pairs, places, rights, half, D)
+
+    low_cross = cross_weights.astype(bf16)
+    query_both = jnp.stack(
+        [
+            lax.dynamic_slice_in_dim(low_cross[:, 0, :], core * half, half, 1),
+            swap(
+                lax.dynamic_slice_in_dim(low_cross[:, 0, :], (1 - core) * half, half, 1), "c"
+            ),
+        ],
+        0,
+    )
+    cross_query = place(gather_pieces(query_both, "x", "y"), spot)
+    out_own = place(gather_pieces(low_cross[None, :, 1, :], "y", "x"), spot)
+    out_own = out_own.reshape(2, 2, 1, 4 * 48, D)
+    out_kept = pick(out_own, core)
+    out_other = swap(pick(out_own, 1 - core), "c")
+    cross_out = jnp.where(
+        core == 0,
+        jnp.concatenate([out_kept, out_other], 1),
+        jnp.concatenate([out_other, out_kept], 1),
+    ).reshape(half, D)
+    low_kv = key_value.astype(bf16)
+    kv_weights = []
+    for color, (first, second) in enumerate((("x", "y"), ("y", "x"))):
+        own = lax.dynamic_slice_in_dim(low_kv, color * D + core * half, half, 1)
+        other = lax.dynamic_slice_in_dim(low_kv, color * D + (1 - core) * half, half, 1)
+        pieces = gather_pieces(jnp.stack([own, swap(other, "c")], 0), first, second)
+        stacked = jnp.stack(pieces, 0)
+        stacked = stacked[plane ^ four][:, line ^ four]
+        stacked = stacked[:, :, core ^ four[:2]]
+        kv_weights.append(stacked.transpose(0, 2, 1, 3, 4).reshape(DT, half))
+    kv_own = jnp.concatenate(kv_weights, 1)
+
+    low_gate = gate_up.astype(bf16)
+
+    def unit_columns(which, side):
+        return jnp.concatenate(
+            [
+                lax.dynamic_slice_in_dim(
+                    low_gate, which * FF + quadrant * 1536 + side * 768, 768, 1
+                )
+                for quadrant in quads
+            ],
+            1,
+        )
+
+    gate_sides = []
+    for which, (first, second) in enumerate((("x", "y"), ("y", "x"))):
+        block = jnp.stack(
+            [unit_columns(which, core), swap(unit_columns(which, 1 - core), "c")], 0
+        )
+        gate_sides.append(place(gather_pieces(block, first, second), spot))
+    gate_weight, up_weight = gate_sides
+    low_down = down_weight.astype(bf16)
+    down_sides = []
+    for which, (first, second) in enumerate((("x", "y"), ("y", "x"))):
+        block = low_down[None, :, which * half : (which + 1) * half]
+        down_sides.append(place(gather_pieces(block, first, second), spot))
+
+    meta = jnp.concatenate([timesteps[:, None], text_lengths[:, None], negatives], 1)
+    metas = meta
+    for axis in ("c", "x", "y"):
+        metas = grow(metas, axis)
+    base = 4 * plane + 2 * core
+    relative = jnp.arange(items_total, dtype=jnp.int32)
+    metas = metas[(item ^ base) ^ relative]
+    timestep, text_length = metas[0, 0], metas[0, 1]
+    negative_rows = metas[:, 2:]
+    frames = own_quarters(jnp.concatenate([latents, noise_field], 2), core, line)
+    clean, noise = frames[:, :DIN], frames[:, DIN:]
+    tokens = own_quarters(text_tokens, core, line)
+    quarter = line ^ four
+    frame_positions = (
+        (quarter[:, None] * 256 + jnp.arange(256, dtype=jnp.int32)[None, :]).reshape(-1) + 1
+    )
+    token_slots = (
+        quarter[:, None] * 32 + jnp.arange(32, dtype=jnp.int32)[None, :]
+    ).reshape(-1)
+    halfway = HD // 2
+    frequency = jnp.exp(jnp.arange(halfway, dtype=f32) * (-2.0 * math.log(10000.0) / HD))
+    turn = frame_positions.astype(f32)[:, None] * frequency[None, :]
+    cosine_table = jnp.concatenate([jnp.cos(turn)] * 2, -1)
+    sine_table = jnp.concatenate([jnp.sin(turn)] * 2, -1)
+    angle = (timestep.astype(f32) + 0.5) * (0.5 * math.pi / NTIME)
+    signal, spread = jnp.cos(angle), jnp.sin(angle)
+    noised = (signal * clean + spread * noise).astype(bf16)
+    target = signal * noise - spread * clean
+
+    residual = dot_back(noised, weight_in)
+    normed_one, inverse_one = layer_stats(residual)
+    input_one = (normed_one * gain_values[:, 0]).astype(bf16)
+    features = time_features(timestep[None]).astype(bf16)
+    embeds = jnp.dot(features, table_full, preferred_element_type=f32)
+    normed_time, inverse_time = layer_stats(embeds)
+    input_time = (normed_time * gain_values[:, 0]).astype(bf16)
+    joined_rows = jnp.dot(input_one, projection, preferred_element_type=f32)
+    head_shape = (FRAMES, heads, HD)
+    rot_queries = rotate(
+        joined_rows[:, :half].reshape(head_shape), cosine_table, sine_table
+    ).astype(bf16)
+    rot_keys = rotate(
+        joined_rows[:, half : 2 * half].reshape(head_shape), cosine_table, sine_table
+    ).astype(bf16)
+    value_rows = joined_rows[:, 2 * half :].astype(bf16)
+    time_pair = jnp.dot(input_time, projection[:, half:], preferred_element_type=f32).astype(bf16)
+    all_keys = jnp.concatenate([time_pair[:, :half].reshape(1, heads, HD), rot_keys], 0)
+    all_values = jnp.concatenate([time_pair[:, half:], value_rows], 0).reshape(-1, heads, HD)
+    self_bias = jnp.zeros((1, FRAMES + 1), f32)
+    mixed_self, logsum_self = attend_forward(
+        rot_queries[None], all_keys[None], all_values[None], self_bias
+    )
+    mixed_flat = mixed_self.reshape(FRAMES, half)
+    after_self = residual + on_both(jnp.dot(mixed_flat, weight_mix, preferred_element_type=f32))
+    normed_two, inverse_two = layer_stats(after_self)
+    input_two = (normed_two * gain_values[:, 1]).astype(bf16)
+    cross_queries = jnp.dot(input_two, cross_query, preferred_element_type=f32).astype(bf16)
+    cross_heads = cross_queries.reshape(head_shape)
+    projected = jnp.dot(tokens, kv_own, preferred_element_type=f32).astype(bf16)
+    valid = token_slots < text_length
+    cross_bias = jnp.where(valid, 0.0, MASK_VALUE).astype(f32)[None]
+    text_keys = projected[:, :half].reshape(1, -1, heads, HD)
+    text_values = projected[:, half:].reshape(1, -1, heads, HD)
+    mixed_cross, logsum_cross = attend_forward(
+        cross_heads[None], text_keys, text_values, cross_bias
+    )
+    cross_flat = mixed_cross.reshape(FRAMES, half)
+    after_cross = after_self + on_both(jnp.dot(cross_flat, cross_out, preferred_element_type=f32))
+    normed_three, inverse_three = layer_stats(after_cross)
+    input_three = (normed_three * gain_values[:, 2]).astype(bf16)
+    gate_part = jnp.dot(input_three, gate_weight, preferred_element_type=f32)
+    up_part = jnp.dot(input_three, up_weight, preferred_element_type=f32)
+    sigmoid = jax.nn.sigmoid(gate_part)
+    silu_value = gate_part * sigmoid
+    hidden = (silu_value * up_part).astype(bf16)
+    down_out = jnp.concatenate(
+        [on_both(jnp.dot(hidden, side, preferred_element_type=f32)) for side in down_sides], 1
+    )
+    output_rows = after_cross + down_out
+    output_low = output_rows.astype(bf16)
+    predicted = jnp.dot(output_low, weight_out, preferred_element_type=f32)
+    errors = predicted - target
+
+    length_float = text_length.astype(f32)
+    mask = valid.astype(f32)[:, None]
+    text_half = jnp.sum(projected[:, :half].astype(f32) * mask, 0) / length_float
+    text_rest = swap(text_half, "c")
+    text_pool = jnp.where(
+        core == 0,
+        jnp.concatenate([text_half, text_rest]),
+        jnp.concatenate([text_rest, text_half]),
+    )
+    pools = jnp.stack([jnp.sum(output_rows, 0) / FRAMES, text_pool], 0)[None]
+    for axis in ("z", "x", "y"):
+        pools = grow(pools, axis)
+    inverse_pools = lax.rsqrt(jnp.sum(pools * pools, -1, keepdims=True) + POOL_EPS)
+    units = pools * inverse_pools
+    audio_units, text_units = units[:, 0], units[:, 1]
+    similar = (
+        lax.dot_general(
+            audio_units, text_units, (((1,), (1,)), ((), ())), precision=BEST_PRECISION
+        )
+        / CONTRAST_TEMP
+    )
+    same = jnp.eye(items_total, dtype=f32)
+    counts = same + jnp.sum(
+        (negative_rows[:, None, :] == (item ^ relative)[None, :, None]).astype(f32), -1
+    )
+    peak = jnp.max(jnp.where(counts > 0, similar, -jnp.inf), -1, keepdims=True)
+    powers = jnp.where(counts > 0, counts * jnp.exp(similar - peak), 0.0)
+    totals_row = jnp.sum(powers, -1, keepdims=True)
+    contrast_own = peak[0, 0] + jnp.log(totals_row[0, 0]) - similar[0, 0]
+    grad_similar = (powers / totals_row - same) * (
+        CONTRAST_WEIGHT / items_total / CONTRAST_TEMP
+    )
+    grad_audio_unit = jnp.sum(grad_similar[0][:, None] * text_units, 0)
+    grad_text_unit = jnp.sum(grad_similar[:, 0][:, None] * audio_units, 0)
+
+    def unit_back(gradient, unit, inverse):
+        return inverse * (gradient - unit * jnp.sum(unit * gradient))
+
+    grad_audio = unit_back(grad_audio_unit, audio_units[0], inverse_pools[0, 0])
+    grad_text = unit_back(grad_text_unit, text_units[0], inverse_pools[0, 1])
+
+    grad_predicted = (2.0 * mse_scale * errors).astype(bf16)
+    grad_out_weight = tdot(output_low, grad_predicted)
+    grad_output = dot_back(grad_predicted, weight_out) + grad_audio[None, :] / FRAMES
+    grad_low = grad_output.astype(bf16)
+    reduced_down = []
+
+    def columns_of(values, quadrant, width):
+        return lax.dynamic_slice_in_dim(values, (plane ^ quadrant) * width, width, 1)
+
+    for which, first in enumerate(("y", "x")):
+        parts = [
+            tdot(
+                columns_of(hidden, quadrant, 768), grad_low[:, which * half : (which + 1) * half]
+            )
+            .astype(bf16)
+            .reshape(4, 192, half)
+            for quadrant in quads
+        ]
+        reduced_down.append(reduce_quads(parts, first, line, 0))
+    grad_down = jnp.concatenate(reduced_down, 1)
+    grad_hidden = dot_back(grad_low[:, :half], down_sides[0]) + dot_back(
+        grad_low[:, half:], down_sides[1]
+    )
+    grad_gate = (grad_hidden * up_part * sigmoid * (1.0 + gate_part * (1.0 - sigmoid))).astype(bf16)
+    grad_up = (grad_hidden * silu_value).astype(bf16)
+    reduced_gate = []
+    for gradient, first in ((grad_gate, "y"), (grad_up, "x")):
+        parts = [
+            tdot(columns_of(input_three, quadrant, 384), gradient)
+            .astype(bf16)
+            .reshape(2, 4, 48, FF // 2)
+            for quadrant in quads
+        ]
+        both_rows = reduce_quads(parts, first, line, 1)
+        other = swap(pick(both_rows, 1 - core).astype(bf16), "c").astype(f32)
+        reduced_gate.append((pick(both_rows, core), other))
+    gate_columns = []
+    for mine, other in reduced_gate:
+        sides = (jnp.where(core == 0, mine, other), jnp.where(core == 0, other, mine))
+        for quadrant in quads:
+            for side in sides:
+                gate_columns.append(side[:, quadrant * 768 : (quadrant + 1) * 768])
+    grad_gate_up = jnp.concatenate(gate_columns, 1)
+    grad_input_three = on_both(dot_back(grad_gate, gate_weight) + dot_back(grad_up, up_weight))
+    grad_after_cross, gain_three = layer_back(
+        grad_input_three, normed_three, inverse_three, gain_values[:, 2]
+    )
+    grad_after_cross = grad_after_cross + grad_output
+    grad_cross_in = grad_after_cross.astype(bf16)
+    cross_rows = tdot(cross_flat, grad_cross_in).astype(bf16).reshape(2, 2, 192, D)
+    cross_kept = pick(cross_rows, core, 1)
+    cross_received = swap(pick(cross_rows, 1 - core, 1), "c")
+    cross_pair = jnp.stack([cross_kept, cross_received], 0)
+    parts = [
+        pick(pick(cross_pair, row ^ (quadrant // 2) ^ core), column ^ (quadrant % 2)).reshape(
+            4, 48, D
+        )
+        for quadrant in quads
+    ]
+    grad_cross_out = reduce_quads(parts, "x", line, 0)
+    grad_mixed_cross = dot_back(grad_cross_in, cross_out).astype(bf16).reshape(head_shape)
+    grad_cq, grad_text_keys, grad_text_values = attend_backward(
+        cross_heads[None],
+        text_keys,
+        text_values,
+        cross_bias,
+        logsum_cross,
+        grad_mixed_cross[None],
+    )
+    grad_cq_low = grad_cq.reshape(FRAMES, half).astype(bf16)
+    parts = [
+        tdot(columns_of(input_two, quadrant, 384), grad_cq_low).astype(bf16).reshape(2, 4, 48, half)
+        for quadrant in quads
+    ]
+    both_rows = reduce_quads(parts, "y", line, 1)
+    query_other = swap(pick(both_rows, 1 - core).astype(bf16), "c").astype(f32)
+    query_mine = pick(both_rows, core)
+    grad_cross_query = jnp.where(
+        core == 0,
+        jnp.concatenate([query_mine, query_other], 1),
+        jnp.concatenate([query_other, query_mine], 1),
+    )
+    grad_cross = jnp.stack([grad_cross_query, grad_cross_out], 1)
+    grad_input_two = on_both(dot_back(grad_cq_low, cross_query))
+    text_half_grad = lax.dynamic_slice_in_dim(grad_text, core * half, half, 0)
+    grad_pair_keys = (
+        grad_text_keys.reshape(-1, half) + mask * (text_half_grad[None, :] / length_float)
+    ).astype(bf16)
+    grad_pair_values = grad_text_values.reshape(-1, half).astype(bf16)
+    kv_columns = []
+    for gradient, first in ((grad_pair_keys, "y"), (grad_pair_values, "x")):
+        parts = [
+            tdot(columns_of(tokens, quadrant, 192), gradient).astype(bf16).reshape(2, 4, 24, half)
+            for quadrant in quads
+        ]
+        both_rows = reduce_quads(parts, first, line, 1)
+        other = swap(pick(both_rows, 1 - core).astype(bf16), "c").astype(f32)
+        mine = pick(both_rows, core)
+        kv_columns.append(jnp.where(core == 0, mine, other))
+        kv_columns.append(jnp.where(core == 0, other, mine))
+    grad_key_value = jnp.concatenate(kv_columns, 1)
+    grad_after_self, gain_two = layer_back(
+        grad_input_two, normed_two, inverse_two, gain_values[:, 1]
+    )
+    grad_after_self = grad_after_self + grad_after_cross
+    grad_self_in = grad_after_self.astype(bf16)
+    grad_mix = tdot(mixed_flat, grad_self_in).astype(bf16)
+    grad_mixed_self = dot_back(grad_self_in, weight_mix).astype(bf16).reshape(head_shape)
+    grad_rot_queries, grad_keys, grad_values = attend_backward(
+        rot_queries[None],
+        all_keys[None],
+        all_values[None],
+        self_bias,
+        logsum_self,
+        grad_mixed_self[None],
+    )
+    grad_queries = rotate_back(grad_rot_queries[0], cosine_table, sine_table)
+    grad_key_rows = rotate_back(grad_keys[0, 1:], cosine_table, sine_table)
+    grad_joined = jnp.concatenate(
+        [
+            grad_queries.astype(bf16).reshape(FRAMES, half),
+            grad_key_rows.astype(bf16).reshape(FRAMES, half),
+            grad_values[0, 1:].astype(bf16).reshape(FRAMES, half),
+        ],
+        1,
+    )
+    grad_time_pair = jnp.concatenate(
+        [grad_keys[0, 0].reshape(1, half), grad_values[0, 0].reshape(1, half)], 1
+    )
+    grad_projection = tdot(input_one, grad_joined)
+    time_rows = input_time.astype(f32).reshape(D, 1) * grad_time_pair
+    grad_projection = jnp.concatenate(
+        [
+            grad_projection[:, :half].astype(bf16),
+            (grad_projection[:, half:] + time_rows).astype(bf16),
+            jnp.concatenate([grad_mix[:, :half], grad_mix[:, half:]], 0),
+        ],
+        1,
+    )
+
+    position = jnp.arange(256, dtype=jnp.int32)
+    owner_core = core ^ (position // 128)
+    owner_plane = plane ^ ((position // 16) % 4)
+    owner_line = (position // 4) % 4
+    inner = ((position // 64) % 2) * 4 + position % 4
+    block = assignment[owner_plane * 64 + owner_core * 32 + owner_line * 8 + inner]
+    matrix, block_row, block_column = block // 64, (block // 8) % 8, block % 8
+    is_out = matrix == 3
+    out_pair = block_column // 2
+    tile_row = jnp.where(is_out, block_row % 4 + 4 * (out_pair // 2), block_row)
+    tile_column = jnp.where(is_out, 6 + out_pair % 2, matrix * 2 + (block_column % 4) // 2)
+    held = jnp.where(is_out, block_row // 4, block_column // 4) == core
+    collected = collect(
+        grad_projection,
+        jnp.where(held, tile_row * 8 + tile_column, 0),
+        jnp.where(held, block_column % 2, 2 + block_column % 2),
+    ).reshape(2, 2, 4, 4, 2, BLK, 2 * BLK)
+    slot_sums = low_sum(collected[0], swap(collected[1], "c")).astype(bf16)
+    slot_colors = [
+        reduce_quads([slot_sums[color, quadrant] for quadrant in quads], first, line, 0)
+        for color, first in enumerate(("y", "x"))
+    ]
+    slot_rows = jnp.concatenate(slot_colors, 0)
+    grad_slots = jnp.stack([slot_rows[:, :, :BLK], slot_rows[:, :, BLK:]], 1).reshape(8, BLK, BLK)
+
+    partial_one = dot_back(grad_joined, projection)
+    partial_time = jnp.dot(
+        grad_time_pair, projection[:, half:].astype(f32).T, precision=BEST_PRECISION
+    )
+    grad_input_one = on_both(partial_one)
+    grad_input_time = partial_time + swap(partial_time, "c")
+    grad_residual, gain_one = layer_back(grad_input_one, normed_one, inverse_one, gain_values[:, 0])
+    grad_residual = (grad_residual + grad_after_self).astype(bf16)
+    grad_embeds, gain_time = layer_back(
+        grad_input_time, normed_time, inverse_time, gain_values[:, 0]
+    )
+    grad_in_weight = tdot(grad_residual, noised)
+    grad_table = features.astype(f32).reshape(NTIME, 1) * grad_embeds
+    grad_gains = jnp.stack([gain_one + gain_time, gain_two, gain_three], 1)
+    grad_ends = jnp.stack([grad_in_weight, grad_out_weight], 1)
+
+    def own_rows(values, width):
+        return pick(values.reshape(2, 2, 2, 4, -1, width), core, 2)
+
+    small = jnp.concatenate(
+        [
+            own_rows(grad_ends.reshape(-1, D), D),
+            own_rows(grad_table, D),
+            jnp.pad(
+                own_rows(grad_gains.reshape(32, 144), 144),
+                ((0, 0), (0, 0), (0, 0), (0, 3), (0, D - 144)),
+            ),
+        ],
+        3,
+    )
+    small = reduce_small(small, row, column, line)
+    grad_ends = small[:4].reshape(48, 2, DIN)
+    grad_table = small[4:12]
+    grad_gains = small[12, :144].reshape(48, 3)
+
+    reduced = (
+        grad_ends,
+        grad_table,
+        grad_slots,
+        grad_cross,
+        grad_key_value,
+        grad_gate_up,
+        grad_down,
+        grad_gains,
+    )
+    square_sum = jnp.zeros((), f32)
+    for member in reduced:
+        square_sum = square_sum + jnp.sum(member * member)
+    loss_part = jnp.where(
+        core == 0,
+        jnp.sum(errors * errors) * mse_scale + contrast_own * (CONTRAST_WEIGHT / items_total),
+        0.0,
+    )
+    loss_total, norm_square = all_sum(loss_part, square_sum)
+    return finish(
+        loss_total,
+        jnp.sqrt(norm_square),
+        reduced,
+        (
+            end_weights,
+            time_table,
+            square_slots,
+            cross_weights,
+            key_value,
+            gate_up,
+            down_weight,
+            norm_gains,
+        ),
+        (
+            first_ends,
+            first_table,
+            None,
+            first_cross,
+            first_key_value,
+            first_gate_up,
+            first_down,
+            first_gains,
+        ),
+        (
+            second_ends,
+            second_table,
+            None,
+            second_cross,
+            second_key_value,
+            second_gate_up,
+            second_down,
+            second_gains,
+        ),
+        (left_stats, right_stats, left_roots, right_roots),
+    )
+
+
+def all_sum(*values):
+    total = jnp.stack(values)
+    for axis in ("c", "z", "x", "y"):
+        bit = 1
+        while bit < lax.axis_size(axis):
+            total = total + swap(total, axis, bit)
+            bit *= 2
+    return total[0], total[1]
+
+
+def finish(loss_total, gradient_norm, reduced, masters, firsts, seconds, statistics):
+    factor = CLIP_NORM / jnp.maximum(gradient_norm, CLIP_NORM)
     results = [loss_total, gradient_norm]
     for index_value in (0, 1, 3, 4, 5, 6, 7):
         results.extend(
@@ -673,76 +1443,28 @@
             )
         )
     clipped_slots = factor * reduced[2]
-    left_new, right_new, slots_new = shampoo_update(
-        square_slots, clipped_slots, left_stats, right_stats, left_roots, right_roots
-    )
+    left_new, right_new, slots_new = shampoo_update(masters[2], clipped_slots, *statistics)
     results.extend([clipped_slots, left_new, right_new, slots_new])
     return tuple(results)
 
 
 def solution(mesh):
+    lines = mesh.shape["text"]
+    chips = mesh.devices.size // 2
+    if mesh.shape["dp"] == 8 and lines == 4 and 2 * mesh.shape["dp"] == chips:
+        mesh = Mesh(mesh.devices.reshape(2, 2, 2, lines), ("y", "x", "c", "z"))
+        dp, text, body = ("y", "x", "c"), ("z",), item_per_chip
+    else:
+        dp, text, body = ("dp",), ("text",), shards
+    own = dp + text
     in_specs = (
-        P("dp", "text", None),
-        P("dp", "text", None),
-        P("dp"),
-        P("dp", "text", None),
-        P("dp"),
-        P("dp", None),
+        P(dp, text, None),
+        P(dp, text, None),
+        P(dp),
+        P(dp, text, None),
+        P(dp),
+        P(dp, None),
         P(),
-        P(("dp", "text"), None, None),
-        P(("dp", "text"), None),
-        P(("dp", "text"), None, None),
-        P(("dp", "text"), None, None),
-        P(("dp", "text"), None),
-        P(("dp", "text"), None),
-        P(("dp", "text"), None),
-        P(("dp", "text"), None),
-        P(("dp", "text"), None, None),
-        P(("dp", "text"), None, None),
-        P(("dp", "text"), None),
-        P(("dp", "text"), None),
-        P(("dp", "text"), None, None),
-        P(("dp", "text"), None, None),
-        P(("dp", "text"), None),
-        P(("dp", "text"), None),
-        P(("dp", "text"), None),
-        P(("dp", "text"), None),
-        P(("dp", "text"), None),
-        P(("dp", "text"), None),
-        P(("dp", "text"), None),
-        P(("dp", "text"), None),
-        P(("dp", "text"), None, None),
-        P(("dp", "text"), None, None),
-        P(("dp", "text"), None, None),
-        P(("dp", "text"), None, None),
-    )
-    out_specs = (
-        P(),
-        P(),
-        P(("dp", "text"), None, None),
-        P(("dp", "text"), None, None),
-        P(("dp", "text"), None, None),
-        P(("dp", "text"), None),
-        P(("dp", "text"), None),
-        P(("dp", "text"), None),
-        P(("dp", "text"), None, None),
-        P(("dp", "text"), None, None),
-        P(("dp", "text"), None, None),
-        P(("dp", "text"), None),
-        P(("dp", "text"), None),
-        P(("dp", "text"), None),
-        P(("dp", "text"), None),
-        P(("dp", "text"), None),
-        P(("dp", "text"), None),
-        P(("dp", "text"), None),
-        P(("dp", "text"), None),
-        P(("dp", "text"), None),
-        P(("dp", "text"), None),
-        P(("dp", "text"), None),
-        P(("dp", "text"), None),
-        P(("dp", "text"), None, None),
-        P(("dp", "text"), None, None),
-        P(("dp", "text"), None, None),
-        P(("dp", "text"), None, None),
-    )
-    return jax.shard_map(shards, mesh=mesh, in_specs=in_specs, out_specs=out_specs, check_vma=False)
+    ) + (P(own),) * 26
+    out_specs = (P(), P()) + (P(own),) * 25
+    return jax.shard_map(body, mesh=mesh, in_specs=in_specs, out_specs=out_specs, check_vma=False)

time: 2940 us -> 2180 us (0.74)
  blocking collectives: 362 us -> 0 us
  local copies, waits for them, and re-layouts: 557 us -> 201 us
  waiting for transfers between devices: 1200 us -> 869 us
  Pallas kernels: 0 us -> 198 us
  starting transfers between devices: 3.52 us -> 131 us
  matrix products: 506 us -> 421 us
  other arithmetic: 268 us -> 333 us
    ppermute x0 -> x152, waiting for transfers between devices: none -> 869 us  [swap(): lax.ppermute(values, axis, [(i, i ^ bit) for i in range(lax.axis_size(axi...]
    reduce_scatter x15 -> x0, waiting for transfers between devices: 641 us -> none  [the longest x1 161 us: shards(): lax.psum_scatter(grad_slots.astype(jnp.bfloat16), 'dp', scatter_dimension...]
    all_gather x13 -> x0, waiting for transfers between devices: 501 us -> none  [the longest x1 114 us: shards(): lax.all_gather(grad_down_in.reshape(item_count, frames_dev, D), 'text', a...]
    all_gather x10 -> x0, blocking collectives: 299 us -> none  [the longest x1 73 us: shards(): lax.all_gather(text_part, ('dp', 'text'), axis=0, tiled=True)]
    pallas_call x0 -> x9, Pallas kernels: none -> 198 us  [the longest x1 80.7 us: collect(): pl.pallas_call(collect_kernel, grid_spec=pltpu.PrefetchScalarGridSpec(num...]
    ppermute x0 -> x152, starting transfers between devices: none -> 131 us  [swap(): lax.ppermute(values, axis, [(i, i ^ bit) for i in range(lax.axis_size(axi...]
    dynamic_update_slice x4 -> x0, local copies, waits for them, and re-layouts: 67.7 us -> none  [attend_backward(): lax.map(single, (queries, all_keys, values, key_bias, logsums, grad_mixtu...]
    reshape x16 -> x14, local copies, waits for them, and re-layouts: 69.3 us -> 11.5 us  [the longest x4 8.33 us: item_per_chip(): parts = [tdot(columns_of(input_three, quadrant, 384), gradient).astype(bf...]
  transfers between devices with their start and end apart: 32 -> 152, of which waited for: 19 -> 76; matrix products, arithmetic and copies ran while one was open for 38% -> 32% of each run, Pallas kernels for 0% -> 9%
where the time goes in v1:
time: 2180 us; the launch traced here: 2170 us
  waiting for transfers between devices  869 us (40%)
  matrix products  421 us (19%)
  other arithmetic  333 us (15%)
  local copies, waits for them, and re-layouts  201 us (9%)
  Pallas kernels  198 us (9%)
  starting transfers between devices  131 us (6%)
    ppermute x152, waiting for transfers between devices, swap(): lax.ppermute(values, axis, [(i, i ^ bit) for i in range(lax.axis_size(axi...  869 us
    ppermute x152, starting transfers between devices, swap(): lax.ppermute(values, axis, [(i, i ^ bit) for i in range(lax.axis_size(axi...  131 us
    dot_general x33, matrix products, tdot(): lax.dot_general(left, right, (((0,), (0,)), ((), ())), preferred_element_...  105 us
    dot_general x10, matrix products, dot_back(): lax.dot_general(left, right, (((1,), (1,)), ((), ())), preferred_element_...  84.1 us
    pallas_call x1, Pallas kernels, collect(): pl.pallas_call(collect_kernel, grid_spec=pltpu.PrefetchScalarGridSpec(num...  80.7 us
    pallas_call x6, Pallas kernels, place(): pl.pallas_call(place_kernel, grid_spec=pltpu.PrefetchScalarGridSpec(num_s...  73.2 us
    unnamed x581, local copies, waits for them, and re-layouts  65.6 us
    pallas_call x2, Pallas kernels, assemble(): pl.pallas_call(assemble_kernel, grid_spec=pltpu.PrefetchScalarGridSpec(nu...  44.1 us
  transfers between devices with their start and end apart: 152, of which 76 were waited for; matrix products, arithmetic and copies ran while one was open for 32% of the time, Pallas kernels for 9%

profile of v1, /device:TPU:0, one launch (start us, length us, event | category | flops | bytes accessed | tf_op | source)
XLA Modules:
  0.0 2169.6 jit_solution(10139195639944124345)
XLA Ops:
  29.6 19.2 collective-permute-done.13
  91.1 19.5 collective-permute-done.16
  127.3 21.8 %collective-permute-done.18 = bf16[2,2,192,384]{3,2,1,0:T(8,128)(2,1)S(1)} collective-permute-done((bf16[2,2,192,384]{3,2,1,0:T(8,128)(2,1)}, bf16[2,2,192,384]{3,2,1,0:T(8,128)(2,1)S(1)}, u32[]{:S(2)}, u32[]{:S(2)}) %collective-permute-start.18) | collective-permute-done | bytes 589856 | tf_op jit(solution)/shard_map/ppermute | solution.py:677
  157.9 19.7 collective-permute-done.20
  189.3 17.9 collective-permute-done.21
  366.3 32.1 %shard_map.520 = bf16[1536,2304]{1,0:T(8,128)(2,1)} custom-call(s32[48]{0:T(128)} %slice.348.left_at, s32[48]{0:T(128)} %slice.349.right_at, s32[48]{0:T(128)} %slice.350.left_half, s32[48]{0:T(128)} %slice.351.right_half, bf16[128,192,384]{2,1,0:T(8,128)(2,1)} %pad_maximum_fusion.left.right, bf16[128,192,384]{2,1,0:T(8,128)(2,1)} %pad_maximum_fusion.left.right), custom_call_target="tpu_custom_call" | custom-call | bytes 21233664 | tf_op jit(solution)/shard_map/pallas_call | solution.py:773
  432.5 24.1 %multiply_reduce_fusion.1 = (f32[12,1024]{1,0:T(8,128)S(1)}, f32[12,1024,1025]{1,2,0:T(8,128)}) fusion(bf16[1024,12,64]{0,2,1:T(8,128)(2,1)S(1)} %get-tuple-element.426, bf16[1024,12,64]{0,2,1:T(8,128)(2,1)} %get-tuple-element.425, bf16[1,12,64]{0,2,1:T(8,128)(2,1)S(1)} %reshape.2187), kind=kOutput, calls=%fused_computation.18 | convolution fusion | flops 1640512512 | bytes 53577216 | tf_op jit(solution)/shard_map/while/body/eval_jaxpr/fhd,khd->hfk/dot_general | solution.py:121
  456.5 20.0 fusion
  485.8 20.4 fusion.48
  586.5 25.5 %collective-permute-done.72 = bf16[2,1,192,768]{3,2,1,0:T(8,128)(2,1)} collective-permute-done((bf16[2,1,192,768]{3,2,1,0:T(8,128)(2,1)}, bf16[2,1,192,768]{3,2,1,0:T(8,128)(2,1)}, u32[]{:S(2)}, u32[]{:S(2)}) %collective-permute-start.72) | collective-permute-done | bytes 589856 | tf_op jit(solution)/shard_map/ppermute | solution.py:677
  638.4 24.1 %collective-permute-done.61 = bf16[2,2,48,3072]{3,2,1,0:T(8,128)(2,1)} collective-permute-done((bf16[2,2,48,3072]{3,2,1,0:T(8,128)(2,1)}, bf16[2,2,48,3072]{3,2,1,0:T(8,128)(2,1)}, u32[]{:S(2)}, u32[]{:S(2)}) %collective-permute-start.61) | collective-permute-done | bytes 1179680 | tf_op jit(solution)/shard_map/ppermute | solution.py:677
  667.2 20.5 collective-permute-done.55
  722.1 53.8 %collective-permute-done.68.refs_2_ = bf16[4,1,192,768]{3,2,1,0:T(8,128)(2,1)S(1)} collective-permute-done((bf16[4,1,192,768]{3,2,1,0:T(8,128)(2,1)S(1)}, bf16[4,1,192,768]{3,2,1,0:T(8,128)(2,1)S(1)}, u32[]{:S(2)}, u32[]{:S(2)}) %collective-permute-start.68) | collective-permute-done | bytes 1179680 | tf_op jit(solution)/shard_map/ppermute | solution.py:677
  832.4 19.5 collective-permute-done.57.refs_2_
  851.9 49.0 %collective-permute-done.58.refs_3_ = bf16[4,2,48,3072]{3,2,1,0:T(8,128)(2,1)} collective-permute-done((bf16[4,2,48,3072]{3,2,1,0:T(8,128)(2,1)}, bf16[4,2,48,3072]{3,2,1,0:T(8,128)(2,1)}, u32[]{:S(2)}, u32[]{:S(2)}) %collective-permute-start.58) | collective-permute-done | bytes 2359328 | tf_op jit(solution)/shard_map/ppermute | solution.py:677
  951.6 20.3 multiply_convert_fusion.3
  1044.9 22.1 %multiply_convert_fusion.2 = (bf16[1024,3072]{1,0:T(8,128)(2,1)}, bf16[1024,3072]{1,0:T(8,128)(2,1)}) fusion(f32[1024,3072]{1,0:T(8,128)} %fusion.318, f32[1024,3072]{1,0:T(8,128)} %get-tuple-element.489, f32[1024,3072]{1,0:T(8,128)} %fusion.85, bf16[3072,768]{1,0:T(8,128)(2,1)S(1)} %bitcast.696, bf16[1024,1536]{1,0:T(8,128)(2,1)} %copy-done.42), kind=kOutput, calls=%fused_computation.26 | convolution fusion | flops 4875878400 | bytes 56623104 | tf_op jit(solution)/shard_map/dot_general | solution.py:878
  1169.1 16.5 collective-permute-done.144
  1211.2 25.0 %collective-permute-done.139 = bf16[4,192,768]{2,1,0:T(8,128)(2,1)} collective-permute-done((bf16[4,192,768]{2,1,0:T(8,128)(2,1)}, bf16[4,192,768]{2,1,0:T(8,128)(2,1)}, u32[]{:S(2)}, u32[]{:S(2)}) %collective-permute-start.139) | collective-permute-done | bytes 1179680 | tf_op jit(solution)/shard_map/ppermute | solution.py:677
  1320.4 17.4 collective-permute-done.121
  1366.3 35.5 %collective-permute-done.101 = bf16[2,4,48,768]{3,2,0,1:T(8,128)(2,1)S(1)} collective-permute-done((bf16[2,4,48,768]{3,2,0,1:T(8,128)(2,1)S(1)}, bf16[2,4,48,768]{3,2,0,1:T(8,128)(2,1)S(1)}, u32[]{:S(2)}, u32[]{:S(2)}) %collective-permute-start.101) | collective-permute-done | bytes 589856 | tf_op jit(solution)/shard_map/ppermute | solution.py:677
  1429.5 27.6 %collective-permute-done.125 = bf16[2,4,48,3072]{3,2,0,1:T(8,128)(2,1)S(1)} collective-permute-done((bf16[2,4,48,3072]{3,2,0,1:T(8,128)(2,1)S(1)}, bf16[2,4,48,3072]{3,2,0,1:T(8,128)(2,1)S(1)}, u32[]{:S(2)}, u32[]{:S(2)}) %collective-permute-start.125) | collective-permute-done | bytes 2359328 | tf_op jit(solution)/shard_map/ppermute | solution.py:677
  1486.0 88.9 %collective-permute-done.111 = bf16[2,48,1536]{2,1,0:T(8,128)(2,1)S(1)} collective-permute-done((bf16[2,48,1536]{2,1,0:T(8,128)(2,1)S(1)}, bf16[2,48,1536]{2,1,0:T(8,128)(2,1)S(1)}, u32[]{:S(2)}, u32[]{:S(2)}) %collective-permute-start.111) | collective-permute-done | bytes 294944 | tf_op jit(solution)/shard_map/ppermute | solution.py:677
  1597.0 18.0 fusion.23
  1616.9 32.8 %multiply_reduce_fusion = (f32[12,1024]{1,0:T(8,128)S(1)}, f32[12,1024,1025]{1,2,0:T(8,128)}) fusion(f32[12,1024,1025]{1,2,0:T(8,128)} %get-tuple-element.485, f32[12,1024]{1,0:T(8,128)S(1)} %copy-done.53, bf16[1024,12,64]{0,2,1:T(8,128)(2,1)} %bitcast.678, bf16[1025,12,64]{0,2,1:T(8,128)(2,1)S(1)} %bitcast.672), kind=kOutput, calls=%fused_computation.13 | convolution fusion | flops 1662554112 | bytes 104007168 | tf_op jit(solution)/shard_map/while/body/eval_jaxpr/fhd,khd->hfk/dot_general | solution.py:149
  1649.7 41.2 %multiply_convert_fusion = bf16[12,1024,1025]{1,2,0:T(8,128)(2,1)} fusion(f32[12,1024,1025]{1,2,0:T(8,128)} %get-tuple-element.497, f32[12,1024,1025]{1,2,0:T(8,128)} %get-tuple-element.485, f32[12,1024]{1,0:T(8,128)S(1)} %get-tuple-element.496, f32[12,1024]{1,0:T(8,128)S(1)} %copy-done.53), kind=kLoop, calls=%fused_computation.12 | loop fusion | flops 62976000 | bytes 126050304 | tf_op jit(solution)/shard_map/while/body/eval_jaxpr/convert_element_type | solution.py:161
  1771.8 32.9 %maximum_maximum_fusion.left.right = bf16[1536,3072]{1,0:T(8,128)(2,1)} fusion(bf16[768,768]{1,0:T(8,128)(2,1)S(1)} %copy-done.34, bf16[768,768]{1,0:T(8,128)(2,1)S(1)} %get-tuple-element.385, bf16[1536,1536]{1,0:T(8,128)(2,1)S(1)} %fusion.7, bf16[1536,768]{1,0:T(8,128)(2,1)S(1)} %slice.674), kind=kLoop, calls=%fused_computation.32 | loop fusion | flops 37748736 | bytes 18874368 | tf_op jit(solution)/shard_map/concatenate | solution.py:1296
  1804.7 80.7 %shard_map.528 = bf16[128,192,384]{2,1,0:T(8,128)(2,1)} custom-call(s32[128]{0:T(128)} %slice.402.left_at, s32[128]{0:T(128)} %slice.403.right_at, s32[128]{0:T(128)} %slice.404.left_half, s32[128]{0:T(128)} %slice.405.right_half, bf16[1536,3072]{1,0:T(8,128)(2,1)} %maximum_maximum_fusion.left.right, bf16[1536,3072]{1,0:T(8,128)(2,1)} %maximum_maximum_fusion.left.right), custom_call_target="tpu_custom_call" | custom-call | bytes 28311552 | tf_op jit(solution)/shard_map/pallas_call | solution.py:804
  1965.8 20.1 collective-permute-done.97
  1996.1 19.3 collective-permute-done.96
  2015.4 21.1 collective-permute-done.98
  2041.1 35.3 %collective-permute-done.99 = bf16[2,2,192,384]{3,2,1,0:T(8,128)(2,1)S(1)} collective-permute-done((bf16[2,2,192,384]{3,2,1,0:T(8,128)(2,1)S(1)}, bf16[2,2,192,384]{3,2,1,0:T(8,128)(2,1)S(1)}, u32[]{:S(2)}, u32[]{:S(2)}) %collective-permute-start.99) | collective-permute-done | bytes 589856 | tf_op jit(solution)/shard_map/ppermute | solution.py:677
  (1348 shorter events, 1210.2 us)
Async XLA Ops:
  3.6 209.6 %collective-permute-start = (s32[2,17]{1,0:T(2,128)}, s32[2,17]{1,0:T(2,128)}, u32[]{:S(2)}, u32[]{:S(2)}) collective-permute-start(s32[2,17]{1,0:T(2,128)} %pad_add_fusion.3), channel_id=1, source_target_pairs={{0,4},{4,0},{1,5},{5,1},{2,6},{6,2},{3,7},{7,3},{8,12},{12,8},{9,1... | collective-permute-start | bytes 416 | tf_op jit(solution)/shard_map/ppermute | solution.py:677
  4.1 231.8 %collective-permute-start.24 = (bf16[2,32,768]{2,1,0:T(8,128)(2,1)}, bf16[2,32,768]{2,1,0:T(8,128)(2,1)}, u32[]{:S(2)}, u32[]{:S(2)}) collective-permute-start(bf16[2,32,768]{2,1,0:T(8,128)(2,1)} %param.36), channel_id=1, source_target_pairs={{0,4},{4,0},{1,5},{5,1},{2,6},{6,2},{3,7},{7,3},{8,12},{12,8},{9,1... | collective-permute-start | bytes 294920 | tf_op jit(solution)/shard_map/ppermute | solution.py:677
  5.8 223.6 %collective-permute-start.34 = (bf16[24,768]{1,0:T(8,128)(2,1)}, bf16[24,768]{1,0:T(8,128)(2,1)}, u32[]{:S(2)}, u32[]{:S(2)}) collective-permute-start(bf16[24,768]{1,0:T(8,128)(2,1)} %get-tuple-element.456), channel_id=1, source_target_pairs={{0,4},{4,0},{1,5},{5,1},{2,6},{6,2},{3,7},{7,3},{8,12},{12,8},{9,1... | collective-permute-start | bytes 110600 | tf_op jit(solution)/shard_map/ppermute | solution.py:677
  208.4 144.4 %collective-permute-start.22 = (bf16[64,192,384]{2,1,0:T(8,128)(2,1)}, bf16[64,192,384]{2,1,0:T(8,128)(2,1)}, u32[]{:S(2)}, u32[]{:S(2)}) collective-permute-start(bf16[64,192,384]{2,1,0:T(8,128)(2,1)} %bitcast.658), channel_id=1, source_target_pairs={{0,4},{4,0},{1,5},{5,1},{2,6},{6,2},{3,7},{7,3},{8,12},{12,8},{9,1... | collective-permute-start | bytes 28311560 | tf_op jit(solution)/shard_map/ppermute | solution.py:677
  305.8 175.0 %collective-permute-start.27 = (bf16[32,768]{1,0:T(8,128)(2,1)}, bf16[32,768]{1,0:T(8,128)(2,1)}, u32[]{:S(2)}, u32[]{:S(2)}) collective-permute-start(bf16[32,768]{1,0:T(8,128)(2,1)} %get-tuple-element.444), channel_id=1, source_target_pairs={{0,3},{1,2},{2,1},{3,0},{4,7},{5,6},{6,5},{7,4},{8,11},{9,10},{10,... | collective-permute-start | bytes 147464 | tf_op jit(solution)/shard_map/ppermute | solution.py:677
  310.6 171.8 %collective-permute-start.26 = (bf16[32,768]{1,0:T(8,128)(2,1)}, bf16[32,768]{1,0:T(8,128)(2,1)}, u32[]{:S(2)}, u32[]{:S(2)}) collective-permute-start(bf16[32,768]{1,0:T(8,128)(2,1)} %get-tuple-element.445), channel_id=1, source_target_pairs={{0,2},{1,3},{2,0},{3,1},{4,6},{5,7},{6,4},{7,5},{8,10},{9,11},{10,... | collective-permute-start | bytes 147464 | tf_op jit(solution)/shard_map/ppermute | solution.py:677
  328.2 155.5 %collective-permute-start.25 = (bf16[32,768]{1,0:T(8,128)(2,1)}, bf16[32,768]{1,0:T(8,128)(2,1)}, u32[]{:S(2)}, u32[]{:S(2)}) collective-permute-start(bf16[32,768]{1,0:T(8,128)(2,1)} %get-tuple-element.446), channel_id=1, source_target_pairs={{0,1},{1,0},{2,3},{3,2},{4,5},{5,4},{6,7},{7,6},{8,9},{9,8},{10,11... | collective-permute-start | bytes 147464 | tf_op jit(solution)/shard_map/ppermute | solution.py:677
  329.1 189.2 %collective-permute-start.42 = (bf16[2,2,48,768]{3,2,1,0:T(8,128)(2,1)}, bf16[2,2,48,768]{3,2,1,0:T(8,128)(2,1)}, u32[]{:S(2)}, u32[]{:S(2)}) collective-permute-start(bf16[2,2,48,768]{3,2,1,0:T(8,128)(2,1)} %pad_maximum_fusion.41), channel_id=1, source_target_pairs={{0,2},{1,3},{2,0},{3,1},{4,6},{5,7},{6,4},{7,5},{8,10},{9,11},{10,... | collective-permute-start | bytes 884744 | tf_op jit(solution)/shard_map/ppermute | solution.py:677
  352.8 131.4 %collective-permute-start.31 = (bf16[4,2,24,768]{3,2,1,0:T(8,128)(2,1)}, bf16[4,2,24,768]{3,2,1,0:T(8,128)(2,1)}, u32[]{:S(2)}, u32[]{:S(2)}) collective-permute-start(bf16[4,2,24,768]{3,2,1,0:T(8,128)(2,1)} %get-tuple-element.440), channel_id=1, source_target_pairs={{0,8},{8,0},{1,9},{9,1},{2,10},{10,2},{3,11},{11,3},{4,12},{12,4},... | collective-permute-start | bytes 884744 | tf_op jit(solution)/shard_map/ppermute | solution.py:677
  528.9 167.3 %collective-permute-start.23 = (bf16[1024,1536]{1,0:T(8,128)(2,1)}, bf16[1024,1536]{1,0:T(8,128)(2,1)}, u32[]{:S(2)}, u32[]{:S(2)}) collective-permute-start(bf16[1024,1536]{1,0:T(8,128)(2,1)} %convolution_convert_fusion.11), channel_id=1, source_target_pairs={{0,4},{4,0},{1,5},{5,1},{2,6},{6,2},{3,7},{7,3},{8,12},{12,8},{9,1... | collective-permute-start | bytes 9437192 | tf_op jit(solution)/shard_map/ppermute | solution.py:677
  573.9 88.6 %collective-permute-start.61 = (bf16[2,2,48,3072]{3,2,1,0:T(8,128)(2,1)}, bf16[2,2,48,3072]{3,2,1,0:T(8,128)(2,1)}, u32[]{:S(2)}, u32[]{:S(2)}) collective-permute-start(bf16[2,2,48,3072]{3,2,1,0:T(8,128)(2,1)} %pad_maximum_fusion.15), channel_id=1, source_target_pairs={{0,2},{1,3},{2,0},{3,1},{4,6},{5,7},{6,4},{7,5},{8,10},{9,11},{10,... | collective-permute-start | bytes 3538952 | tf_op jit(solution)/shard_map/ppermute | solution.py:677
  627.4 83.0 %collective-permute-start.74 = (bf16[4,1,192,768]{3,2,1,0:T(8,128)(2,1)}, bf16[4,1,192,768]{3,2,1,0:T(8,128)(2,1)}, u32[]{:S(2)}, u32[]{:S(2)}) collective-permute-start(bf16[4,1,192,768]{3,2,1,0:T(8,128)(2,1)} %pad_maximum_fusion.17.refs_0_), channel_id=1, source_target_pairs={{0,16},{16,0},{1,17},{17,1},{2,18},{18,2},{3,19},{19,3},{4,20},{20... | collective-permute-start | bytes 3538952 | tf_op jit(solution)/shard_map/ppermute | solution.py:677
  691.8 100.0 %collective-permute-start.56 = (bf16[4,2,48,3072]{3,2,1,0:T(8,128)(2,1)}, bf16[4,2,48,3072]{3,2,1,0:T(8,128)(2,1)}, u32[]{:S(2)}, u32[]{:S(2)}) collective-permute-start(bf16[4,2,48,3072]{3,2,1,0:T(8,128)(2,1)} %pad_maximum_fusion.3.refs_0_), channel_id=1, source_target_pairs={{0,8},{8,0},{1,9},{9,1},{2,10},{10,2},{3,11},{11,3},{4,12},{12,4},... | collective-permute-start | bytes 7077896 | tf_op jit(solution)/shard_map/ppermute | solution.py:677
  696.3 106.0 %collective-permute-start.63 = (bf16[4,2,48,3072]{3,2,1,0:T(8,128)(2,1)}, bf16[4,2,48,3072]{3,2,1,0:T(8,128)(2,1)}, u32[]{:S(2)}, u32[]{:S(2)}) collective-permute-start(bf16[4,2,48,3072]{3,2,1,0:T(8,128)(2,1)} %pad_maximum_fusion.4.refs_0_), channel_id=1, source_target_pairs={{0,16},{16,0},{1,17},{17,1},{2,18},{18,2},{3,19},{19,3},{4,20},{20... | collective-permute-start | bytes 7077896 | tf_op jit(solution)/shard_map/ppermute | solution.py:677
  713.5 78.2 %collective-permute-start.75 = (bf16[4,1,192,768]{3,2,1,0:T(8,128)(2,1)}, bf16[4,1,192,768]{3,2,1,0:T(8,128)(2,1)}, u32[]{:S(2)}, u32[]{:S(2)}) collective-permute-start(bf16[4,1,192,768]{3,2,1,0:T(8,128)(2,1)} %collective-permute-done.74.refs_2_), channel_id=1, source_target_pairs={{0,8},{8,0},{1,9},{9,1},{2,10},{10,2},{3,11},{11,3},{4,12},{12,4},... | collective-permute-start | bytes 3538952 | tf_op jit(solution)/shard_map/ppermute | solution.py:677
  716.6 84.7 %collective-permute-start.69 = (bf16[4,1,192,768]{3,2,1,0:T(8,128)(2,1)}, bf16[4,1,192,768]{3,2,1,0:T(8,128)(2,1)}, u32[]{:S(2)}, u32[]{:S(2)}) collective-permute-start(bf16[4,1,192,768]{3,2,1,0:T(8,128)(2,1)} %collective-permute-done.67.refs_1_), channel_id=1, source_target_pairs={{0,16},{16,0},{1,17},{17,1},{2,18},{18,2},{3,19},{19,3},{4,20},{20... | collective-permute-start | bytes 3538952 | tf_op jit(solution)/shard_map/ppermute | solution.py:677
  777.0 152.9 %collective-permute-start.52 = (bf16[1024,1536]{1,0:T(8,128)(2,1)}, bf16[1024,1536]{1,0:T(8,128)(2,1)}, u32[]{:S(2)}, u32[]{:S(2)}) collective-permute-start(bf16[1024,1536]{1,0:T(8,128)(2,1)} %convolution_convert_fusion.10), channel_id=1, source_target_pairs={{0,4},{4,0},{1,5},{5,1},{2,6},{6,2},{3,7},{7,3},{8,12},{12,8},{9,1... | collective-permute-start | bytes 9437192 | tf_op jit(solution)/shard_map/ppermute | solution.py:677
  791.7 109.1 %collective-permute-start.58 = (bf16[4,2,48,3072]{3,2,1,0:T(8,128)(2,1)}, bf16[4,2,48,3072]{3,2,1,0:T(8,128)(2,1)}, u32[]{:S(2)}, u32[]{:S(2)}) collective-permute-start(bf16[4,2,48,3072]{3,2,1,0:T(8,128)(2,1)} %collective-permute-done.56.refs_1_), channel_id=1, source_target_pairs={{0,16},{16,0},{1,17},{17,1},{2,18},{18,2},{3,19},{19,3},{4,20},{20... | collective-permute-start | bytes 7077896 | tf_op jit(solution)/shard_map/ppermute | solution.py:677
  801.3 114.0 %collective-permute-start.62 = (bf16[4,2,48,3072]{3,2,1,0:T(8,128)(2,1)}, bf16[4,2,48,3072]{3,2,1,0:T(8,128)(2,1)}, u32[]{:S(2)}, u32[]{:S(2)}) collective-permute-start(bf16[4,2,48,3072]{3,2,1,0:T(8,128)(2,1)} %pad_maximum_fusion.4.refs_0_), channel_id=1, source_target_pairs={{0,8},{8,0},{1,9},{9,1},{2,10},{10,2},{3,11},{11,3},{4,12},{12,4},... | collective-permute-start | bytes 7077896 | tf_op jit(solution)/shard_map/ppermute | solution.py:677
  802.3 113.1 %collective-permute-start.64 = (bf16[4,2,48,3072]{3,2,1,0:T(8,128)(2,1)}, bf16[4,2,48,3072]{3,2,1,0:T(8,128)(2,1)}, u32[]{:S(2)}, u32[]{:S(2)}) collective-permute-start(bf16[4,2,48,3072]{3,2,1,0:T(8,128)(2,1)} %collective-permute-done.63.refs_2_), channel_id=1, source_target_pairs={{0,8},{8,0},{1,9},{9,1},{2,10},{10,2},{3,11},{11,3},{4,12},{12,4},... | collective-permute-start | bytes 7077896 | tf_op jit(solution)/shard_map/ppermute | solution.py:677
  1149.7 88.5 %collective-permute-start.132 = (bf16[2,4,48,3072]{3,2,0,1:T(8,128)(2,1)}, bf16[2,4,48,3072]{3,2,0,1:T(8,128)(2,1)}, u32[]{:S(2)}, u32[]{:S(2)}) collective-permute-start(bf16[2,4,48,3072]{3,2,0,1:T(8,128)(2,1)} %copy.536), channel_id=1, source_target_pairs={{0,8},{8,0},{1,9},{9,1},{2,10},{10,2},{3,11},{11,3},{4,12},{12,4},... | collective-permute-start | bytes 7077896 | tf_op jit(solution)/shard_map/ppermute | solution.py:677
  1160.3 95.5 %collective-permute-start.126 = (bf16[2,4,48,3072]{3,2,0,1:T(8,128)(2,1)}, bf16[2,4,48,3072]{3,2,0,1:T(8,128)(2,1)}, u32[]{:S(2)}, u32[]{:S(2)}) collective-permute-start(bf16[2,4,48,3072]{3,2,0,1:T(8,128)(2,1)} %copy.529), channel_id=1, source_target_pairs={{0,16},{16,0},{1,17},{17,1},{2,18},{18,2},{3,19},{19,3},{4,20},{20... | collective-permute-start | bytes 7077896 | tf_op jit(solution)/shard_map/ppermute | solution.py:677
  1319.9 106.8 %collective-permute-start.131 = (bf16[2,4,48,3072]{3,2,0,1:T(8,128)(2,1)S(1)}, bf16[2,4,48,3072]{3,2,0,1:T(8,128)(2,1)S(1)}, u32[]{:S(2)}, u32[]{:S(2)}) collective-permute-start(bf16[2,4,48,3072]{3,2,0,1:T(8,128)(2,1)S(1)} %copy-done.80), channel_id=1, source_target_pairs={{0,8},{8,0},{1,9},{9,1},{2,10},{10,2},{3,11},{11,3},{4,12},{12,4},... | collective-permute-start | bytes 7077896 | tf_op jit(solution)/shard_map/ppermute | solution.py:677
  1337.8 89.8 %collective-permute-start.133 = (bf16[2,4,48,3072]{3,2,0,1:T(8,128)(2,1)S(1)}, bf16[2,4,48,3072]{3,2,0,1:T(8,128)(2,1)S(1)}, u32[]{:S(2)}, u32[]{:S(2)}) collective-permute-start(bf16[2,4,48,3072]{3,2,0,1:T(8,128)(2,1)S(1)} %copy-done.71), channel_id=1, source_target_pairs={{0,16},{16,0},{1,17},{17,1},{2,18},{18,2},{3,19},{19,3},{4,20},{20... | collective-permute-start | bytes 7077896 | tf_op jit(solution)/shard_map/ppermute | solution.py:677
  1426.6 156.8 %collective-permute-start.83 = (bf16[1024,1536]{1,0:T(8,128)(2,1)S(1)}, bf16[1024,1536]{1,0:T(8,128)(2,1)S(1)}, u32[]{:S(2)}, u32[]{:S(2)}) collective-permute-start(bf16[1024,1536]{1,0:T(8,128)(2,1)S(1)} %convolution_convert_fusion.9), channel_id=1, source_target_pairs={{0,4},{4,0},{1,5},{5,1},{2,6},{6,2},{3,7},{7,3},{8,12},{12,8},{9,1... | collective-permute-start | bytes 9437192 | tf_op jit(solution)/shard_map/ppermute | solution.py:677
  1458.2 116.8 %collective-permute-start.134 = (bf16[2,2,48,3072]{3,2,1,0:T(8,128)(2,1)S(1)}, bf16[2,2,48,3072]{3,2,1,0:T(8,128)(2,1)S(1)}, u32[]{:S(2)}, u32[]{:S(2)}) collective-permute-start(bf16[2,2,48,3072]{3,2,1,0:T(8,128)(2,1)S(1)} %pad_maximum_fusion.19), channel_id=1, source_target_pairs={{0,2},{1,3},{2,0},{3,1},{4,6},{5,7},{6,4},{7,5},{8,10},{9,11},{10,... | collective-permute-start | bytes 3538952 | tf_op jit(solution)/shard_map/ppermute | solution.py:677
  1472.6 105.7 %collective-permute-start.128 = (bf16[2,2,48,3072]{3,2,1,0:T(8,128)(2,1)S(1)}, bf16[2,2,48,3072]{3,2,1,0:T(8,128)(2,1)S(1)}, u32[]{:S(2)}, u32[]{:S(2)}) collective-permute-start(bf16[2,2,48,3072]{3,2,1,0:T(8,128)(2,1)S(1)} %pad_maximum_fusion.18), channel_id=1, source_target_pairs={{0,2},{1,3},{2,0},{3,1},{4,6},{5,7},{6,4},{7,5},{8,10},{9,11},{10,... | collective-permute-start | bytes 3538952 | tf_op jit(solution)/shard_map/ppermute | solution.py:677
  1485.8 89.0 %collective-permute-start.111 = (bf16[2,48,1536]{2,1,0:T(8,128)(2,1)S(1)}, bf16[2,48,1536]{2,1,0:T(8,128)(2,1)S(1)}, u32[]{:S(2)}, u32[]{:S(2)}) collective-permute-start(bf16[2,48,1536]{2,1,0:T(8,128)(2,1)S(1)} %pad_maximum_fusion.46), channel_id=1, source_target_pairs={{0,2},{1,3},{2,0},{3,1},{4,6},{5,7},{6,4},{7,5},{8,10},{9,11},{10,... | collective-permute-start | bytes 884744 | tf_op jit(solution)/shard_map/ppermute | solution.py:677
  1576.2 330.4 %collective-permute-start.135 = (bf16[2,48,3072]{2,1,0:T(8,128)(2,1)}, bf16[2,48,3072]{2,1,0:T(8,128)(2,1)}, u32[]{:S(2)}, u32[]{:S(2)}) collective-permute-start(bf16[2,48,3072]{2,1,0:T(8,128)(2,1)} %fusion.67), channel_id=1, source_target_pairs={{0,1},{1,0},{2,3},{3,2},{4,5},{5,4},{6,7},{7,6},{8,9},{9,8},{10,11... | collective-permute-start | bytes 1769480 | tf_op jit(solution)/shard_map/ppermute | solution.py:677
  1579.4 324.8 %collective-permute-start.129 = (bf16[2,48,3072]{2,1,0:T(8,128)(2,1)}, bf16[2,48,3072]{2,1,0:T(8,128)(2,1)}, u32[]{:S(2)}, u32[]{:S(2)}) collective-permute-start(bf16[2,48,3072]{2,1,0:T(8,128)(2,1)} %fusion.69), channel_id=1, source_target_pairs={{0,1},{1,0},{2,3},{3,2},{4,5},{5,4},{6,7},{7,6},{8,9},{9,8},{10,11... | collective-permute-start | bytes 1769480 | tf_op jit(solution)/shard_map/ppermute | solution.py:677
  1764.0 137.3 %collective-permute-start.85 = (f32[1,1536]{1,0:T(1,128)S(1)}, f32[1,1536]{1,0:T(1,128)S(1)}, u32[]{:S(2)}, u32[]{:S(2)}) collective-permute-start(f32[1,1536]{1,0:T(1,128)S(1)} %fusion.18), channel_id=1, source_target_pairs={{0,4},{4,0},{1,5},{5,1},{2,6},{6,2},{3,7},{7,3},{8,12},{12,8},{9,1... | collective-permute-start | bytes 18440 | tf_op jit(solution)/shard_map/ppermute | solution.py:677
  1764.1 161.7 %collective-permute-start.84 = (bf16[1024,1536]{1,0:T(8,128)(2,1)}, bf16[1024,1536]{1,0:T(8,128)(2,1)}, u32[]{:S(2)}, u32[]{:S(2)}) collective-permute-start(bf16[1024,1536]{1,0:T(8,128)(2,1)} %convolution_convert_fusion.8), channel_id=1, source_target_pairs={{0,4},{4,0},{1,5},{5,1},{2,6},{6,2},{3,7},{7,3},{8,12},{12,8},{9,1... | collective-permute-start | bytes 9437192 | tf_op jit(solution)/shard_map/ppermute | solution.py:677
  (392 other events, 10178.9 us)

commit v2 on v1

--- a/solution.py
+++ b/solution.py
@@ -699,130 +699,6 @@
     return jnp.concatenate(pieces, 0)
 
 
-def gather_pieces(block, first, second):
-    base = grow(block[None], "z")
-    near = swap(base, first)
-    across = swap(base, second)
-    far = swap(near, second)
-    return (base, near, across, far) if first == "x" else (base, across, near, far)
-
-
-def place_kernel(spot, *refs):
-    sources, target = refs[:4], refs[4]
-    quadrant = pl.program_id(0)
-    pair = target.shape[1] == 2
-    for index_value, source in enumerate(sources):
-
-        @pl.when(quadrant == index_value)
-        def store():
-            if pair:
-                target[0, spot[2], 0] = source[0, 0]
-                target[0, 1 - spot[2], 0] = source[0, 1]
-            else:
-                target[0, 0, 0] = source[0, 0]
-
-
-def place(pieces, spot):
-    lines, cores, height, width = pieces[0].shape
-
-    def source_map(index_value):
-        def at(quadrant, line, where):
-            return (jnp.clip((quadrant - index_value) * lines + line, 0, lines - 1), 0, 0, 0)
-
-        return at
-
-    placed = pl.pallas_call(
-        place_kernel,
-        grid_spec=pltpu.PrefetchScalarGridSpec(
-            num_scalar_prefetch=1,
-            grid=(4, lines),
-            in_specs=[
-                pl.BlockSpec((1, cores, height, width), source_map(index_value))
-                for index_value in range(4)
-            ],
-            out_specs=pl.BlockSpec(
-                (1, cores, 1, height, width),
-                lambda quadrant, line, where: (where[0] ^ quadrant, 0, where[1] ^ line, 0, 0),
-            ),
-        ),
-        out_shape=jax.ShapeDtypeStruct((4, cores, lines, height, width), pieces[0].dtype),
-        cost_estimate=pl.CostEstimate(
-            flops=0, bytes_accessed=16 * lines * cores * height * width, transcendentals=0
-        ),
-    )(spot, *pieces)
-    return placed.reshape(4 * cores * lines * height, width)
-
-
-def half_block(tile, is_right, to_right):
-    wide = tile.astype(jnp.float32)
-    turned = pltpu.roll(wide, BLK, 1)
-    return jnp.where(is_right == to_right, wide, turned)
-
-
-def assemble_kernel(left_at, right_at, left_half, right_half, left, right, target):
-    step = pl.program_id(0)
-    left_tile = half_block(left[0], left_half[step], 0)
-    right_tile = half_block(right[0], right_half[step], 1)
-    lane = lax.broadcasted_iota(jnp.int32, left_tile.shape, 1)
-    target[...] = jnp.where(lane < BLK, left_tile, right_tile).astype(target.dtype)
-
-
-def assemble(pairs, places, rights, rows, columns):
-    steps = places.shape[0] // 2
-    across = columns // (2 * BLK)
-    return pl.pallas_call(
-        assemble_kernel,
-        grid_spec=pltpu.PrefetchScalarGridSpec(
-            num_scalar_prefetch=4,
-            grid=(steps,),
-            in_specs=[
-                pl.BlockSpec((1, BLK, 2 * BLK), lambda step, a, b, c, d: (a[step], 0, 0)),
-                pl.BlockSpec((1, BLK, 2 * BLK), lambda step, a, b, c, d: (b[step], 0, 0)),
-            ],
-            out_specs=pl.BlockSpec(
-                (BLK, 2 * BLK), lambda step, a, b, c, d: (step // across, step % across)
-            ),
-        ),
-        out_shape=jax.ShapeDtypeStruct((rows, columns), pairs.dtype),
-        cost_estimate=pl.CostEstimate(flops=0, bytes_accessed=6 * rows * columns, transcendentals=0),
-    )(places[0::2], places[1::2], rights[0::2], rights[1::2], pairs, pairs)
-
-
-def collect_kernel(left_at, right_at, left_half, right_half, left, right, target):
-    step = pl.program_id(0)
-    left_tile = half_block(left[...], left_half[step] % 2, 0)
-    right_tile = half_block(right[...], right_half[step] % 2, 1)
-    left_tile = jnp.where(left_half[step] < 2, left_tile, 0.0)
-    right_tile = jnp.where(right_half[step] < 2, right_tile, 0.0)
-    lane = lax.broadcasted_iota(jnp.int32, left_tile.shape, 1)
-    target[0] = jnp.where(lane < BLK, left_tile, right_tile).astype(target.dtype)
-
-
-def collect(matrix, places, halves):
-    steps = places.shape[0] // 2
-    across = matrix.shape[1] // (2 * BLK)
-    return pl.pallas_call(
-        collect_kernel,
-        grid_spec=pltpu.PrefetchScalarGridSpec(
-            num_scalar_prefetch=4,
-            grid=(steps,),
-            in_specs=[
-                pl.BlockSpec(
-                    (BLK, 2 * BLK), lambda step, a, b, c, d: (a[step] // across, a[step] % across)
-                ),
-                pl.BlockSpec(
-                    (BLK, 2 * BLK), lambda step, a, b, c, d: (b[step] // across, b[step] % across)
-                ),
-            ],
-            out_specs=pl.BlockSpec((1, BLK, 2 * BLK), lambda step, a, b, c, d: (step, 0, 0)),
-        ),
-        out_shape=jax.ShapeDtypeStruct((steps, BLK, 2 * BLK), matrix.dtype),
-        cost_estimate=pl.CostEstimate(
-            flops=0, bytes_accessed=6 * matrix.size, transcendentals=0
-        ),
-    )(places[0::2], places[1::2], halves[0::2], halves[1::2], matrix, matrix)
-
-
 def low_sum(*terms):
     total = terms[0].astype(jnp.float32)
     for term in terms[1:]:
@@ -830,41 +706,6 @@
     return total
 
 
-def reduce_quads(quads, first, line, line_axis):
-    mine, near_x, near_y, far = quads
-    if first == "y":
-        from_far = swap(far, "y")
-        from_side = swap(near_y, "y")
-        onward = low_sum(near_x, from_far).astype(jnp.bfloat16)
-        from_onward = swap(onward, "x")
-    else:
-        from_far = swap(far, "x")
-        from_side = swap(near_x, "x")
-        onward = low_sum(near_y, from_far).astype(jnp.bfloat16)
-        from_onward = swap(onward, "y")
-    return reduce_line((mine, from_side, from_onward), line, line_axis)
-
-
-def reduce_line(terms, line, line_axis):
-    def part(index_value):
-        return low_sum(*[pick(term, index_value, line_axis) for term in terms])
-
-    far_send = jnp.stack(
-        [part((line ^ 2) & 2), part(((line ^ 2) & 2) + 1)], 0
-    ).astype(jnp.bfloat16)
-    received = swap(far_send, "z", 2)
-    near_send = part(line ^ 1) + pick(received, (line ^ 1) % 2).astype(jnp.float32)
-    last = swap(near_send.astype(jnp.bfloat16), "z", 1)
-    return part(line) + low_sum(pick(received, line % 2), last)
-
-
-def reduce_small(values, row, column, line):
-    for axis, me in (("y", row), ("x", column)):
-        received = swap(pick(values, 1 - me).astype(jnp.bfloat16), axis)
-        values = pick(values, me) + received.astype(jnp.float32)
-    return reduce_line((values,), line, 0)
-
-
 def on_both(partial_sum):
     low = partial_sum.astype(jnp.bfloat16)
     return low_sum(low, swap(low, "c"))
@@ -876,6 +717,712 @@
 
 def dot_back(left, right):
     return lax.dot_general(left, right, (((1,), (1,)), ((), ())), preferred_element_type=jnp.float32)
+
+
+MESH_ID = pl.DeviceIdType.MESH
+TILE = 256
+
+
+def anywhere(count):
+    return [pl.BlockSpec(memory_space=pl.ANY)] * count
+
+
+def coordinates():
+    return tuple(lax.axis_index(axis) for axis in ("y", "x", "c", "z"))
+
+
+def chip_peers(me):
+    row, column, core, line = me
+    beside = {
+        "c": (row, column, 1 - core, line),
+        "x": (row, 1 - column, core, line),
+        "y": (1 - row, column, core, line),
+    }
+    for offset in (1, 2, 3):
+        beside[offset] = (row, column, core, line ^ offset)
+    return beside
+
+
+def greet(peers):
+    barrier = pltpu.get_barrier_semaphore()
+    for peer in peers.values():
+        pl.semaphore_signal(barrier, inc=1, device_id=peer, device_id_type=MESH_ID)
+    pl.semaphore_wait(barrier, len(peers))
+
+
+def send(source, target, send_sem, recv_sem, peer):
+    return pltpu.make_async_remote_copy(
+        src_ref=source,
+        dst_ref=target,
+        send_sem=send_sem,
+        recv_sem=recv_sem,
+        device_id=peer,
+        device_id_type=MESH_ID,
+    )
+
+
+def gather_kernel(arrays, groups, *refs):
+    count = len(arrays)
+    inputs = sum(2 if kind == "cols" else 1 for kind, _, _ in arrays)
+    sources, bufs = list(refs[:inputs]), refs[inputs : inputs + count]
+    send_sem, recv_sem, core_send, core_recv, local_sem = refs[inputs + count :]
+    me = coordinates()
+    row, column, core, line = me
+    plane = 2 * row + column
+    peers = chip_peers(me)
+    greet(peers)
+    local, cross = [], []
+    for index_value, (kind, _, _) in enumerate(arrays):
+        spot = bufs[index_value].at[plane, 0 if kind == "one" else core, line]
+        copy = pltpu.make_async_copy(sources.pop(0), spot, local_sem.at[index_value])
+        copy.start()
+        local.append(copy)
+        cross.append(None)
+        if kind == "cols":
+            cross[-1] = send(
+                sources.pop(0),
+                spot,
+                core_send.at[index_value],
+                core_recv.at[index_value],
+                peers["c"],
+            )
+            cross[-1].start()
+    whole = slice(None)
+    flat = [unit for group in groups for unit in group]
+    ready = set()
+
+    def move(number, slot, planes, lines, peer):
+        array, _, rows, columns = flat[number]
+        cores = {"cols": whole, "one": 0}.get(arrays[array][0], core)
+        view = bufs[array].at[planes, cores, lines, rows, columns]
+        return send(view, view, send_sem.at[number, slot], recv_sem.at[number, slot], peer)
+
+    def line_copies(number):
+        return [move(number, o - 1, plane, line, peers[o]) for o in (1, 2, 3)]
+
+    def near_copy(number):
+        axis = "y" if flat[number][1] else "x"
+        return move(number, 3, plane, whole, peers[axis])
+
+    def side_copy(number):
+        axis = "x" if flat[number][1] else "y"
+        return move(number, 4, plane, whole, peers[axis])
+
+    def far_copy(number):
+        color = flat[number][1]
+        return move(number, 5, plane ^ (2 if color else 1), whole, peers["x" if color else "y"])
+
+    def core_copy(number):
+        array, _, rows, columns = flat[number]
+        kind = arrays[array][0]
+        if kind not in ("both", "half"):
+            return None
+        planes = whole if kind == "both" else pl.ds(2 * (1 - core), 2)
+        view = bufs[array].at[planes, core, whole, rows, columns]
+        return send(view, view, send_sem.at[number, 6], recv_sem.at[number, 6], peers["c"])
+
+    def start_line(number):
+        array = flat[number][0]
+        if array not in ready:
+            ready.add(array)
+            local[array].wait()
+            if cross[array] is not None:
+                cross[array].wait()
+        for copy in line_copies(number):
+            copy.start()
+
+    def start_near(number):
+        for copy in line_copies(number):
+            copy.wait_recv()
+        near_copy(number).start()
+        side_copy(number).start()
+
+    def start_far(number):
+        near_copy(number).wait_recv()
+        far_copy(number).start()
+
+    def close(number):
+        side_copy(number).wait_recv()
+        far_copy(number).wait_recv()
+        last = core_copy(number)
+        if last is not None:
+            last.start()
+        for copy in line_copies(number) + [near_copy(number), side_copy(number), far_copy(number)]:
+            copy.wait_send()
+
+    stages = (start_line, start_near, start_far, close)
+    numbers, at = [], 0
+    for group in groups:
+        numbers.append(range(at, at + len(group)))
+        at += len(group)
+    for step in range(len(groups) + 3):
+        for lag, stage in enumerate(stages):
+            if 0 <= step - lag < len(groups):
+                for number in numbers[step - lag]:
+                    stage(number)
+    for number in range(len(flat)):
+        last = core_copy(number)
+        if last is not None:
+            last.wait()
+
+
+def gather_weights(arrays, groups, sources, collective_id):
+    units = sum(len(group) for group in groups)
+    dma = pltpu.SemaphoreType.DMA
+    return pl.pallas_call(
+        partial(gather_kernel, arrays, groups),
+        out_shape=[
+            jax.ShapeDtypeStruct((4, 1 if kind == "one" else 2, 4) + shape, dtype)
+            for kind, shape, dtype in arrays
+        ],
+        in_specs=anywhere(len(sources)),
+        out_specs=anywhere(len(arrays)),
+        scratch_shapes=[
+            dma((units, 7)),
+            dma((units, 7)),
+            dma((len(arrays),)),
+            dma((len(arrays),)),
+            dma((len(arrays),)),
+        ],
+        compiler_params=pltpu.CompilerParams(collective_id=collective_id, has_side_effects=True),
+    )(*sources)
+
+
+def reduce_kernel(arrays, groups, *refs):
+    count = len(arrays)
+    flat = [unit for group in groups for unit in group]
+    total = len(flat)
+    sources = refs[:count]
+    outputs = sum(2 if kind == "cols" else 1 for kind, _ in arrays)
+    targets, at = [], count
+    for kind, _ in arrays:
+        width = 2 if kind == "cols" else 1
+        targets.append(refs[at : at + width])
+        at += width
+    scratch = refs[at:]
+    sides, onwards, mines, from_ons, from_lines, from_cores = (
+        scratch[index_value * total : (index_value + 1) * total] for index_value in range(6)
+    )
+    send_sem, recv_sem, load_sem = scratch[6 * total :]
+    me = coordinates()
+    row, column, core, line = me
+    plane = 2 * row + column
+    peers = chip_peers(me)
+    greet(peers)
+    whole = slice(None)
+
+    def source(number, planes):
+        array, _, rows, columns = flat[number]
+        return sources[array].at[planes, whole, whole, rows, columns]
+
+    def first_copy(number, slot):
+        bit, axis = (1, "x") if flat[number][1] else (2, "y")
+        return send(
+            source(number, plane ^ (3 if slot else bit)),
+            sides[number].at[slot],
+            send_sem.at[number, slot],
+            recv_sem.at[number, slot],
+            peers[axis],
+        )
+
+    def load_onward(number):
+        off = 2 if flat[number][1] else 1
+        return pltpu.make_async_copy(
+            source(number, plane ^ off), onwards[number], load_sem.at[number, 0]
+        )
+
+    def load_mine(number):
+        return pltpu.make_async_copy(source(number, plane), mines[number], load_sem.at[number, 1])
+
+    def onward_copy(number):
+        axis = "y" if flat[number][1] else "x"
+        return send(
+            onwards[number],
+            from_ons[number],
+            send_sem.at[number, 2],
+            recv_sem.at[number, 2],
+            peers[axis],
+        )
+
+    def line_copies(number):
+        return [
+            send(
+                mines[number].at[whole, line ^ offset],
+                from_lines[number].at[offset - 1],
+                send_sem.at[number, 2 + offset],
+                recv_sem.at[number, 2 + offset],
+                peers[offset],
+            )
+            for offset in (1, 2, 3)
+        ]
+
+    def core_copy(number):
+        return send(
+            mines[number].at[1 - core, line],
+            from_cores[number],
+            send_sem.at[number, 6],
+            recv_sem.at[number, 6],
+            peers["c"],
+        )
+
+    def is_cols(number):
+        return arrays[flat[number][0]][0] == "cols"
+
+    def add_into(target, *terms):
+        cores, lines, height, _ = target.shape
+
+        def body(step, carry):
+            side = step // (lines * (height // 16))
+            rest = step % (lines * (height // 16))
+            at_line = rest // (height // 16)
+            rows = pl.ds(pl.multiple_of((rest % (height // 16)) * 16, 16), 16)
+            value = target[side, at_line, rows].astype(jnp.float32)
+            for term in terms:
+                value = value + term[side, at_line, rows].astype(jnp.float32)
+            target[side, at_line, rows] = value.astype(target.dtype)
+            return carry
+
+        lax.fori_loop(0, cores * lines * (height // 16), body, 0)
+
+    def stage_one(number):
+        first_copy(number, 1).start()
+        first_copy(number, 0).start()
+        load_onward(number).start()
+        load_mine(number).start()
+
+    def stage_two(number):
+        first_copy(number, 1).wait_recv()
+        load_onward(number).wait()
+        add_into(onwards[number], sides[number].at[1])
+        onward_copy(number).start()
+
+    def stage_three(number):
+        first_copy(number, 0).wait_recv()
+        load_mine(number).wait()
+        onward_copy(number).wait_recv()
+        add_into(mines[number], sides[number].at[0], from_ons[number])
+        for copy in line_copies(number):
+            copy.start()
+
+    def stage_four(number):
+        for copy in line_copies(number):
+            copy.wait_recv()
+        array, _, rows, columns = flat[number]
+        mine, pieces = mines[number], from_lines[number]
+        for side in range(mine.shape[0]):
+            value = mine[side, line].astype(jnp.float32)
+            for offset in range(3):
+                value = value + pieces[offset, side].astype(jnp.float32)
+            mine[side, line] = value.astype(mine.dtype)
+        if is_cols(number):
+            core_copy(number).start()
+            targets[array][0][rows, columns] = mine[core, line]
+        else:
+            targets[array][0][rows, columns] = mine[0, line]
+
+    def stage_five(number):
+        if is_cols(number):
+            core_copy(number).wait()
+            array, _, rows, columns = flat[number]
+            targets[array][1][rows, columns] = from_cores[number][...]
+        first_copy(number, 0).wait_send()
+        first_copy(number, 1).wait_send()
+        onward_copy(number).wait_send()
+        for copy in line_copies(number):
+            copy.wait_send()
+
+    stages = (stage_one, stage_two, stage_three, stage_four, stage_five)
+    numbers, at = [], 0
+    for group in groups:
+        numbers.append(range(at, at + len(group)))
+        at += len(group)
+    for step in range(len(groups) + 4):
+        for lag, stage in enumerate(stages):
+            if 0 <= step - lag < len(groups):
+                for number in numbers[step - lag]:
+                    stage(number)
+
+
+def extent(sel, size):
+    return size if isinstance(sel, slice) else sel.size
+
+
+def reduce_gradients(arrays, groups, sources, collective_id):
+    flat = [unit for group in groups for unit in group]
+    vmem, dma, low = pltpu.VMEM, pltpu.SemaphoreType.DMA, jnp.bfloat16
+    shapes = []
+    for array, _, rows, columns in flat:
+        kind, (height, width) = arrays[array]
+        shapes.append((2 if kind == "cols" else 1, extent(rows, height), extent(columns, width)))
+    scratch = [vmem((2, c, 4, h, w), low) for c, h, w in shapes]
+    for _ in range(3):
+        scratch += [vmem((c, 4, h, w), low) for c, h, w in shapes]
+    scratch += [vmem((3, c, h, w), low) for c, h, w in shapes]
+    scratch += [vmem((h, w) if c == 2 else (16, 128), low) for c, h, w in shapes]
+    out_shape = []
+    for kind, shape in arrays:
+        out_shape += [jax.ShapeDtypeStruct(shape, low)] * (2 if kind == "cols" else 1)
+    return pl.pallas_call(
+        partial(reduce_kernel, arrays, groups),
+        out_shape=out_shape,
+        in_specs=anywhere(len(sources)),
+        out_specs=[pl.BlockSpec(memory_space=pltpu.VMEM)] * len(out_shape),
+        scratch_shapes=scratch
+        + [dma((len(flat), 7)), dma((len(flat), 7)), dma((len(flat), 2))],
+        compiler_params=pltpu.CompilerParams(
+            collective_id=collective_id, has_side_effects=True, vmem_limit_bytes=60 * 2**20
+        ),
+    )(*sources)
+
+
+def turned(values, cosine, sine):
+    lane = lax.broadcasted_iota(jnp.int32, values.shape, 1)
+    halfway = HD // 2
+    partner = jnp.where(
+        lane % HD < halfway,
+        pltpu.roll(values, 128 - halfway, 1),
+        pltpu.roll(values, halfway, 1),
+    )
+    return values * cosine + partner * sine
+
+
+def join_kernel(rows, times, weights, cosine, sine, joined, joined_time):
+    is_turned = pl.program_id(0) < 6
+
+    def body(step, carry):
+        at = pl.ds(pl.multiple_of(step * TILE, TILE), TILE)
+        values = jnp.dot(rows[at, :], weights[...], preferred_element_type=jnp.float32)
+
+        @pl.when(is_turned)
+        def turn():
+            for side in (0, 128):
+                joined[at, side : side + 128] = turned(
+                    values[:, side : side + 128], cosine[at, :], sine[at, :]
+                ).astype(joined.dtype)
+
+        @pl.when(jnp.logical_not(is_turned))
+        def keep():
+            joined[at, :] = values.astype(joined.dtype)
+
+        return carry
+
+    lax.fori_loop(0, rows.shape[0] // TILE, body, 0)
+    joined_time[...] = jnp.dot(
+        times[...], weights[...], preferred_element_type=jnp.float32
+    ).astype(joined_time.dtype)
+
+
+def join(rows, times, weights, cosine, sine):
+    width = weights.shape[1]
+
+    def fixed(array):
+        return pl.BlockSpec(array.shape, lambda step: (0, 0))
+
+    return pl.pallas_call(
+        join_kernel,
+        grid=(width // 256,),
+        in_specs=[
+            fixed(rows),
+            fixed(times),
+            pl.BlockSpec((D, 256), lambda step: (0, step)),
+            fixed(cosine),
+            fixed(sine),
+        ],
+        out_specs=[
+            pl.BlockSpec((rows.shape[0], 256), lambda step: (0, step)),
+            pl.BlockSpec((times.shape[0], 256), lambda step: (0, step)),
+        ],
+        out_shape=[
+            jax.ShapeDtypeStruct((rows.shape[0], width), jnp.bfloat16),
+            jax.ShapeDtypeStruct((times.shape[0], width), jnp.bfloat16),
+        ],
+        compiler_params=pltpu.CompilerParams(vmem_limit_bytes=48 * 2**20),
+        cost_estimate=pl.CostEstimate(
+            flops=2 * rows.shape[0] * D * width,
+            bytes_accessed=2 * (rows.size + weights.size + rows.shape[0] * width),
+            transcendentals=0,
+        ),
+    )(rows, times, weights, cosine, sine)
+
+
+def head_lanes(shape, head):
+    return lax.broadcasted_iota(jnp.int32, shape, 1) // HD == head
+
+
+def attend_kernel(timed, queries, keys, values, first, second, mixed, logsum):
+    def body(step, carry):
+        at = pl.ds(pl.multiple_of(step * TILE, TILE), TILE)
+        rows = queries[at, :]
+        total = jnp.zeros(rows.shape, jnp.float32)
+        sums = jnp.zeros(rows.shape, jnp.float32)
+        for head in range(2):
+            own = head_lanes(rows.shape, head)
+            query = jnp.where(own, rows, jnp.zeros_like(rows))
+            scores = dot_back(query, keys[...]) * SCORE_SCALE
+            if timed:
+                extra = (
+                    jnp.sum(
+                        query.astype(jnp.float32) * first[0:1, :].astype(jnp.float32),
+                        -1,
+                        keepdims=True,
+                    )
+                    * SCORE_SCALE
+                )
+                peak = jnp.maximum(jnp.max(scores, -1, keepdims=True), extra)
+            else:
+                scores = scores + first[0:1, :]
+                peak = jnp.max(scores, -1, keepdims=True)
+            powers = jnp.exp(scores - peak)
+            row_total = jnp.sum(powers, -1, keepdims=True)
+            mixture = jnp.dot(
+                powers.astype(jnp.bfloat16), values[...], preferred_element_type=jnp.float32
+            )
+            if timed:
+                power = jnp.exp(extra - peak)
+                row_total = row_total + power
+                mixture = mixture + power * second[0:1, :].astype(jnp.float32)
+            total = jnp.where(own, mixture / row_total, total)
+            sums = jnp.where(own, peak + jnp.log(row_total), sums)
+        mixed[at, :] = total.astype(mixed.dtype)
+        logsum[at, :] = sums
+        return carry
+
+    lax.fori_loop(0, queries.shape[0] // TILE, body, 0)
+
+
+def lane_block(array, offset):
+    return pl.BlockSpec((array.shape[0], 128), lambda pair: (0, pair + offset))
+
+
+def attend(queries, keys, values, extras, offsets, timed):
+    rows, count, pairs = queries.shape[0], keys.shape[0], HEADS // 4
+    extra_specs = (
+        [lane_block(extras[0], offsets[1]), lane_block(extras[1], offsets[2])]
+        if timed
+        else [pl.BlockSpec(extra.shape, lambda pair: (0, 0)) for extra in extras]
+    )
+    return pl.pallas_call(
+        partial(attend_kernel, timed),
+        grid=(pairs,),
+        in_specs=[
+            lane_block(queries, offsets[0]),
+            lane_block(keys, offsets[1]),
+            lane_block(values, offsets[2]),
+        ]
+        + extra_specs,
+        out_specs=[pl.BlockSpec((rows, 128), lambda pair: (0, pair))] * 2,
+        out_shape=[
+            jax.ShapeDtypeStruct((rows, 128 * pairs), jnp.bfloat16),
+            jax.ShapeDtypeStruct((rows, 128 * pairs), jnp.float32),
+        ],
+        compiler_params=pltpu.CompilerParams(vmem_limit_bytes=48 * 2**20),
+        cost_estimate=pl.CostEstimate(
+            flops=pairs * 2 * rows * count * 128 * 4,
+            bytes_accessed=pairs * 128 * (rows * 10 + count * 4),
+            transcendentals=pairs * 2 * rows * count,
+        ),
+    )(queries, keys, values, *extras)
+
+
+def attend_back_kernel(timed, *refs):
+    queries, keys, values, first, second, mixed, logsum, gradient = refs[:8]
+    if timed:
+        cosine, sine, out_q, out_k, out_v, out_first, out_second, sum_k, sum_v = refs[8:]
+    else:
+        out_q, out_k, out_v, sum_k, sum_v = refs[8:]
+    sum_k[...] = jnp.zeros_like(sum_k)
+    sum_v[...] = jnp.zeros_like(sum_v)
+    if timed:
+        out_first[...] = jnp.zeros_like(out_first)
+        out_second[...] = jnp.zeros_like(out_second)
+
+    def body(step, carry):
+        at = pl.ds(pl.multiple_of(step * TILE, TILE), TILE)
+        rows, grad = queries[at, :], gradient[at, :]
+        product = grad.astype(jnp.float32) * mixed[at, :].astype(jnp.float32)
+        sums = logsum[at, :]
+        sums_row = sums.T
+        grad_query = jnp.zeros(rows.shape, jnp.float32)
+        for head in range(2):
+            own = head_lanes(rows.shape, head)
+            query = jnp.where(own, rows, jnp.zeros_like(rows))
+            grad_own = jnp.where(own, grad, jnp.zeros_like(grad))
+            inner = jnp.sum(jnp.where(own, product, 0.0), -1, keepdims=True)
+            inner_row = jnp.broadcast_to(inner, rows.shape).T[0:1, :]
+            scores = dot_back(keys[...], query) * SCORE_SCALE
+            if not timed:
+                scores = scores + second[:, 0:1]
+            attention = jnp.exp(scores - sums_row[head * HD : head * HD + 1, :])
+            grad_attention = dot_back(values[...], grad_own)
+            sum_v[...] += jnp.dot(
+                attention.astype(jnp.bfloat16), grad_own, preferred_element_type=jnp.float32
+            )
+            grad_scores = (attention * (grad_attention - inner_row)).astype(jnp.bfloat16)
+            sum_k[...] += jnp.dot(grad_scores, query, preferred_element_type=jnp.float32)
+            key_own = jnp.where(
+                head_lanes(keys.shape, head), keys[...], jnp.zeros(keys.shape, keys.dtype)
+            )
+            grad_query = grad_query + tdot(grad_scores, key_own)
+            if timed:
+                key_time = jnp.where(
+                    own[0:1, :], first[0:1, :].astype(jnp.float32), jnp.zeros((1, 128), jnp.float32)
+                )
+                wide_query, wide_grad = query.astype(jnp.float32), grad_own.astype(jnp.float32)
+                score = jnp.sum(wide_query * key_time, -1, keepdims=True) * SCORE_SCALE
+                power = jnp.exp(score - sums[:, head * HD : head * HD + 1])
+                back = jnp.sum(
+                    wide_grad * second[0:1, :].astype(jnp.float32), -1, keepdims=True
+                )
+                grad_score = (power * (back - inner)).astype(jnp.bfloat16).astype(jnp.float32)
+                grad_query = grad_query + grad_score * key_time
+                out_first[0:1, :] += SCORE_SCALE * jnp.sum(
+                    grad_score * wide_query, 0, keepdims=True
+                )
+                out_second[0:1, :] += jnp.sum(
+                    power.astype(jnp.bfloat16).astype(jnp.float32) * wide_grad, 0, keepdims=True
+                )
+        grad_query = grad_query * SCORE_SCALE
+        if timed:
+            grad_query = turned(grad_query, cosine[at, :], -sine[at, :])
+        out_q[at, :] = grad_query.astype(out_q.dtype)
+        return carry
+
+    lax.fori_loop(0, queries.shape[0] // TILE, body, 0)
+    grad_key = sum_k[...] * SCORE_SCALE
+    if timed:
+        grad_key = turned(grad_key, cosine[...], -sine[...])
+    out_k[...] = grad_key.astype(out_k.dtype)
+    out_v[...] = sum_v[...].astype(out_v.dtype)
+
+
+def attend_back(queries, keys, values, extras, offsets, mixed, logsum, gradient, tables):
+    timed = tables is not None
+    rows, count, pairs = queries.shape[0], keys.shape[0], HEADS // 4
+    extra_specs = (
+        [lane_block(extras[0], offsets[1]), lane_block(extras[1], offsets[2])]
+        if timed
+        else [pl.BlockSpec(extra.shape, lambda pair: (0, 0)) for extra in extras]
+    )
+    low = jnp.bfloat16 if timed else jnp.float32
+
+    def out(height, dtype):
+        return (
+            jax.ShapeDtypeStruct((height, 128 * pairs), dtype),
+            pl.BlockSpec((height, 128), lambda pair: (0, pair)),
+        )
+
+    outs = [out(rows, jnp.bfloat16), out(count, low), out(count, low)]
+    operands = [queries, keys, values, *extras, mixed, logsum, gradient]
+    specs = (
+        [
+            lane_block(queries, offsets[0]),
+            lane_block(keys, offsets[1]),
+            lane_block(values, offsets[2]),
+        ]
+        + extra_specs
+        + [lane_block(mixed, 0), lane_block(logsum, 0), lane_block(gradient, 0)]
+    )
+    if timed:
+        outs += [out(8, jnp.float32), out(8, jnp.float32)]
+        operands += list(tables)
+        specs += [pl.BlockSpec(table.shape, lambda pair: (0, 0)) for table in tables]
+    return pl.pallas_call(
+        partial(attend_back_kernel, timed),
+        grid=(pairs,),
+        in_specs=specs,
+        out_specs=[spec for _, spec in outs],
+        out_shape=[shape for shape, _ in outs],
+        scratch_shapes=[pltpu.VMEM((count, 128), jnp.float32)] * 2,
+        compiler_params=pltpu.CompilerParams(vmem_limit_bytes=48 * 2**20),
+        cost_estimate=pl.CostEstimate(
+            flops=pairs * 2 * rows * count * 128 * 10,
+            bytes_accessed=pairs * 128 * (rows * 16 + count * 8),
+            transcendentals=pairs * 2 * rows * count,
+        ),
+    )(*operands)
+
+
+def lane_moves():
+    source = lax.broadcasted_iota(jnp.int32, (6, 2 * BLK, 2 * BLK), 1)
+    target = lax.broadcasted_iota(jnp.int32, (6, 2 * BLK, 2 * BLK), 2)
+    code = lax.broadcasted_iota(jnp.int32, (6, 2 * BLK, 2 * BLK), 0)
+    to_right, taken = code // 3, code % 3
+    moves = (target // BLK == to_right) & (taken < 2)
+    moves = moves & (source == target + (taken - to_right) * BLK)
+    return moves.astype(jnp.bfloat16)
+
+
+def pair_kernel(left_at, right_at, left_half, right_half, left, right, moves, target):
+    step = pl.program_id(0)
+    tile_shape = (BLK, 2 * BLK)
+    total = jnp.dot(
+        left[...].reshape(tile_shape), moves[left_half[step]], preferred_element_type=jnp.float32
+    )
+    total = total + jnp.dot(
+        right[...].reshape(tile_shape),
+        moves[3 + right_half[step]],
+        preferred_element_type=jnp.float32,
+    )
+    target[...] = total.astype(target.dtype).reshape(target.shape)
+
+
+def pair_up(blocks, places, halves, moves, source_spec, target_spec, shape):
+    steps = places.shape[0] // 2
+    return pl.pallas_call(
+        pair_kernel,
+        grid_spec=pltpu.PrefetchScalarGridSpec(
+            num_scalar_prefetch=4,
+            grid=(steps,),
+            in_specs=[
+                source_spec(lambda step, a, b, c, d: a[step]),
+                source_spec(lambda step, a, b, c, d: b[step]),
+                pl.BlockSpec(moves.shape, lambda step, a, b, c, d: (0, 0, 0)),
+            ],
+            out_specs=target_spec,
+        ),
+        out_shape=jax.ShapeDtypeStruct(shape, blocks.dtype),
+        cost_estimate=pl.CostEstimate(
+            flops=8 * steps * BLK**3, bytes_accessed=12 * steps * BLK * BLK, transcendentals=0
+        ),
+    )(places[0::2], places[1::2], halves[0::2], halves[1::2], blocks, blocks, moves)
+
+
+def stacked_spec(where):
+    return pl.BlockSpec((1, BLK, 2 * BLK), lambda *at: (where(*at), 0, 0))
+
+
+def tiled_spec(across):
+    def spec(where):
+        return pl.BlockSpec(
+            (BLK, 2 * BLK), lambda *at: (where(*at) // across, where(*at) % across)
+        )
+
+    return spec
+
+
+def assemble(pairs, slots, moves, rows, columns):
+    across = columns // (2 * BLK)
+    return pair_up(
+        pairs,
+        slots // 2,
+        slots % 2,
+        moves,
+        stacked_spec,
+        pl.BlockSpec((BLK, 2 * BLK), lambda step, *_: (step // across, step % across)),
+        (rows, columns),
+    )
+
+
+def collect(matrix, places, halves, moves):
+    return pair_up(
+        matrix,
+        places,
+        halves,
+        moves,
+        tiled_spec(matrix.shape[1] // (2 * BLK)),
+        pl.BlockSpec((1, BLK, 2 * BLK), lambda step, *_: (step, 0, 0)),
+        (places.shape[0] // 2, BLK, 2 * BLK),
+    )
 
 
 def item_per_chip(
@@ -918,10 +1465,8 @@
     core, line = lax.axis_index("c"), lax.axis_index("z")
     plane = 2 * row + column
     item = 4 * plane + line
-    spot = jnp.stack([plane, line, core]).astype(jnp.int32)
     quads = range(4)
     half = D // 2
-    heads = HEADS // 2
     items_total = 16
     mse_scale = 1.0 / (items_total * FRAMES * DIN)
 
@@ -933,86 +1478,15 @@
         ],
         0,
     ).astype(bf16)
-    packs = pack[None]
-    for axis in ("c", "z", "x", "y"):
-        packs = grow(packs, axis)
-    owner = jnp.arange(32, dtype=jnp.int32)
-    packs = packs[
-        ((owner // 4) % 2 ^ core) + 2 * (owner % 4 ^ line) + 8 * (owner // 8 ^ plane)
-    ]
-    ends_full = packs[:, :4].reshape(D, 2, DIN)
-    table_full = packs[:, 4:12].reshape(NTIME, D)
-    gain_values = packs[:, 12, :144].reshape(D, 3).astype(f32)
-    weight_in, weight_out = ends_full[:, 0, :], ends_full[:, 1, :]
-
     low_slots = square_slots.astype(bf16).reshape(4, 2, BLK, BLK)
-    low_pairs = jnp.concatenate([low_slots[:, 0], low_slots[:, 1]], 2)
-    slot_pieces = []
-    for color, (first, second) in enumerate((("x", "y"), ("y", "x"))):
-        pieces = gather_pieces(low_pairs[2 * color : 2 * color + 2], first, second)
-        slot_pieces.append(jnp.concatenate(pieces, 0))
-    own_pairs = jnp.concatenate(slot_pieces, 0).reshape(64, BLK, 2 * BLK)
-    all_pairs = jnp.concatenate([own_pairs, swap(own_pairs, "c")], 0)
-    inverse_order = (
-        jnp.zeros_like(assignment)
-        .at[assignment]
-        .set(jnp.arange(assignment.shape[0], dtype=jnp.int32))
-    )
-
-    def pair_place(slot):
-        device, inner = slot // 8, slot % 8
-        place_value = ((device // 4) % 2 ^ core) * 2 + inner // 4
-        place_value = (place_value * 4 + (device // 8 ^ plane)) * 4 + (device % 4 ^ line)
-        return place_value * 2 + (inner // 2) % 2, inner % 2
-
-    def grid_blocks(matrix, rows, columns):
-        return (matrix * 64 + rows * 8 + columns).reshape(-1)
-
-    eight, four = jnp.arange(8, dtype=jnp.int32), jnp.arange(4, dtype=jnp.int32)
-    joined_blocks = grid_blocks(
-        jnp.arange(3, dtype=jnp.int32)[None, :, None],
-        eight[:, None, None],
-        (4 * core + four)[None, None, :],
-    )
-    out_blocks = grid_blocks(3, (4 * core + four)[:, None], eight[None, :])
-    places, rights = pair_place(inverse_order[joined_blocks])
-    projection = assemble(all_pairs, places, rights, D, 3 * half)
-    places, rights = pair_place(inverse_order[out_blocks])
-    weight_mix = assemble(all_pairs, places, rights, half, D)
-
+    low_pairs = jnp.concatenate([low_slots[:, 0], low_slots[:, 1]], 2).reshape(4 * BLK, 2 * BLK)
     low_cross = cross_weights.astype(bf16)
-    query_both = jnp.stack(
-        [
-            lax.dynamic_slice_in_dim(low_cross[:, 0, :], core * half, half, 1),
-            swap(
-                lax.dynamic_slice_in_dim(low_cross[:, 0, :], (1 - core) * half, half, 1), "c"
-            ),
-        ],
-        0,
-    )
-    cross_query = place(gather_pieces(query_both, "x", "y"), spot)
-    out_own = place(gather_pieces(low_cross[None, :, 1, :], "y", "x"), spot)
-    out_own = out_own.reshape(2, 2, 1, 4 * 48, D)
-    out_kept = pick(out_own, core)
-    out_other = swap(pick(out_own, 1 - core), "c")
-    cross_out = jnp.where(
-        core == 0,
-        jnp.concatenate([out_kept, out_other], 1),
-        jnp.concatenate([out_other, out_kept], 1),
-    ).reshape(half, D)
     low_kv = key_value.astype(bf16)
-    kv_weights = []
-    for color, (first, second) in enumerate((("x", "y"), ("y", "x"))):
-        own = lax.dynamic_slice_in_dim(low_kv, color * D + core * half, half, 1)
-        other = lax.dynamic_slice_in_dim(low_kv, color * D + (1 - core) * half, half, 1)
-        pieces = gather_pieces(jnp.stack([own, swap(other, "c")], 0), first, second)
-        stacked = jnp.stack(pieces, 0)
-        stacked = stacked[plane ^ four][:, line ^ four]
-        stacked = stacked[:, :, core ^ four[:2]]
-        kv_weights.append(stacked.transpose(0, 2, 1, 3, 4).reshape(DT, half))
-    kv_own = jnp.concatenate(kv_weights, 1)
-
     low_gate = gate_up.astype(bf16)
+    low_down = down_weight.astype(bf16)
+
+    def head_columns(array, which, side):
+        return lax.dynamic_slice_in_dim(array, which * D + side * half, half, 1)
 
     def unit_columns(which, side):
         return jnp.concatenate(
@@ -1025,18 +1499,91 @@
             1,
         )
 
-    gate_sides = []
-    for which, (first, second) in enumerate((("x", "y"), ("y", "x"))):
-        block = jnp.stack(
-            [unit_columns(which, core), swap(unit_columns(which, 1 - core), "c")], 0
+    def kv_block(which, side):
+        return head_columns(low_kv, which, side).reshape(16, 1152)
+
+    arrays = (
+        ("cols", (16, D), bf16),
+        ("both", (4 * BLK, 2 * BLK), bf16),
+        ("cols", (48, half), bf16),
+        ("half", (48, D), bf16),
+        ("cols", (16, 1152), bf16),
+        ("cols", (16, 1152), bf16),
+        ("cols", (48, FF // 2), bf16),
+        ("cols", (48, FF // 2), bf16),
+        ("one", (192, D), bf16),
+    )
+    whole = slice(None)
+    groups = [((0, 0, whole, whole), (5, 1, whole, whole))]
+    groups += [
+        ((1, 0, pl.ds(step * 192, 192), whole), (1, 1, pl.ds(384 + step * 192, 192), whole))
+        for step in range(2)
+    ]
+    groups += [((2, 0, whole, whole), (3, 1, whole, whole), (4, 0, whole, whole))]
+    groups += [
+        ((6, 0, whole, pl.ds(step * 768, 768)), (7, 1, whole, pl.ds(step * 768, 768)))
+        for step in range(4)
+    ]
+    groups += [
+        ((8, 0, whole, pl.ds(step * 384, 384)), (8, 1, whole, pl.ds(half + step * 384, 384)))
+        for step in range(2)
+    ]
+    packs, all_pairs, cross_query, cross_out, keys_own, values_own, gate_weight, up_weight, down = (
+        gather_weights(
+            arrays,
+            groups,
+            (
+                pack,
+                pack,
+                low_pairs,
+                head_columns(low_cross[:, 0, :], 0, core),
+                head_columns(low_cross[:, 0, :], 0, 1 - core),
+                low_cross[:, 1, :],
+                kv_block(0, core),
+                kv_block(0, 1 - core),
+                kv_block(1, core),
+                kv_block(1, 1 - core),
+                unit_columns(0, core),
+                unit_columns(0, 1 - core),
+                unit_columns(1, core),
+                unit_columns(1, 1 - core),
+                low_down,
+            ),
+            1,
         )
-        gate_sides.append(place(gather_pieces(block, first, second), spot))
-    gate_weight, up_weight = gate_sides
-    low_down = down_weight.astype(bf16)
-    down_sides = []
-    for which, (first, second) in enumerate((("x", "y"), ("y", "x"))):
-        block = low_down[None, :, which * half : (which + 1) * half]
-        down_sides.append(place(gather_pieces(block, first, second), spot))
+    )
+    packs = packs.reshape(32, 16, D)
+    ends_full = packs[:, :4].reshape(D, 2, DIN)
+    table_full = packs[:, 4:12].reshape(NTIME, D)
+    gain_values = packs[:, 12, :144].reshape(D, 3).astype(f32)
+    weight_in, weight_out = ends_full[:, 0, :], ends_full[:, 1, :]
+    all_pairs = all_pairs.reshape(128, BLK, 2 * BLK)
+    inverse_order = (
+        jnp.zeros_like(assignment)
+        .at[assignment]
+        .set(jnp.arange(assignment.shape[0], dtype=jnp.int32))
+    )
+
+    def grid_blocks(matrix, rows, columns):
+        return (matrix * 64 + rows * 8 + columns).reshape(-1)
+
+    eight, four = jnp.arange(8, dtype=jnp.int32), jnp.arange(4, dtype=jnp.int32)
+    joined_blocks = grid_blocks(
+        jnp.arange(3, dtype=jnp.int32)[None, :, None],
+        eight[:, None, None],
+        (4 * core + four)[None, None, :],
+    )
+    out_blocks = grid_blocks(3, (4 * core + four)[:, None], eight[None, :])
+    moves = lane_moves()
+    projection = assemble(all_pairs, inverse_order[joined_blocks], moves, D, 3 * half)
+    weight_mix = assemble(all_pairs, inverse_order[out_blocks], moves, half, D)
+    cross_query = cross_query.reshape(D, half)
+    cross_out = lax.dynamic_slice_in_dim(cross_out.reshape(D, D), core * half, half, 0)
+    kv_own = jnp.concatenate(
+        [keys_own.reshape(DT, half), values_own.reshape(DT, half)], 1
+    )
+    gate_weight, up_weight = gate_weight.reshape(D, FF // 2), up_weight.reshape(D, FF // 2)
+    down = down.reshape(FF // 2, D)
 
     meta = jnp.concatenate([timesteps[:, None], text_lengths[:, None], negatives], 1)
     metas = meta
@@ -1060,8 +1607,8 @@
     halfway = HD // 2
     frequency = jnp.exp(jnp.arange(halfway, dtype=f32) * (-2.0 * math.log(10000.0) / HD))
     turn = frame_positions.astype(f32)[:, None] * frequency[None, :]
-    cosine_table = jnp.concatenate([jnp.cos(turn)] * 2, -1)
-    sine_table = jnp.concatenate([jnp.sin(turn)] * 2, -1)
+    cosine_table = jnp.concatenate([jnp.cos(turn)] * 4, -1)
+    sine_table = jnp.concatenate([-jnp.sin(turn), jnp.sin(turn)] * 2, -1)
     angle = (timestep.astype(f32) + 0.5) * (0.5 * math.pi / NTIME)
     signal, spread = jnp.cos(angle), jnp.sin(angle)
     noised = (signal * clean + spread * noise).astype(bf16)
@@ -1074,37 +1621,28 @@
     embeds = jnp.dot(features, table_full, preferred_element_type=f32)
     normed_time, inverse_time = layer_stats(embeds)
     input_time = (normed_time * gain_values[:, 0]).astype(bf16)
-    joined_rows = jnp.dot(input_one, projection, preferred_element_type=f32)
-    head_shape = (FRAMES, heads, HD)
-    rot_queries = rotate(
-        joined_rows[:, :half].reshape(head_shape), cosine_table, sine_table
-    ).astype(bf16)
-    rot_keys = rotate(
-        joined_rows[:, half : 2 * half].reshape(head_shape), cosine_table, sine_table
-    ).astype(bf16)
-    value_rows = joined_rows[:, 2 * half :].astype(bf16)
-    time_pair = jnp.dot(input_time, projection[:, half:], preferred_element_type=f32).astype(bf16)
-    all_keys = jnp.concatenate([time_pair[:, :half].reshape(1, heads, HD), rot_keys], 0)
-    all_values = jnp.concatenate([time_pair[:, half:], value_rows], 0).reshape(-1, heads, HD)
-    self_bias = jnp.zeros((1, FRAMES + 1), f32)
-    mixed_self, logsum_self = attend_forward(
-        rot_queries[None], all_keys[None], all_values[None], self_bias
-    )
-    mixed_flat = mixed_self.reshape(FRAMES, half)
+    time_block = jnp.pad(input_time, ((0, 15), (0, 0)))
+    joined, joined_time = join(input_one, time_block, projection, cosine_table, sine_table)
+    pairs = half // 128
+    self_offsets = (0, pairs, 2 * pairs)
+    mixed_flat, logsum_self = attend(
+        joined, joined, joined, (joined_time, joined_time), self_offsets, True
+    )
     after_self = residual + on_both(jnp.dot(mixed_flat, weight_mix, preferred_element_type=f32))
     normed_two, inverse_two = layer_stats(after_self)
     input_two = (normed_two * gain_values[:, 1]).astype(bf16)
     cross_queries = jnp.dot(input_two, cross_query, preferred_element_type=f32).astype(bf16)
-    cross_heads = cross_queries.reshape(head_shape)
     projected = jnp.dot(tokens, kv_own, preferred_element_type=f32).astype(bf16)
     valid = token_slots < text_length
     cross_bias = jnp.where(valid, 0.0, MASK_VALUE).astype(f32)[None]
-    text_keys = projected[:, :half].reshape(1, -1, heads, HD)
-    text_values = projected[:, half:].reshape(1, -1, heads, HD)
-    mixed_cross, logsum_cross = attend_forward(
-        cross_heads[None], text_keys, text_values, cross_bias
-    )
-    cross_flat = mixed_cross.reshape(FRAMES, half)
+    text_biases = (
+        jnp.broadcast_to(cross_bias, (8, 128)),
+        jnp.broadcast_to(cross_bias.T, (128, 128)),
+    )
+    cross_offsets = (0, 0, pairs)
+    cross_flat, logsum_cross = attend(
+        cross_queries, projected, projected, text_biases, cross_offsets, False
+    )
     after_cross = after_self + on_both(jnp.dot(cross_flat, cross_out, preferred_element_type=f32))
     normed_three, inverse_three = layer_stats(after_cross)
     input_three = (normed_three * gain_values[:, 2]).astype(bf16)
@@ -1113,9 +1651,7 @@
     sigmoid = jax.nn.sigmoid(gate_part)
     silu_value = gate_part * sigmoid
     hidden = (silu_value * up_part).astype(bf16)
-    down_out = jnp.concatenate(
-        [on_both(jnp.dot(hidden, side, preferred_element_type=f32)) for side in down_sides], 1
-    )
+    down_out = on_both(jnp.dot(hidden, down, preferred_element_type=f32))
     output_rows = after_cross + down_out
     output_low = output_rows.astype(bf16)
     predicted = jnp.dot(output_low, weight_out, preferred_element_type=f32)
@@ -1166,45 +1702,39 @@
     grad_out_weight = tdot(output_low, grad_predicted)
     grad_output = dot_back(grad_predicted, weight_out) + grad_audio[None, :] / FRAMES
     grad_low = grad_output.astype(bf16)
-    reduced_down = []
-
-    def columns_of(values, quadrant, width):
-        return lax.dynamic_slice_in_dim(values, (plane ^ quadrant) * width, width, 1)
-
-    for which, first in enumerate(("y", "x")):
-        parts = [
-            tdot(
-                columns_of(hidden, quadrant, 768), grad_low[:, which * half : (which + 1) * half]
-            )
-            .astype(bf16)
-            .reshape(4, 192, half)
-            for quadrant in quads
-        ]
-        reduced_down.append(reduce_quads(parts, first, line, 0))
-    grad_down = jnp.concatenate(reduced_down, 1)
-    grad_hidden = dot_back(grad_low[:, :half], down_sides[0]) + dot_back(
-        grad_low[:, half:], down_sides[1]
-    )
+    grad_down = tdot(hidden, grad_low).astype(bf16)
+    grad_hidden = dot_back(grad_low, down)
     grad_gate = (grad_hidden * up_part * sigmoid * (1.0 + gate_part * (1.0 - sigmoid))).astype(bf16)
     grad_up = (grad_hidden * silu_value).astype(bf16)
-    reduced_gate = []
-    for gradient, first in ((grad_gate, "y"), (grad_up, "x")):
-        parts = [
-            tdot(columns_of(input_three, quadrant, 384), gradient)
-            .astype(bf16)
-            .reshape(2, 4, 48, FF // 2)
-            for quadrant in quads
-        ]
-        both_rows = reduce_quads(parts, first, line, 1)
-        other = swap(pick(both_rows, 1 - core).astype(bf16), "c").astype(f32)
-        reduced_gate.append((pick(both_rows, core), other))
+    grad_gate_weight = tdot(input_three, grad_gate).astype(bf16)
+    grad_up_weight = tdot(input_three, grad_up).astype(bf16)
+    feed_arrays = (("cols", (48, FF // 2)), ("cols", (48, FF // 2)), ("one", (192, D)))
+    feed_groups = [
+        ((2, 0, whole, pl.ds(step * 384, 384)), (2, 1, whole, pl.ds(half + step * 384, 384)))
+        for step in range(2)
+    ]
+    feed_groups += [
+        ((0, 0, whole, pl.ds(step * 768, 768)), (1, 1, whole, pl.ds(step * 768, 768)))
+        for step in range(4)
+    ]
+    feed_sums = reduce_gradients(
+        feed_arrays,
+        feed_groups,
+        (
+            grad_gate_weight.reshape(4, 2, 4, 48, FF // 2),
+            grad_up_weight.reshape(4, 2, 4, 48, FF // 2),
+            grad_down.reshape(4, 1, 4, 192, D),
+        ),
+        2,
+    )
     gate_columns = []
-    for mine, other in reduced_gate:
+    for mine, other in ((feed_sums[0], feed_sums[1]), (feed_sums[2], feed_sums[3])):
         sides = (jnp.where(core == 0, mine, other), jnp.where(core == 0, other, mine))
         for quadrant in quads:
             for side in sides:
                 gate_columns.append(side[:, quadrant * 768 : (quadrant + 1) * 768])
-    grad_gate_up = jnp.concatenate(gate_columns, 1)
+    grad_gate_up = jnp.concatenate(gate_columns, 1).astype(f32)
+    grad_down = feed_sums[4].astype(f32)
     grad_input_three = on_both(dot_back(grad_gate, gate_weight) + dot_back(grad_up, up_weight))
     grad_after_cross, gain_three = layer_back(
         grad_input_three, normed_three, inverse_three, gain_values[:, 2]
@@ -1215,99 +1745,62 @@
     cross_kept = pick(cross_rows, core, 1)
     cross_received = swap(pick(cross_rows, 1 - core, 1), "c")
     cross_pair = jnp.stack([cross_kept, cross_received], 0)
-    parts = [
-        pick(pick(cross_pair, row ^ (quadrant // 2) ^ core), column ^ (quadrant % 2)).reshape(
-            4, 48, D
-        )
-        for quadrant in quads
-    ]
-    grad_cross_out = reduce_quads(parts, "x", line, 0)
-    grad_mixed_cross = dot_back(grad_cross_in, cross_out).astype(bf16).reshape(head_shape)
-    grad_cq, grad_text_keys, grad_text_values = attend_backward(
-        cross_heads[None],
-        text_keys,
-        text_values,
-        cross_bias,
+    out_rows = jnp.where(core == 0, cross_pair, cross_pair[::-1]).reshape(4, 1, 4, 48, D)
+    grad_mixed_cross = dot_back(grad_cross_in, cross_out).astype(bf16)
+    grad_cq, grad_text_keys, grad_text_values = attend_back(
+        cross_queries,
+        projected,
+        projected,
+        text_biases,
+        cross_offsets,
+        cross_flat,
         logsum_cross,
-        grad_mixed_cross[None],
-    )
-    grad_cq_low = grad_cq.reshape(FRAMES, half).astype(bf16)
-    parts = [
-        tdot(columns_of(input_two, quadrant, 384), grad_cq_low).astype(bf16).reshape(2, 4, 48, half)
-        for quadrant in quads
-    ]
-    both_rows = reduce_quads(parts, "y", line, 1)
-    query_other = swap(pick(both_rows, 1 - core).astype(bf16), "c").astype(f32)
-    query_mine = pick(both_rows, core)
-    grad_cross_query = jnp.where(
-        core == 0,
-        jnp.concatenate([query_mine, query_other], 1),
-        jnp.concatenate([query_other, query_mine], 1),
-    )
-    grad_cross = jnp.stack([grad_cross_query, grad_cross_out], 1)
-    grad_input_two = on_both(dot_back(grad_cq_low, cross_query))
+        grad_mixed_cross,
+        None,
+    )
+    grad_query_weight = tdot(input_two, grad_cq).astype(bf16).reshape(4, 2, 4, 48, half)
+    grad_input_two = on_both(dot_back(grad_cq, cross_query))
     text_half_grad = lax.dynamic_slice_in_dim(grad_text, core * half, half, 0)
     grad_pair_keys = (
-        grad_text_keys.reshape(-1, half) + mask * (text_half_grad[None, :] / length_float)
+        grad_text_keys + mask * (text_half_grad[None, :] / length_float)
     ).astype(bf16)
-    grad_pair_values = grad_text_values.reshape(-1, half).astype(bf16)
-    kv_columns = []
-    for gradient, first in ((grad_pair_keys, "y"), (grad_pair_values, "x")):
-        parts = [
-            tdot(columns_of(tokens, quadrant, 192), gradient).astype(bf16).reshape(2, 4, 24, half)
-            for quadrant in quads
-        ]
-        both_rows = reduce_quads(parts, first, line, 1)
-        other = swap(pick(both_rows, 1 - core).astype(bf16), "c").astype(f32)
-        mine = pick(both_rows, core)
-        kv_columns.append(jnp.where(core == 0, mine, other))
-        kv_columns.append(jnp.where(core == 0, other, mine))
-    grad_key_value = jnp.concatenate(kv_columns, 1)
+    kv_sources = [
+        tdot(tokens, gradient.astype(bf16)).astype(bf16).reshape(4, 2, 4, 16, 1152)
+        for gradient in (grad_pair_keys, grad_text_values)
+    ]
     grad_after_self, gain_two = layer_back(
         grad_input_two, normed_two, inverse_two, gain_values[:, 1]
     )
     grad_after_self = grad_after_self + grad_after_cross
     grad_self_in = grad_after_self.astype(bf16)
     grad_mix = tdot(mixed_flat, grad_self_in).astype(bf16)
-    grad_mixed_self = dot_back(grad_self_in, weight_mix).astype(bf16).reshape(head_shape)
-    grad_rot_queries, grad_keys, grad_values = attend_backward(
-        rot_queries[None],
-        all_keys[None],
-        all_values[None],
-        self_bias,
+    grad_mixed_self = dot_back(grad_self_in, weight_mix).astype(bf16)
+    grad_queries, grad_keys, grad_values, grad_time_keys, grad_time_values = attend_back(
+        joined,
+        joined,
+        joined,
+        (joined_time, joined_time),
+        self_offsets,
+        mixed_flat,
         logsum_self,
-        grad_mixed_self[None],
-    )
-    grad_queries = rotate_back(grad_rot_queries[0], cosine_table, sine_table)
-    grad_key_rows = rotate_back(grad_keys[0, 1:], cosine_table, sine_table)
-    grad_joined = jnp.concatenate(
-        [
-            grad_queries.astype(bf16).reshape(FRAMES, half),
-            grad_key_rows.astype(bf16).reshape(FRAMES, half),
-            grad_values[0, 1:].astype(bf16).reshape(FRAMES, half),
-        ],
-        1,
-    )
-    grad_time_pair = jnp.concatenate(
-        [grad_keys[0, 0].reshape(1, half), grad_values[0, 0].reshape(1, half)], 1
-    )
-    grad_projection = tdot(input_one, grad_joined)
-    time_rows = input_time.astype(f32).reshape(D, 1) * grad_time_pair
-    grad_projection = jnp.concatenate(
-        [
-            grad_projection[:, :half].astype(bf16),
-            (grad_projection[:, half:] + time_rows).astype(bf16),
-            jnp.concatenate([grad_mix[:, :half], grad_mix[:, half:]], 0),
-        ],
-        1,
+        grad_mixed_self,
+        (cosine_table, sine_table),
+    )
+    grad_joined = jnp.concatenate([grad_queries, grad_keys, grad_values], 1)
+    grad_time_pair = jnp.concatenate([grad_time_keys[:1], grad_time_values[:1]], 1)
+    time_row = jnp.concatenate([jnp.zeros((1, half), f32), grad_time_pair], 1)
+    grad_projection = (
+        tdot(input_one, grad_joined) + input_time.astype(f32).reshape(D, 1) * time_row
+    ).astype(bf16)
+    grad_squares = jnp.concatenate(
+        [grad_projection, jnp.concatenate([grad_mix[:, :half], grad_mix[:, half:]], 0)], 1
     )
 
     position = jnp.arange(256, dtype=jnp.int32)
     owner_core = core ^ (position // 128)
-    owner_plane = plane ^ ((position // 16) % 4)
-    owner_line = (position // 4) % 4
-    inner = ((position // 64) % 2) * 4 + position % 4
-    block = assignment[owner_plane * 64 + owner_core * 32 + owner_line * 8 + inner]
+    block = assignment[
+        (position // 32) % 4 * 64 + owner_core * 32 + (position // 8) % 4 * 8 + position % 8
+    ]
     matrix, block_row, block_column = block // 64, (block // 8) % 8, block % 8
     is_out = matrix == 3
     out_pair = block_column // 2
@@ -1315,17 +1808,12 @@
     tile_column = jnp.where(is_out, 6 + out_pair % 2, matrix * 2 + (block_column % 4) // 2)
     held = jnp.where(is_out, block_row // 4, block_column // 4) == core
     collected = collect(
-        grad_projection,
+        grad_squares,
         jnp.where(held, tile_row * 8 + tile_column, 0),
-        jnp.where(held, block_column % 2, 2 + block_column % 2),
-    ).reshape(2, 2, 4, 4, 2, BLK, 2 * BLK)
+        jnp.where(held, block_column % 2, 2),
+        moves,
+    ).reshape(2, 4, 1, 4, 4 * BLK, 2 * BLK)
     slot_sums = low_sum(collected[0], swap(collected[1], "c")).astype(bf16)
-    slot_colors = [
-        reduce_quads([slot_sums[color, quadrant] for quadrant in quads], first, line, 0)
-        for color, first in enumerate(("y", "x"))
-    ]
-    slot_rows = jnp.concatenate(slot_colors, 0)
-    grad_slots = jnp.stack([slot_rows[:, :, :BLK], slot_rows[:, :, BLK:]], 1).reshape(8, BLK, BLK)
 
     partial_one = dot_back(grad_joined, projection)
     partial_time = jnp.dot(
@@ -1357,7 +1845,52 @@
         ],
         3,
     )
-    small = reduce_small(small, row, column, line)
+    rest_arrays = (
+        ("one", (4 * BLK, 2 * BLK)),
+        ("cols", (48, half)),
+        ("one", (48, D)),
+        ("cols", (16, 1152)),
+        ("cols", (16, 1152)),
+        ("one", (16, D)),
+    )
+    rest_groups = [
+        ((1, 0, whole, whole), (2, 1, whole, whole), (3, 0, whole, whole), (4, 1, whole, whole))
+    ]
+    rest_groups += [
+        ((0, 0, pl.ds(step * 192, 192), whole), (0, 1, pl.ds(384 + step * 192, 192), whole))
+        for step in range(2)
+    ]
+    rest_groups += [((5, 0, whole, whole),)]
+    rest_sums = reduce_gradients(
+        rest_arrays,
+        rest_groups,
+        (
+            slot_sums,
+            grad_query_weight,
+            out_rows,
+            kv_sources[0],
+            kv_sources[1],
+            small.astype(bf16).reshape(4, 1, 4, 16, D),
+        ),
+        3,
+    )
+    slot_rows, query_mine, query_other, grad_cross_out, *kv_sums, small = (
+        value.astype(f32) for value in rest_sums
+    )
+    slot_rows = slot_rows.reshape(4, BLK, 2 * BLK)
+    grad_slots = jnp.stack([slot_rows[:, :, :BLK], slot_rows[:, :, BLK:]], 1).reshape(8, BLK, BLK)
+    grad_cross_query = jnp.where(
+        core == 0,
+        jnp.concatenate([query_mine, query_other], 1),
+        jnp.concatenate([query_other, query_mine], 1),
+    )
+    grad_cross = jnp.stack([grad_cross_query, grad_cross_out], 1)
+    kv_columns = []
+    for mine, other in (kv_sums[:2], kv_sums[2:]):
+        mine, other = mine.reshape(24, half), other.reshape(24, half)
+        kv_columns.append(jnp.where(core == 0, mine, other))
+        kv_columns.append(jnp.where(core == 0, other, mine))
+    grad_key_value = jnp.concatenate(kv_columns, 1)
     grad_ends = small[:4].reshape(48, 2, DIN)
     grad_table = small[4:12]
     grad_gains = small[12, :144].reshape(48, 3)

time: 2180 us -> 1780 us (0.82)
  Pallas kernels: 198 us -> 1160 us
  waiting for transfers between devices: 869 us -> 34.7 us
  other arithmetic: 333 us -> 162 us
  matrix products: 421 us -> 258 us
  starting transfers between devices: 131 us -> 27.2 us
  local copies, waits for them, and re-layouts: 201 us -> 105 us
    pallas_call x9 -> x11, Pallas kernels: 198 us -> 1160 us  [the longest x2 458 us: reduce_gradients(): pl.pallas_call(partial(reduce_kernel, arrays, groups), out_shape=out_shap...]
    ppermute x152 -> x30, waiting for transfers between devices: 869 us -> 34.7 us  [swap(): lax.ppermute(values, axis, [(i, i ^ bit) for i in range(lax.axis_size(axi...]
    dot_general x16 -> x1, matrix products: 160 us -> 15.9 us  [item_per_chip(): down_out = on_both(jnp.dot(hidden, down, preferred_element_type=f32))]
    ppermute x152 -> x30, starting transfers between devices: 131 us -> 27.2 us  [swap(): lax.ppermute(values, axis, [(i, i ^ bit) for i in range(lax.axis_size(axi...]
    convert_element_type x25 -> x4, other arithmetic: 70.8 us -> 4.18 us  [the longest x1 1.87 us: lane_moves(): return moves.astype(jnp.bfloat16)]
    unnamed x581 -> x318, local copies, waits for them, and re-layouts: 65.6 us -> 29.5 us
    dot_general x33 -> x11, matrix products: 105 us -> 75.8 us  [tdot(): lax.dot_general(left, right, (((0,), (0,)), ((), ())), preferred_element_...]
    slice x26 -> x16, local copies, waits for them, and re-layouts: 37.2 us -> 9.19 us  [the longest x3 2.15 us: pair_up(): halves[1::2]]
  transfers between devices with their start and end apart: 152 -> 30, of which waited for: 76 -> 15; matrix products, arithmetic and copies ran while one was open for 32% -> 10% of each run, Pallas kernels for 9% -> 43%
where the time goes in v2:
time: 1780 us; the launch traced here: 1760 us
  Pallas kernels  1160 us (65%)
  matrix products  258 us (14%)
  other arithmetic  162 us (9%)
  local copies, waits for them, and re-layouts  105 us (6%)
  waiting for transfers between devices  34.7 us (2%)
  starting transfers between devices  27.2 us (2%)
    pallas_call x2, Pallas kernels, reduce_gradients(): pl.pallas_call(partial(reduce_kernel, arrays, groups), out_shape=out_shap...  458 us
    pallas_call x1, Pallas kernels, gather_weights(): pl.pallas_call(partial(gather_kernel, arrays, groups), out_shape=[jax.Sha...  426 us
    pallas_call x3, Pallas kernels, pair_up(): pl.pallas_call(pair_kernel, grid_spec=pltpu.PrefetchScalarGridSpec(num_sc...  141 us
    dot_general x9, matrix products, dot_back(): lax.dot_general(left, right, (((1,), (1,)), ((), ())), preferred_element_...  89.7 us
    dot_general x11, matrix products, tdot(): lax.dot_general(left, right, (((0,), (0,)), ((), ())), preferred_element_...  75.8 us
    pallas_call x2, Pallas kernels, attend_back(): pl.pallas_call(partial(attend_back_kernel, timed), grid=(pairs,), in_spec...  63.8 us
    pallas_call x2, Pallas kernels, attend(): pl.pallas_call(partial(attend_kernel, timed), grid=(pairs,), in_specs=[la...  47.8 us
  transfers between devices with their start and end apart: 30, of which 15 were waited for; matrix products, arithmetic and copies ran while one was open for 10% of the time, Pallas kernels for 43%

profile of v2, /device:TPU:0, one launch (start us, length us, event | category | flops | bytes accessed | tf_op | source)
XLA Modules:
  0.0 1763.6 jit_solution(6730610049030022061)
XLA Ops:
  39.8 426.4 %shard_map.520 = (bf16[4,2,4,16,1536]{4,3,2,1,0:T(8,128)(2,1)}, bf16[4,2,4,768,384]{4,3,2,1,0:T(8,128)(2,1)}, bf16[4,2,4,48,768]{4,3,2,1,0:T(8,128)(2,1)}, bf16[...) custom-call(bf16[16,1536]{1,0:T(8,128)(2,1)} %fusion.68.refs_0_.refs, ...), custom_call_target="tpu_custom_call" | custom-call | tf_op jit(solution)/shard_map/pallas_call | solution.py:872
  479.3 13.9 shard_map.524
  493.2 36.8 %shard_map.521.weights = bf16[1536,2304]{1,0:T(8,128)(2,1)} custom-call(s32[48]{0:T(128)} %slice.239.left_at, s32[48]{0:T(128)} %slice.240.right_at, s32[48]{0:T(128)} %slice.241.left_half, s32[48]{0:T(128)} %slice.242.right_half, bf16[128,192,384]{2,1,0:T(8,128)(2,1)} %bitcast.199, bf16[128,192,384]{2,1,0:T(8,128)(2,1)} %bitcast.200, ...), custom_call_target="tpu_custom_call" | custom-call | flops 2717908992 | bytes 21233664 | tf_op jit(solution)/shard_map/pallas_call | solution.py:1371
  547.0 8.0 collective-permute-start.4
  567.9 23.1 %shard_map.522 = (bf16[1024,2304]{1,0:T(8,128)(2,1)}, bf16[16,2304]{1,0:T(8,128)(2,1)S(1)}) custom-call(bf16[1024,1536]{1,0:T(8,128)(2,1)S(1)} %multiply_convert_fusion.5.rows, bf16[16,1536]{1,0:T(8,128)(2,1)S(1)} %pad.15.times, bf16[1536,2304]{1,0:T(8,128)(2,1)} %shard_map.521.weights, f32[1024,128]{1,0:T(8,128)S(1)} %pad_maximum_fusion.7.cosine.refs_8_, ...), custom_call_target="tpu_custom_call" | custom-call | flops 7247757312 | bytes 14942208 | tf_op jit(solution)/shard_map/pallas_call | solution.py:1121
  591.0 31.0 %shard_map.523 = (bf16[1024,768]{1,0:T(8,128)(2,1)S(1)}, f32[1024,768]{1,0:T(8,128)S(1)}) custom-call(bf16[1024,2304]{1,0:T(8,128)(2,1)} %get-tuple-element.66.queries.keys.values.refs_0_.refs_1_.refs_2_, bf16[1024,2304]{1,0:T(8,128)(2,1)} %get-tuple-element.66.queries.keys.values.refs_0_.refs_1_.refs_2_, ...), custom_call_target="tpu_custom_call" | custom-call | flops 6442450944 | bytes 11010048 | tf_op jit(solution)/shard_map/pallas_call | solution.py:1204
  656.9 16.7 shard_map.525
  692.2 16.2 fusion.144
  708.5 19.3 %multiply_convert_fusion.2 = (bf16[1024,3072]{1,0:T(8,128)(2,1)S(1)}, f32[1024,3072]{1,0:T(8,128)}) fusion(f32[1024,3072]{1,0:T(8,128)} %fusion.144, bf16[1024,1536]{1,0:T(8,128)(2,1)} %copy-done.36, bf16[1536,3072]{1,0:T(8,128)(2,1)} %bitcast.236), kind=kOutput, calls=%fused_computation.10 | convolution fusion | flops 9682550784 | bytes 44040192 | tf_op jit(solution)/shard_map/dot_general | solution.py:1650
  727.8 15.9 convolution_convert_fusion.3
  756.3 7.7 fusion.18
  786.5 25.3 %multiply_convert_fusion = (bf16[1024,3072]{1,0:T(8,128)(2,1)}, bf16[1024,3072]{1,0:T(8,128)(2,1)}) fusion(f32[1024,3072]{1,0:T(8,128)} %fusion.144, f32[1024,3072]{1,0:T(8,128)} %get-tuple-element.333, bf16[3072,1536]{1,0:T(8,128)(2,1)} %bitcast.241, f32[1024,1536]{1,0:T(8,128)} %fusion.48, f32[1536]{0:T(1024)S(1)} %multiply_multiply_fusion.6), kind=kOutput, calls=%fused_computation.8 | convolution fusion | flops 9707716608 | bytes 53483520 | tf_op jit(solution)/shard_map/dot_general | solution.py:719
  811.8 15.6 fusion.145
  827.4 12.8 convolution_convert_fusion.2
  840.2 12.4 convolution_convert_fusion.1
  852.5 15.0 add_convert_fusion.2
  867.5 15.3 convolution_convert_fusion
  884.1 274.2 %shard_map.530 = (bf16[48,3072]{1,0:T(8,128)(2,1)}, bf16[48,3072]{1,0:T(8,128)(2,1)}, bf16[48,3072]{1,0:T(8,128)(2,1)}, bf16[48,3072]{1,0:T(8,128)(2,1)}, bf16[192,1536]{1,0:T(8,128)(2,1)}) custom-call(bf16[4,2,4,48,3072]{4,3,2,1,0:T(8,128)(2,1)} %bitcast.216, bf16[4,2,4,48,3072]{4,3,2,1,0:T(8,128)(2,1)} %bitcast.217, bf16[4,1,4,192,1536]{4,3,2,1,0:T(8,128)(2,1)} %bitcast.218), custom_call_target="tpu_custom_call" | custom-call | tf_op jit(solution)/shard_map/pallas_call | solution.py:1065
  1166.2 6.3 multiply_reduce_fusion
  1178.8 7.5 fusion.30.refs_7_
  1186.3 17.8 %shard_map.526 = (bf16[1024,768]{1,0:T(8,128)(2,1)S(1)}, f32[128,768]{1,0:T(8,128)S(1)}, f32[128,768]{1,0:T(8,128)S(1)}) custom-call(bf16[1024,768]{1,0:T(8,128)(2,1)S(1)} %copy-done.6, bf16[128,1536]{1,0:T(8,128)(2,1)S(1)} %convolution_convert_fusion.11.keys.values.refs_1_.refs_2_, ...), custom_call_target="tpu_custom_call" | custom-call | flops 2013265920 | bytes 13369344 | tf_op jit(solution)/shard_map/pallas_call | solution.py:1329
  1232.9 46.0 %shard_map.527 = (bf16[1024,768]{1,0:T(8,128)(2,1)S(1)}, bf16[1024,768]{1,0:T(8,128)(2,1)S(1)}, bf16[1024,768]{1,0:T(8,128)(2,1)S(1)}, f32[8,768]{1,0:T(8,128)S(1)}, f32[8,768]{1,0:T(8,128)S(1)}) custom-call(bf16[1024,2304]{1,0:T(8,128)(2,1)} %get-tuple-element.66.queries.keys.values.refs_0_.refs_1_.refs_2_, ...), custom_call_target="tpu_custom_call" | custom-call | flops 16106127360 | bytes 18874368 | tf_op jit(solution)/shard_map/pallas_call | solution.py:1329
  1281.7 8.6 add_convert_fusion
  1290.3 32.2 %maximum_maximum_fusion.left.right = bf16[1536,3072]{1,0:T(8,128)(2,1)} fusion(bf16[768,768]{1,0:T(8,128)(2,1)S(1)} %get-tuple-element.268, bf16[768,768]{1,0:T(8,128)(2,1)S(1)} %get-tuple-element.267, bf16[1536,2304]{1,0:T(8,128)(2,1)S(1)} %add_convert_fusion), kind=kLoop, calls=%fused_computation.16 | loop fusion | flops 28311552 | bytes 18874368 | tf_op jit(solution)/shard_map/concatenate | solution.py:1795
  1322.5 90.3 %shard_map.528 = bf16[128,192,384]{2,1,0:T(8,128)(2,1)} custom-call(s32[128]{0:T(128)} %slice.258.left_at, s32[128]{0:T(128)} %slice.259.right_at, s32[128]{0:T(128)} %slice.260.left_half, s32[128]{0:T(128)} %slice.261.right_half, bf16[1536,3072]{1,0:T(8,128)(2,1)} %maximum_maximum_fusion.left.right, bf16[1536,3072]{1,0:T(8,128)(2,1)} %maximum_maximum_fusion.left.right, ...), custom_call_target="tpu_custom_call" | custom-call | flops 7247757312 | bytes 56623104 | tf_op jit(solution)/shard_map/pallas_call | solution.py:1371
  1412.9 15.0 fusion.136
  1436.2 12.5 convolution_convert_fusion.4
  1453.4 6.5 convolution_convert_fusion.9
  1472.0 6.3 multiply_reduce_fusion.3
  1479.2 8.0 fusion.26
  1489.5 11.9 fusion.refs_0_
  1501.5 184.3 %shard_map.529 = (bf16[768,384]{1,0:T(8,128)(2,1)}, bf16[48,768]{1,0:T(8,128)(2,1)}, bf16[48,768]{1,0:T(8,128)(2,1)}, bf16[48,1536]{1,0:T(8,128)(2,1)}, bf16[16,...) custom-call(bf16[4,1,4,768,384]{4,3,2,1,0:T(8,128)(2,1)} %fusion.ref, ...), custom_call_target="tpu_custom_call" | custom-call | tf_op jit(solution)/shard_map/pallas_call | solution.py:1065
  (649 shorter events, 308.6 us)
Async XLA Ops:
  0.7 1731.2 %copy-start = (f32[8,192,192]{2,1,0:T(8,128)S(1)}, f32[8,192,192]{2,1,0:T(8,128)}, u32[]{:S(2)}) copy-start(f32[8,192,192]{2,1,0:T(8,128)} %param.65) | copy-start | bytes 3538948
  3.6 526.4 %collective-permute-start = (s32[2,17]{1,0:T(2,128)}, s32[2,17]{1,0:T(2,128)}, u32[]{:S(2)}, u32[]{:S(2)}) collective-permute-start(s32[2,17]{1,0:T(2,128)} %pad_add_fusion.3), channel_id=1, source_target_pairs={{0,4},{4,0},{1,5},{5,1},{2,6},{6,2},{3,7},{7,3},{8,12},{12,8},{9,1... | collective-permute-start | bytes 416 | tf_op jit(solution)/shard_map/ppermute | solution.py:677
  7.2 538.5 %collective-permute-start.3 = (f32[2,256,128]{1,2,0:T(8,128)}, f32[2,256,128]{1,2,0:T(8,128)}, u32[]{:S(2)}, u32[]{:S(2)}) collective-permute-start(f32[2,256,128]{1,2,0:T(8,128)} %constant_dynamic-update-slice_fusion), channel_id=1, source_target_pairs={{0,4},{4,0},{1,5},{5,1},{2,6},{6,2},{3,7},{7,3},{8,12},{12,8},{9,1... | collective-permute-start | bytes 786440 | tf_op jit(solution)/shard_map/ppermute | solution.py:677
  38.0 430.4 %copy-start.128 = (f32[32]{0:T(128)S(1)}, f32[32]{0:T(128)}, u32[]{:S(2)}) copy-start(f32[32]{0:T(128)} %multiply_exponential_fusion) | copy-start | bytes 388
  530.7 3.6 collective-permute-start.1
  535.1 3.6 collective-permute-start.2
  547.0 11.1 collective-permute-start.4
  555.0 8.2 collective-permute-start.5
  555.0 8.2 collective-permute-start.6
  626.1 17.7 %collective-permute-start.7 = (bf16[1024,1536]{1,0:T(8,128)(2,1)}, bf16[1024,1536]{1,0:T(8,128)(2,1)}, u32[]{:S(2)}, u32[]{:S(2)}) collective-permute-start(bf16[1024,1536]{1,0:T(8,128)(2,1)} %convolution_convert_fusion.7), channel_id=1, source_target_pairs={{0,4},{4,0},{1,5},{5,1},{2,6},{6,2},{3,7},{7,3},{8,12},{12,8},{9,1... | collective-permute-start | bytes 9437192 | tf_op jit(solution)/shard_map/ppermute | solution.py:677
  626.2 7.0 collective-permute-start.8
  633.3 6.5 collective-permute-start.11
  634.9 6.8 collective-permute-start.10
  636.8 4.9 collective-permute-start.9
  678.8 5.9 collective-permute-start.12
  743.7 12.6 collective-permute-start.13
  755.1 1.3 collective-permute-start.14
  764.1 3.8 collective-permute-start.15
  767.9 4.8 collective-permute-start.16
  772.7 5.7 collective-permute-start.17
  778.5 4.7 collective-permute-start.18
  867.5 298.7 %collective-permute-start.19 = (bf16[1024,1536]{1,0:T(8,128)(2,1)}, bf16[1024,1536]{1,0:T(8,128)(2,1)}, u32[]{:S(2)}, u32[]{:S(2)}) collective-permute-start(bf16[1024,1536]{1,0:T(8,128)(2,1)} %add_convert_fusion.2), channel_id=1, source_target_pairs={{0,4},{4,0},{1,5},{5,1},{2,6},{6,2},{3,7},{7,3},{8,12},{12,8},{9,1... | collective-permute-start | bytes 9437192 | tf_op jit(solution)/shard_map/ppermute | solution.py:677
  1209.6 7.6 collective-permute-start.20
  1427.8 61.7 %collective-permute-start.21 = (bf16[4,1,4,768,384]{4,3,2,1,0:T(8,128)(2,1)}, bf16[4,1,4,768,384]{4,3,2,1,0:T(8,128)(2,1)}, u32[]{:S(2)}, u32[]{:S(2)}) collective-permute-start(bf16[4,1,4,768,384]{4,3,2,1,0:T(8,128)(2,1)} %bitcast.42), channel_id=1, source_target_pairs={{0,4},{4,0},{1,5},{5,1},{2,6},{6,2},{3,7},{7,3},{8,12},{12,8},{9,1... | collective-permute-start | bytes 28311560 | tf_op jit(solution)/shard_map/ppermute | solution.py:677
  1435.8 24.1 %collective-permute-start.22 = (bf16[2,192,1536]{2,1,0:T(8,128)(2,1)}, bf16[2,192,1536]{2,1,0:T(8,128)(2,1)}, u32[]{:S(2)}, u32[]{:S(2)}) collective-permute-start(bf16[2,192,1536]{2,1,0:T(8,128)(2,1)} %get-tuple-element.266), channel_id=1, source_target_pairs={{0,4},{4,0},{1,5},{5,1},{2,6},{6,2},{3,7},{7,3},{8,12},{12,8},{9,1... | collective-permute-start | bytes 3538952 | tf_op jit(solution)/shard_map/ppermute | solution.py:677
  1448.7 23.3 %collective-permute-start.23 = (bf16[1024,1536]{1,0:T(8,128)(2,1)}, bf16[1024,1536]{1,0:T(8,128)(2,1)}, u32[]{:S(2)}, u32[]{:S(2)}) collective-permute-start(bf16[1024,1536]{1,0:T(8,128)(2,1)} %convolution_convert_fusion.4), channel_id=1, source_target_pairs={{0,4},{4,0},{1,5},{5,1},{2,6},{6,2},{3,7},{7,3},{8,12},{12,8},{9,1... | collective-permute-start | bytes 9437192 | tf_op jit(solution)/shard_map/ppermute | solution.py:677
  1467.6 2.3 collective-permute-start.24
  1704.2 1.1 collective-permute-start.25
  1705.4 3.5 collective-permute-start.26
  1709.1 4.4 collective-permute-start.27
  1713.5 3.5 collective-permute-start.28
  1717.1 3.5 collective-permute-start.29
  (142 other events, 2219.4 us)

commit v3 on v2

--- a/solution.py
+++ b/solution.py
@@ -720,7 +720,7 @@
 
 
 MESH_ID = pl.DeviceIdType.MESH
-TILE = 256
+JOIN_TILE = 512
 
 
 def anywhere(count):
@@ -1090,7 +1090,7 @@
     is_turned = pl.program_id(0) < 6
 
     def body(step, carry):
-        at = pl.ds(pl.multiple_of(step * TILE, TILE), TILE)
+        at = pl.ds(pl.multiple_of(step * JOIN_TILE, JOIN_TILE), JOIN_TILE)
         values = jnp.dot(rows[at, :], weights[...], preferred_element_type=jnp.float32)
 
         @pl.when(is_turned)
@@ -1106,7 +1106,7 @@
 
         return carry
 
-    lax.fori_loop(0, rows.shape[0] // TILE, body, 0)
+    lax.fori_loop(0, rows.shape[0] // JOIN_TILE, body, 0)
     joined_time[...] = jnp.dot(
         times[...], weights[...], preferred_element_type=jnp.float32
     ).astype(joined_time.dtype)
@@ -1150,8 +1150,10 @@
 
 
 def attend_kernel(timed, queries, keys, values, first, second, mixed, logsum):
+    tile = 256 if timed else 512
+
     def body(step, carry):
-        at = pl.ds(pl.multiple_of(step * TILE, TILE), TILE)
+        at = pl.ds(pl.multiple_of(step * tile, tile), tile)
         rows = queries[at, :]
         total = jnp.zeros(rows.shape, jnp.float32)
         sums = jnp.zeros(rows.shape, jnp.float32)
@@ -1187,7 +1189,7 @@
         logsum[at, :] = sums
         return carry
 
-    lax.fori_loop(0, queries.shape[0] // TILE, body, 0)
+    lax.fori_loop(0, queries.shape[0] // tile, body, 0)
 
 
 def lane_block(array, offset):
@@ -1236,8 +1238,10 @@
         out_first[...] = jnp.zeros_like(out_first)
         out_second[...] = jnp.zeros_like(out_second)
 
+    tile = 256 if timed else 512
+
     def body(step, carry):
-        at = pl.ds(pl.multiple_of(step * TILE, TILE), TILE)
+        at = pl.ds(pl.multiple_of(step * tile, tile), tile)
         rows, grad = queries[at, :], gradient[at, :]
         product = grad.astype(jnp.float32) * mixed[at, :].astype(jnp.float32)
         sums = logsum[at, :]
@@ -1287,7 +1291,7 @@
         out_q[at, :] = grad_query.astype(out_q.dtype)
         return carry
 
-    lax.fori_loop(0, queries.shape[0] // TILE, body, 0)
+    lax.fori_loop(0, queries.shape[0] // tile, body, 0)
     grad_key = sum_k[...] * SCORE_SCALE
     if timed:
         grad_key = turned(grad_key, cosine[...], -sine[...])
@@ -1342,87 +1346,109 @@
     )(*operands)
 
 
-def lane_moves():
-    source = lax.broadcasted_iota(jnp.int32, (6, 2 * BLK, 2 * BLK), 1)
-    target = lax.broadcasted_iota(jnp.int32, (6, 2 * BLK, 2 * BLK), 2)
-    code = lax.broadcasted_iota(jnp.int32, (6, 2 * BLK, 2 * BLK), 0)
-    to_right, taken = code // 3, code % 3
-    moves = (target // BLK == to_right) & (taken < 2)
-    moves = moves & (source == target + (taken - to_right) * BLK)
-    return moves.astype(jnp.bfloat16)
-
-
-def pair_kernel(left_at, right_at, left_half, right_half, left, right, moves, target):
+def shifted(tile, is_shifted):
+    wide = tile.astype(jnp.float32)
+    return jnp.where(is_shifted, pltpu.roll(wide, BLK, 1), wide)
+
+
+def assemble_kernel(joined_at, mix_at, pairs, joined, mix):
     step = pl.program_id(0)
-    tile_shape = (BLK, 2 * BLK)
-    total = jnp.dot(
-        left[...].reshape(tile_shape), moves[left_half[step]], preferred_element_type=jnp.float32
-    )
-    total = total + jnp.dot(
-        right[...].reshape(tile_shape),
-        moves[3 + right_half[step]],
-        preferred_element_type=jnp.float32,
-    )
-    target[...] = total.astype(target.dtype).reshape(target.shape)
-
-
-def pair_up(blocks, places, halves, moves, source_spec, target_spec, shape):
-    steps = places.shape[0] // 2
+    lane = lax.broadcasted_iota(jnp.int32, (BLK, 2 * BLK), 1)
+
+    def fill(places, target, count):
+        for pair in range(count):
+            first = (step * count + pair) * 2
+            left, right = places[first], places[first + 1]
+            tile = jnp.where(
+                lane < BLK,
+                shifted(pairs[left // 2], left % 2 == 1),
+                shifted(pairs[right // 2], right % 2 == 0),
+            )
+            target[:, pair * 2 * BLK : (pair + 1) * 2 * BLK] = tile.astype(target.dtype)
+
+    fill(joined_at, joined, 6)
+    fill(mix_at, mix, 2)
+
+
+def assemble(pairs, joined_at, mix_at):
+    half = D // 2
     return pl.pallas_call(
-        pair_kernel,
+        assemble_kernel,
         grid_spec=pltpu.PrefetchScalarGridSpec(
-            num_scalar_prefetch=4,
+            num_scalar_prefetch=2,
+            grid=(8,),
+            in_specs=[
+                pl.BlockSpec(
+                    pairs.shape, lambda step, *_: (0, 0, 0), pipeline_mode=pl.Buffered(1)
+                )
+            ],
+            out_specs=[
+                pl.BlockSpec((BLK, 3 * half), lambda step, *_: (step, 0)),
+                pl.BlockSpec((BLK, half), lambda step, *_: (step // 2, step % 2)),
+            ],
+        ),
+        out_shape=[
+            jax.ShapeDtypeStruct((D, 3 * half), pairs.dtype),
+            jax.ShapeDtypeStruct((half, D), pairs.dtype),
+        ],
+        compiler_params=pltpu.CompilerParams(vmem_limit_bytes=48 * 2**20),
+        cost_estimate=pl.CostEstimate(
+            flops=0, bytes_accessed=2 * pairs.size + 8 * half * D, transcendentals=0
+        ),
+    )(joined_at, mix_at, pairs)
+
+
+SLOTS_STEP = 8
+
+
+def collect_kernel(rows_at, columns_at, sides, joined, mix, target):
+    step = pl.program_id(0)
+    lane = lax.broadcasted_iota(jnp.int32, (BLK, 2 * BLK), 1)
+    target[...] = jnp.zeros_like(target)
+    for inner in range(SLOTS_STEP):
+        slot, pair, right = step * SLOTS_STEP + inner, inner // 2, inner % 2
+        code = sides[slot]
+        rows = pl.ds(pl.multiple_of(rows_at[slot] * BLK, BLK), BLK)
+        columns = pl.ds(pl.multiple_of(columns_at[slot] * 2 * BLK, 128), 2 * BLK)
+
+        def put(source):
+            tile = shifted(source[rows, columns], code % 2 != right).astype(target.dtype)
+            own = lane // BLK == right
+            target[pair] = jnp.where(own, tile, target[pair])
+
+        @pl.when(code // 2 == 0)
+        def from_joined():
+            put(joined)
+
+        @pl.when(code // 2 == 1)
+        def from_mix():
+            put(mix)
+
+
+def collect(joined, mix, rows_at, columns_at, sides):
+    steps = sides.shape[0] // SLOTS_STEP
+
+    def resident(array):
+        return pl.BlockSpec(array.shape, lambda step, *_: (0, 0), pipeline_mode=pl.Buffered(1))
+
+    return pl.pallas_call(
+        collect_kernel,
+        grid_spec=pltpu.PrefetchScalarGridSpec(
+            num_scalar_prefetch=3,
             grid=(steps,),
-            in_specs=[
-                source_spec(lambda step, a, b, c, d: a[step]),
-                source_spec(lambda step, a, b, c, d: b[step]),
-                pl.BlockSpec(moves.shape, lambda step, a, b, c, d: (0, 0, 0)),
-            ],
-            out_specs=target_spec,
+            in_specs=[resident(joined), resident(mix)],
+            out_specs=pl.BlockSpec(
+                (SLOTS_STEP // 2, BLK, 2 * BLK), lambda step, *_: (step, 0, 0)
+            ),
         ),
-        out_shape=jax.ShapeDtypeStruct(shape, blocks.dtype),
+        out_shape=jax.ShapeDtypeStruct((sides.shape[0] // 2, BLK, 2 * BLK), joined.dtype),
+        compiler_params=pltpu.CompilerParams(vmem_limit_bytes=48 * 2**20),
         cost_estimate=pl.CostEstimate(
-            flops=8 * steps * BLK**3, bytes_accessed=12 * steps * BLK * BLK, transcendentals=0
+            flops=0,
+            bytes_accessed=2 * (joined.size + mix.size) + 2 * sides.shape[0] * BLK * BLK,
+            transcendentals=0,
         ),
-    )(places[0::2], places[1::2], halves[0::2], halves[1::2], blocks, blocks, moves)
-
-
-def stacked_spec(where):
-    return pl.BlockSpec((1, BLK, 2 * BLK), lambda *at: (where(*at), 0, 0))
-
-
-def tiled_spec(across):
-    def spec(where):
-        return pl.BlockSpec(
-            (BLK, 2 * BLK), lambda *at: (where(*at) // across, where(*at) % across)
-        )
-
-    return spec
-
-
-def assemble(pairs, slots, moves, rows, columns):
-    across = columns // (2 * BLK)
-    return pair_up(
-        pairs,
-        slots // 2,
-        slots % 2,
-        moves,
-        stacked_spec,
-        pl.BlockSpec((BLK, 2 * BLK), lambda step, *_: (step // across, step % across)),
-        (rows, columns),
-    )
-
-
-def collect(matrix, places, halves, moves):
-    return pair_up(
-        matrix,
-        places,
-        halves,
-        moves,
-        tiled_spec(matrix.shape[1] // (2 * BLK)),
-        pl.BlockSpec((1, BLK, 2 * BLK), lambda step, *_: (step, 0, 0)),
-        (places.shape[0] // 2, BLK, 2 * BLK),
-    )
+    )(rows_at, columns_at, sides, joined, mix)
 
 
 def item_per_chip(
@@ -1502,6 +1528,20 @@
     def kv_block(which, side):
         return head_columns(low_kv, which, side).reshape(16, 1152)
 
+    def gathered(block):
+        return lax.all_gather(block, ("y", "x", "z"), axis=0)
+
+    feed_blocks = []
+    for which in range(2):
+        kept, received = unit_columns(which, core), swap(unit_columns(which, 1 - core), "c")
+        feed_blocks.append(
+            jnp.where(core == 0, jnp.stack([kept, received]), jnp.stack([received, kept]))
+        )
+    gate_weight, up_weight = (
+        gathered(block).reshape(4, 4, 2, 48, FF // 2).transpose(0, 2, 1, 3, 4).reshape(D, FF // 2)
+        for block in feed_blocks
+    )
+    down = gathered(low_down).reshape(FF // 2, D)
     arrays = (
         ("cols", (16, D), bf16),
         ("both", (4 * BLK, 2 * BLK), bf16),
@@ -1509,48 +1549,34 @@
         ("half", (48, D), bf16),
         ("cols", (16, 1152), bf16),
         ("cols", (16, 1152), bf16),
-        ("cols", (48, FF // 2), bf16),
-        ("cols", (48, FF // 2), bf16),
-        ("one", (192, D), bf16),
     )
     whole = slice(None)
     groups = [((0, 0, whole, whole), (5, 1, whole, whole))]
     groups += [
-        ((1, 0, pl.ds(step * 192, 192), whole), (1, 1, pl.ds(384 + step * 192, 192), whole))
-        for step in range(2)
-    ]
-    groups += [((2, 0, whole, whole), (3, 1, whole, whole), (4, 0, whole, whole))]
-    groups += [
-        ((6, 0, whole, pl.ds(step * 768, 768)), (7, 1, whole, pl.ds(step * 768, 768)))
+        ((1, 0, pl.ds(step * 96, 96), whole), (1, 1, pl.ds(384 + step * 96, 96), whole))
         for step in range(4)
     ]
     groups += [
-        ((8, 0, whole, pl.ds(step * 384, 384)), (8, 1, whole, pl.ds(half + step * 384, 384)))
+        ((2, 0, whole, pl.ds(step * 384, 384)), (3, 1, whole, pl.ds(step * 768, 768)))
         for step in range(2)
     ]
-    packs, all_pairs, cross_query, cross_out, keys_own, values_own, gate_weight, up_weight, down = (
-        gather_weights(
-            arrays,
-            groups,
-            (
-                pack,
-                pack,
-                low_pairs,
-                head_columns(low_cross[:, 0, :], 0, core),
-                head_columns(low_cross[:, 0, :], 0, 1 - core),
-                low_cross[:, 1, :],
-                kv_block(0, core),
-                kv_block(0, 1 - core),
-                kv_block(1, core),
-                kv_block(1, 1 - core),
-                unit_columns(0, core),
-                unit_columns(0, 1 - core),
-                unit_columns(1, core),
-                unit_columns(1, 1 - core),
-                low_down,
-            ),
-            1,
-        )
+    groups += [((4, 0, whole, whole),)]
+    packs, all_pairs, cross_query, cross_out, keys_own, values_own = gather_weights(
+        arrays,
+        groups,
+        (
+            pack,
+            pack,
+            low_pairs,
+            head_columns(low_cross[:, 0, :], 0, core),
+            head_columns(low_cross[:, 0, :], 0, 1 - core),
+            low_cross[:, 1, :],
+            kv_block(0, core),
+            kv_block(0, 1 - core),
+            kv_block(1, core),
+            kv_block(1, 1 - core),
+        ),
+        1,
     )
     packs = packs.reshape(32, 16, D)
     ends_full = packs[:, :4].reshape(D, 2, DIN)
@@ -1574,16 +1600,14 @@
         (4 * core + four)[None, None, :],
     )
     out_blocks = grid_blocks(3, (4 * core + four)[:, None], eight[None, :])
-    moves = lane_moves()
-    projection = assemble(all_pairs, inverse_order[joined_blocks], moves, D, 3 * half)
-    weight_mix = assemble(all_pairs, inverse_order[out_blocks], moves, half, D)
+    projection, weight_mix = assemble(
+        all_pairs, inverse_order[joined_blocks], inverse_order[out_blocks]
+    )
     cross_query = cross_query.reshape(D, half)
     cross_out = lax.dynamic_slice_in_dim(cross_out.reshape(D, D), core * half, half, 0)
     kv_own = jnp.concatenate(
         [keys_own.reshape(DT, half), values_own.reshape(DT, half)], 1
     )
-    gate_weight, up_weight = gate_weight.reshape(D, FF // 2), up_weight.reshape(D, FF // 2)
-    down = down.reshape(FF // 2, D)
 
     meta = jnp.concatenate([timesteps[:, None], text_lengths[:, None], negatives], 1)
     metas = meta
@@ -1708,33 +1732,27 @@
     grad_up = (grad_hidden * silu_value).astype(bf16)
     grad_gate_weight = tdot(input_three, grad_gate).astype(bf16)
     grad_up_weight = tdot(input_three, grad_up).astype(bf16)
-    feed_arrays = (("cols", (48, FF // 2)), ("cols", (48, FF // 2)), ("one", (192, D)))
-    feed_groups = [
-        ((2, 0, whole, pl.ds(step * 384, 384)), (2, 1, whole, pl.ds(half + step * 384, 384)))
-        for step in range(2)
-    ]
-    feed_groups += [
-        ((0, 0, whole, pl.ds(step * 768, 768)), (1, 1, whole, pl.ds(step * 768, 768)))
-        for step in range(4)
-    ]
-    feed_sums = reduce_gradients(
-        feed_arrays,
-        feed_groups,
-        (
-            grad_gate_weight.reshape(4, 2, 4, 48, FF // 2),
-            grad_up_weight.reshape(4, 2, 4, 48, FF // 2),
-            grad_down.reshape(4, 1, 4, 192, D),
-        ),
-        2,
-    )
+    def scattered(gradient, width):
+        total = lax.psum_scatter(
+            gradient.reshape(4, -1, 4, width, gradient.shape[1]),
+            ("y", "x"),
+            scatter_dimension=0,
+            tiled=True,
+        )
+        return lax.psum_scatter(total, "z", scatter_dimension=2, tiled=True)[0, :, 0]
+
+    feed_sums = []
+    for gradient in (grad_gate_weight, grad_up_weight):
+        both_rows = scattered(gradient, 48)
+        feed_sums.append((pick(both_rows, core), swap(pick(both_rows, 1 - core), "c")))
     gate_columns = []
-    for mine, other in ((feed_sums[0], feed_sums[1]), (feed_sums[2], feed_sums[3])):
+    for mine, other in feed_sums:
         sides = (jnp.where(core == 0, mine, other), jnp.where(core == 0, other, mine))
         for quadrant in quads:
             for side in sides:
                 gate_columns.append(side[:, quadrant * 768 : (quadrant + 1) * 768])
     grad_gate_up = jnp.concatenate(gate_columns, 1).astype(f32)
-    grad_down = feed_sums[4].astype(f32)
+    grad_down = scattered(grad_down, 192)[0].astype(f32)
     grad_input_three = on_both(dot_back(grad_gate, gate_weight) + dot_back(grad_up, up_weight))
     grad_after_cross, gain_three = layer_back(
         grad_input_three, normed_three, inverse_three, gain_values[:, 2]
@@ -1792,10 +1810,6 @@
     grad_projection = (
         tdot(input_one, grad_joined) + input_time.astype(f32).reshape(D, 1) * time_row
     ).astype(bf16)
-    grad_squares = jnp.concatenate(
-        [grad_projection, jnp.concatenate([grad_mix[:, :half], grad_mix[:, half:]], 0)], 1
-    )
-
     position = jnp.arange(256, dtype=jnp.int32)
     owner_core = core ^ (position // 128)
     block = assignment[
@@ -1803,15 +1817,14 @@
     ]
     matrix, block_row, block_column = block // 64, (block // 8) % 8, block % 8
     is_out = matrix == 3
-    out_pair = block_column // 2
-    tile_row = jnp.where(is_out, block_row % 4 + 4 * (out_pair // 2), block_row)
-    tile_column = jnp.where(is_out, 6 + out_pair % 2, matrix * 2 + (block_column % 4) // 2)
-    held = jnp.where(is_out, block_row // 4, block_column // 4) == core
+    side = jnp.where(is_out, block_row // 4, block_column // 4)
+    code = jnp.where(side == core, 2 * is_out + block_column % 2, 4)
     collected = collect(
-        grad_squares,
-        jnp.where(held, tile_row * 8 + tile_column, 0),
-        jnp.where(held, block_column % 2, 2),
-        moves,
+        grad_projection,
+        grad_mix,
+        jnp.where(is_out, block_row % 4, block_row),
+        jnp.where(is_out, block_column // 2, matrix * 2 + (block_column % 4) // 2),
+        code.astype(jnp.int32),
     ).reshape(2, 4, 1, 4, 4 * BLK, 2 * BLK)
     slot_sums = low_sum(collected[0], swap(collected[1], "c")).astype(bf16)
 
@@ -1853,12 +1866,14 @@
         ("cols", (16, 1152)),
         ("one", (16, D)),
     )
-    rest_groups = [
-        ((1, 0, whole, whole), (2, 1, whole, whole), (3, 0, whole, whole), (4, 1, whole, whole))
+    rest_groups = [((3, 0, whole, whole), (4, 1, whole, whole))]
+    rest_groups += [
+        ((1, 0, whole, pl.ds(step * 384, 384)), (2, 1, whole, pl.ds(step * 768, 768)))
+        for step in range(2)
     ]
     rest_groups += [
-        ((0, 0, pl.ds(step * 192, 192), whole), (0, 1, pl.ds(384 + step * 192, 192), whole))
-        for step in range(2)
+        ((0, 0, pl.ds(step * 96, 96), whole), (0, 1, pl.ds(384 + step * 96, 96), whole))
+        for step in range(4)
     ]
     rest_groups += [((5, 0, whole, whole),)]
     rest_sums = reduce_gradients(
@@ -1872,7 +1887,7 @@
             kv_sources[1],
             small.astype(bf16).reshape(4, 1, 4, 16, D),
         ),
-        3,
+        2,
     )
     slot_rows, query_mine, query_other, grad_cross_out, *kv_sums, small = (
         value.astype(f32) for value in rest_sums

time: 1780 us -> 1300 us (0.73)
  Pallas kernels: 1160 us -> 634 us
  waiting for transfers between devices: 34.7 us -> 84 us
  other arithmetic: 162 us -> 133 us
    pallas_call x2 -> x1, Pallas kernels: 458 us -> 219 us  [reduce_gradients(): pl.pallas_call(partial(reduce_kernel, arrays, groups), out_shape=out_shap...]
    pallas_call x1, Pallas kernels: 426 us -> 248 us  [gather_weights(): pl.pallas_call(partial(gather_kernel, arrays, groups), out_shape=[jax.Sha...]
    pallas_call x3 -> x2, Pallas kernels: 141 us -> 47.5 us  [the longest x1 31.7 us: collect(): pl.pallas_call(collect_kernel, grid_spec=pltpu.PrefetchScalarGridSpec(num...]
    reduce_scatter x0 -> x1, waiting for transfers between devices: none -> 38.7 us  [scattered(): lax.psum_scatter(total, 'z', scatter_dimension=2, tiled=True)[0, :, 0]]
    concatenate x1 -> x0, other arithmetic: 32.2 us -> none  [item_per_chip(): jnp.concatenate([grad_projection, jnp.concatenate([grad_mix[:, :half], gr...]
    ppermute x30 -> x34, waiting for transfers between devices: 34.7 us -> 45.1 us  [swap(): lax.ppermute(values, axis, [(i, i ^ bit) for i in range(lax.axis_size(axi...]
  transfers between devices with their start and end apart: 30 -> 42, of which waited for: 15 -> 20; matrix products, arithmetic and copies ran while one was open for 10% -> 29% of each run, Pallas kernels for 43% -> 49%
where the time goes in v3:
time: 1300 us; the launch traced here: 1290 us
  Pallas kernels  634 us (49%)
  matrix products  261 us (20%)
  other arithmetic  133 us (10%)
  local copies, waits for them, and re-layouts  112 us (9%)
  waiting for transfers between devices  84 us (6%)
  starting transfers between devices  33.1 us (3%)
  between operations  30.4 us (2%)
    pallas_call x1, Pallas kernels, gather_weights(): pl.pallas_call(partial(gather_kernel, arrays, groups), out_shape=[jax.Sha...  248 us
    pallas_call x1, Pallas kernels, reduce_gradients(): pl.pallas_call(partial(reduce_kernel, arrays, groups), out_shape=out_shap...  219 us
    dot_general x9, matrix products, dot_back(): lax.dot_general(left, right, (((1,), (1,)), ((), ())), preferred_element_...  84.2 us
    dot_general x11, matrix products, tdot(): lax.dot_general(left, right, (((0,), (0,)), ((), ())), preferred_element_...  83.6 us
    pallas_call x2, Pallas kernels, attend_back(): pl.pallas_call(partial(attend_back_kernel, timed), grid=(pairs,), in_spec...  58.7 us
    ppermute x34, waiting for transfers between devices, swap(): lax.ppermute(values, axis, [(i, i ^ bit) for i in range(lax.axis_size(axi...  45.1 us
    pallas_call x2, Pallas kernels, attend(): pl.pallas_call(partial(attend_kernel, timed), grid=(pairs,), in_specs=[la...  41.2 us
    reduce_scatter x1, waiting for transfers between devices, scattered(): lax.psum_scatter(total, 'z', scatter_dimension=2, tiled=True)[0, :, 0]  38.7 us
  transfers between devices with their start and end apart: 42, of which 20 were waited for; matrix products, arithmetic and copies ran while one was open for 29% of the time, Pallas kernels for 49%

profile of v3, /device:TPU:0, one launch (start us, length us, event | category | flops | bytes accessed | tf_op | source)
XLA Modules:
  0.0 1286.5 jit_solution(7102781325689080287)
XLA Ops:
  29.9 248.4 %shard_map.520 = (bf16[4,2,4,16,1536]{4,3,2,1,0:T(8,128)(2,1)}, bf16[4,2,4,768,384]{4,3,2,1,0:T(8,128)(2,1)}, bf16[4,2,4,48,768]{4,3,2,1,0:T(8,128)(2,1)}, bf16[...) custom-call(bf16[16,1536]{1,0:T(8,128)(2,1)} %fusion.63.refs_0_.refs_1_, ...), custom_call_target="tpu_custom_call" | custom-call | tf_op jit(solution)/shard_map/pallas_call | solution.py:872
  297.2 15.7 %shard_map.521 = (bf16[1536,2304]{1,0:T(8,128)(2,1)}, bf16[768,1536]{1,0:T(8,128)(2,1)S(1)}) custom-call(s32[96]{0:T(128)S(1)} %gather_fusion.1, s32[32]{0:T(128)S(1)} %gather_fusion.2, bf16[128,192,384]{2,1,0:T(8,128)(2,1)} %bitcast.264), custom_call_target="tpu_custom_call" | custom-call | bytes 28311552 | tf_op jit(solution)/shard_map/pallas_call | solution.py:1375
  333.6 10.5 collective-permute-done.5
  348.7 19.1 %shard_map.522 = (bf16[1024,2304]{1,0:T(8,128)(2,1)}, bf16[16,2304]{1,0:T(8,128)(2,1)S(1)}) custom-call(bf16[1024,1536]{1,0:T(8,128)(2,1)S(1)} %multiply_convert_fusion.5.rows, bf16[16,1536]{1,0:T(8,128)(2,1)S(1)} %pad.15.times, bf16[1536,2304]{1,0:T(8,128)(2,1)} %get-tuple-element.60.weights, f32[1024,128]{1,0:T(8,128)S(1)} %pad_maximum_fusion.7.cosine.refs_8_, ...), custom_call_target="tpu_custom_call" | custom-call | flops 7247757312 | bytes 14942208 | tf_op jit(solution)/shard_map/pallas_call | solution.py:1121
  367.9 31.0 %shard_map.523 = (bf16[1024,768]{1,0:T(8,128)(2,1)S(1)}, f32[1024,768]{1,0:T(8,128)S(1)}) custom-call(bf16[1024,2304]{1,0:T(8,128)(2,1)} %get-tuple-element.61.queries.keys.values.refs_0_.refs_1_.refs_2_, bf16[1024,2304]{1,0:T(8,128)(2,1)} %get-tuple-element.61.queries.keys.values.refs_0_.refs_1_.refs_2_, ...), custom_call_target="tpu_custom_call" | custom-call | flops 6442450944 | bytes 11010048 | tf_op jit(solution)/shard_map/pallas_call | solution.py:1206
  409.9 9.7 collective-permute-start.10
  441.0 10.1 shard_map.524
  471.2 8.7 copy.258
  479.9 8.7 copy.259
  488.6 17.3 %fusion.130 = f32[1024,3072]{1,0:T(8,128)} fusion(bf16[1024,1536]{1,0:T(8,128)(2,1)} %multiply_convert_fusion.3, bf16[1536,3072]{1,0:T(8,128)(2,1)} %bitcast.270), kind=kOutput, calls=%fused_computation.468 | convolution fusion | flops 9663676416 | bytes 25165824 | tf_op jit(solution)/shard_map/dot_general | solution.py:1673
  505.9 19.4 %multiply_convert_fusion.2 = (bf16[1024,3072]{1,0:T(8,128)(2,1)}, f32[1024,3072]{1,0:T(8,128)}) fusion(f32[1024,3072]{1,0:T(8,128)} %fusion.130, bf16[1024,1536]{1,0:T(8,128)(2,1)S(1)} %copy-done.48, bf16[1536,3072]{1,0:T(8,128)(2,1)} %bitcast.272), kind=kOutput, calls=%fused_computation.10 | convolution fusion | flops 9682550784 | bytes 44040192 | tf_op jit(solution)/shard_map/dot_general | solution.py:1674
  525.4 15.5 %convolution_convert_fusion.3 = bf16[1024,1536]{1,0:T(8,128)(2,1)} fusion(bf16[1024,3072]{1,0:T(8,128)(2,1)} %get-tuple-element.372, bf16[3072,1536]{1,0:T(8,128)(2,1)} %all-gather.9.cloned.1.call-done), kind=kOutput, calls=%fused_computation.50 | convolution fusion | flops 9665249280 | bytes 18874368 | tf_op jit(solution)/shard_map/dot_general | solution.py:1678
  546.9 7.7 fusion.12
  576.3 25.2 %multiply_convert_fusion = (bf16[1024,3072]{1,0:T(8,128)(2,1)}, bf16[1024,3072]{1,0:T(8,128)(2,1)}) fusion(f32[1024,3072]{1,0:T(8,128)} %fusion.130, f32[1024,3072]{1,0:T(8,128)} %get-tuple-element.373, bf16[3072,1536]{1,0:T(8,128)(2,1)} %all-gather.9.cloned.1.call-done, f32[1024,1536]{1,0:T(8,128)} %fusion.43, f32[1536]{0:T(1024)S(1)} %multiply_multiply_fusion.6), kind=kOutput, calls=%fused_computation.8 | convolution fusion | flops 9707716608 | bytes 53483520 | tf_op jit(solution)/shard_map/dot_general | solution.py:719
  601.5 15.3 %convolution_convert_fusion.2 = bf16[1536,3072]{1,0:T(8,128)(2,1)} fusion(bf16[1024,1536]{1,0:T(8,128)(2,1)} %multiply_convert_fusion.3, bf16[1024,3072]{1,0:T(8,128)(2,1)} %get-tuple-element.304), kind=kOutput, calls=%fused_computation.15 | convolution fusion | flops 9668395008 | bytes 18874368 | tf_op jit(solution)/shard_map/dot_general | solution.py:715
  616.8 15.5 %convolution_convert_fusion.1 = bf16[1536,3072]{1,0:T(8,128)(2,1)} fusion(bf16[1024,1536]{1,0:T(8,128)(2,1)} %multiply_convert_fusion.3, bf16[1024,3072]{1,0:T(8,128)(2,1)} %get-tuple-element.303), kind=kOutput, calls=%fused_computation.14 | convolution fusion | flops 9668395008 | bytes 18874368 | tf_op jit(solution)/shard_map/dot_general | solution.py:715
  632.4 15.0 %fusion.131 = f32[1024,1536]{1,0:T(8,128)S(1)} fusion(bf16[1024,3072]{1,0:T(8,128)(2,1)} %get-tuple-element.304, bf16[1536,3072]{1,0:T(8,128)(2,1)} %bitcast.271), kind=kOutput, calls=%fused_computation.469 | convolution fusion | flops 9663676416 | bytes 22020096 | tf_op jit(solution)/shard_map/dot_general | solution.py:719
  647.4 16.0 %add_convert_fusion.2 = bf16[1024,1536]{1,0:T(8,128)(2,1)} fusion(f32[1024,1536]{1,0:T(8,128)S(1)} %fusion.131, bf16[1024,3072]{1,0:T(8,128)(2,1)} %get-tuple-element.303, bf16[1536,3072]{1,0:T(8,128)(2,1)} %bitcast.273), kind=kOutput, calls=%fused_computation.28 | convolution fusion | flops 9666822144 | bytes 25165824 | tf_op jit(solution)/shard_map/dot_general | solution.py:719
  663.5 15.4 %convolution_convert_fusion = bf16[3072,1536]{1,0:T(8,128)(2,1)} fusion(bf16[1024,3072]{1,0:T(8,128)(2,1)} %get-tuple-element.372, f32[1024,1536]{1,0:T(8,128)S(1)} %bitcast.260, f32[1536]{0:T(1024)S(1)} %multiply_multiply_fusion.6), kind=kOutput, calls=%fused_computation.13 | convolution fusion | flops 9671540736 | bytes 22026240 | tf_op jit(solution)/shard_map/dot_general | solution.py:715
  679.6 8.1 multiply_reduce_fusion
  687.8 8.5 multiply_add_fusion.1
  700.7 12.4 shard_map.525
  755.4 46.3 %shard_map.526 = (bf16[1024,768]{1,0:T(8,128)(2,1)S(1)}, bf16[1024,768]{1,0:T(8,128)(2,1)S(1)}, bf16[1024,768]{1,0:T(8,128)(2,1)S(1)}, f32[8,768]{1,0:T(8,128)S(1)}, f32[8,768]{1,0:T(8,128)S(1)}) custom-call(bf16[1024,2304]{1,0:T(8,128)(2,1)} %get-tuple-element.61.queries.keys.values.refs_0_.refs_1_.refs_2_, ...), custom_call_target="tpu_custom_call" | custom-call | flops 16106127360 | bytes 18874368 | tf_op jit(solution)/shard_map/pallas_call | solution.py:1333
  808.7 9.5 add_convert_fusion.joined
  818.3 31.7 %shard_map.527 = bf16[128,192,384]{2,1,0:T(8,128)(2,1)} custom-call(s32[256]{0:T(256)S(1)} %get-tuple-element.367.rows_at, s32[256]{0:T(256)S(1)} %get-tuple-element.366.columns_at, s32[256]{0:T(256)S(1)} %get-tuple-element.300.sides, bf16[1536,2304]{1,0:T(8,128)(2,1)} %add_convert_fusion.joined, bf16[768,1536]{1,0:T(8,128)(2,1)S(1)} %convolution_convert_fusion.10.mix), custom_call_target="tpu_custom_call" | custom-call | bytes 28311552 | tf_op jit(solution)/shard_map/pallas_call | solution.py:1434
  850.0 15.5 %fusion.123 = (bf16[64,192,384]{2,1,0:T(8,128)(2,1)}, bf16[64,192,384]{2,1,0:T(8,128)(2,1)}) fusion(bf16[128,192,384]{2,1,0:T(8,128)(2,1)} %shard_map.527), kind=kLoop, calls=%fused_computation.461 | loop fusion | bytes 37748736 | tf_op jit(solution)/shard_map/slice | solution.py:1829
  871.8 11.4 convolution_convert_fusion.4
  910.5 7.2 multiply_reduce_fusion.3
  927.3 12.0 fusion.refs_0_
  939.3 218.6 %shard_map.528 = (bf16[768,384]{1,0:T(8,128)(2,1)}, bf16[48,768]{1,0:T(8,128)(2,1)}, bf16[48,768]{1,0:T(8,128)(2,1)}, bf16[48,1536]{1,0:T(8,128)(2,1)}, bf16[16,...) custom-call(bf16[4,1,4,768,384]{4,3,2,1,0:T(8,128)(2,1)} %fusion.ref, ...), custom_call_target="tpu_custom_call" | custom-call | tf_op jit(solution)/shard_map/pallas_call | solution.py:1065
  1174.7 38.7 %reduce-scatter.17.cloned.1.call-done = bf16[1,1,1,192,1536]{4,3,2,1,0:T(8,128)(2,1)} async-done(((bf16[1,1,4,192,1536]{4,3,2,1,0:T(8,128)(2,1)}), bf16[1,1,1,192,1536]{4,3,2,1,0:T(8,128)(2,1)}) %reduce-scatter.17.cloned.1.call-update) | async-done | bytes 589840 | tf_op jit(solution)/shard_map/reduce_scatter | solution.py:1742
  1265.2 7.4 multiply_subtract_fusion
  (654 shorter events, 304.2 us)
Async XLA Ops:
  7.2 464.0 %all-gather.5.cloned.1.call-start = ((), (), s32[]{:S(2)}) async-start(), calls=%async_computation.4 | async-start | bytes 10027008 | tf_op jit(solution)/shard_map/all_gather | solution.py:1532
  12.7 467.2 %all-gather.7.cloned.1.call-start = ((), (), s32[]{:S(2)}) async-start(), calls=%async_computation.5 | async-start | bytes 10027008 | tf_op jit(solution)/shard_map/all_gather | solution.py:1532
  16.3 509.1 %all-gather.9.cloned.1.call-start = ((), (), s32[]{:S(2)}) async-start(), calls=%async_computation.7 | async-start | bytes 10027008 | tf_op jit(solution)/shard_map/all_gather | solution.py:1532
  16.6 271.5 %collective-permute-start = (s32[2,17]{1,0:T(2,128)S(1)}, s32[2,17]{1,0:T(2,128)S(1)}, u32[]{:S(2)}, u32[]{:S(2)}) collective-permute-start(s32[2,17]{1,0:T(2,128)S(1)} %pad_add_fusion.3), channel_id=1, source_target_pairs={{0,4},{4,0},{1,5},{5,1},{2,6},{6,2},{3,7},{7,3},{8,12},{12,8},{9,1... | collective-permute-start | bytes 416 | tf_op jit(solution)/shard_map/ppermute | solution.py:677
  20.1 300.8 %collective-permute-start.3 = (f32[2,256,128]{1,2,0:T(8,128)}, f32[2,256,128]{1,2,0:T(8,128)}, u32[]{:S(2)}, u32[]{:S(2)}) collective-permute-start(f32[2,256,128]{1,2,0:T(8,128)} %constant_dynamic-update-slice_fusion), channel_id=1, source_target_pairs={{0,4},{4,0},{1,5},{5,1},{2,6},{6,2},{3,7},{7,3},{8,12},{12,8},{9,1... | collective-permute-start | bytes 786440 | tf_op jit(solution)/shard_map/ppermute | solution.py:677
  22.4 881.2 %reduce-scatter.19.cloned.1.call-start = ((), (), s32[]{:S(2)}) async-start(), calls=%async_computation.8 | async-start | bytes 11796480
  291.9 22.5 %collective-permute-start.2 = (s32[8,17]{1,0:T(8,128)S(1)}, s32[8,17]{1,0:T(8,128)S(1)}, u32[]{:S(2)}, u32[]{:S(2)}) collective-permute-start(s32[8,17]{1,0:T(8,128)S(1)} %pad_add_fusion.1), channel_id=1, source_target_pairs={{0,16},{16,0},{1,17},{17,1},{2,18},{18,2},{3,19},{19,3},{4,20},{20... | collective-permute-start | bytes 1640 | tf_op jit(solution)/shard_map/ppermute | solution.py:677
  322.1 11.5 collective-permute-start.4
  324.7 19.3 %collective-permute-start.5 = (f32[256,128]{0,1:T(8,128)S(1)}, f32[256,128]{0,1:T(8,128)S(1)}, u32[]{:S(2)}, u32[]{:S(2)}) collective-permute-start(f32[256,128]{0,1:T(8,128)S(1)} %get-tuple-element.339), channel_id=1, source_target_pairs={{0,2},{1,3},{2,0},{3,1},{4,6},{5,7},{6,4},{7,5},{8,10},{9,11},{10,... | collective-permute-start | bytes 393224 | tf_op jit(solution)/shard_map/ppermute | solution.py:677
  325.4 18.6 %collective-permute-start.6 = (f32[256,128]{0,1:T(8,128)S(1)}, f32[256,128]{0,1:T(8,128)S(1)}, u32[]{:S(2)}, u32[]{:S(2)}) collective-permute-start(f32[256,128]{0,1:T(8,128)S(1)} %get-tuple-element.340), channel_id=1, source_target_pairs={{0,3},{1,2},{2,1},{3,0},{4,7},{5,6},{6,5},{7,4},{8,11},{9,10},{10,... | collective-permute-start | bytes 393224 | tf_op jit(solution)/shard_map/ppermute | solution.py:677
  403.0 25.0 %collective-permute-start.7 = (bf16[1024,1536]{1,0:T(8,128)(2,1)}, bf16[1024,1536]{1,0:T(8,128)(2,1)}, u32[]{:S(2)}, u32[]{:S(2)}) collective-permute-start(bf16[1024,1536]{1,0:T(8,128)(2,1)} %convolution_convert_fusion.7), channel_id=1, source_target_pairs={{0,4},{4,0},{1,5},{5,1},{2,6},{6,2},{3,7},{7,3},{8,12},{12,8},{9,1... | collective-permute-start | bytes 9437192 | tf_op jit(solution)/shard_map/ppermute | solution.py:677
  403.0 6.8 collective-permute-start.8
  409.9 12.8 collective-permute-start.10
  419.6 6.0 collective-permute-start.11
  421.2 4.6 collective-permute-start.9
  456.3 5.9 collective-permute-start.12
  540.9 6.0 collective-permute-start.15
  558.4 4.8 collective-permute-start.18
  567.7 4.7 collective-permute-start.20
  616.8 286.9 %reduce-scatter.21.cloned.1.call-start = ((), (), s32[]{:S(2)}) async-start(), calls=%async_computation.9 | async-start | bytes 11796480
  632.4 293.7 %reduce-scatter.23.cloned.1.call-start = ((), (), s32[]{:S(2)}) async-start(), calls=%async_computation.10 | async-start | bytes 11796480
  663.5 15.5 %collective-permute-start.21 = (bf16[1024,1536]{1,0:T(8,128)(2,1)}, bf16[1024,1536]{1,0:T(8,128)(2,1)}, u32[]{:S(2)}, u32[]{:S(2)}) collective-permute-start(bf16[1024,1536]{1,0:T(8,128)(2,1)} %add_convert_fusion.2), channel_id=1, source_target_pairs={{0,4},{4,0},{1,5},{5,1},{2,6},{6,2},{3,7},{7,3},{8,12},{12,8},{9,1... | collective-permute-start | bytes 9437192 | tf_op jit(solution)/shard_map/ppermute | solution.py:677
  679.0 485.1 %all-reduce.11.cloned.1.call-start = ((), (), s32[]{:S(2)}) async-start(), calls=%async_computation.11 | async-start | bytes 9437184
  717.4 22.2 %collective-permute-start.22 = (bf16[1024,1536]{1,0:T(8,128)(2,1)}, bf16[1024,1536]{1,0:T(8,128)(2,1)}, u32[]{:S(2)}, u32[]{:S(2)}) collective-permute-start(bf16[1024,1536]{1,0:T(8,128)(2,1)} %convolution_convert_fusion.5), channel_id=1, source_target_pairs={{0,4},{4,0},{1,5},{5,1},{2,6},{6,2},{3,7},{7,3},{8,12},{12,8},{9,1... | collective-permute-start | bytes 9437192 | tf_op jit(solution)/shard_map/ppermute | solution.py:677
  865.5 61.8 %collective-permute-start.23 = (bf16[4,1,4,768,384]{4,3,2,1,0:T(8,128)(2,1)}, bf16[4,1,4,768,384]{4,3,2,1,0:T(8,128)(2,1)}, u32[]{:S(2)}, u32[]{:S(2)}) collective-permute-start(bf16[4,1,4,768,384]{4,3,2,1,0:T(8,128)(2,1)} %bitcast.49), channel_id=1, source_target_pairs={{0,4},{4,0},{1,5},{5,1},{2,6},{6,2},{3,7},{7,3},{8,12},{12,8},{9,1... | collective-permute-start | bytes 28311560 | tf_op jit(solution)/shard_map/ppermute | solution.py:677
  871.3 23.1 %collective-permute-start.24 = (bf16[2,192,1536]{2,1,0:T(8,128)(2,1)}, bf16[2,192,1536]{2,1,0:T(8,128)(2,1)}, u32[]{:S(2)}, u32[]{:S(2)}) collective-permute-start(bf16[2,192,1536]{2,1,0:T(8,128)(2,1)} %get-tuple-element.314), channel_id=1, source_target_pairs={{0,4},{4,0},{1,5},{5,1},{2,6},{6,2},{3,7},{7,3},{8,12},{12,8},{9,1... | collective-permute-start | bytes 3538952 | tf_op jit(solution)/shard_map/ppermute | solution.py:677
  883.2 27.3 %collective-permute-start.25 = (bf16[1024,1536]{1,0:T(8,128)(2,1)}, bf16[1024,1536]{1,0:T(8,128)(2,1)}, u32[]{:S(2)}, u32[]{:S(2)}) collective-permute-start(bf16[1024,1536]{1,0:T(8,128)(2,1)} %convolution_convert_fusion.4), channel_id=1, source_target_pairs={{0,4},{4,0},{1,5},{5,1},{2,6},{6,2},{3,7},{7,3},{8,12},{12,8},{9,1... | collective-permute-start | bytes 9437192 | tf_op jit(solution)/shard_map/ppermute | solution.py:677
  903.6 4.7 collective-permute-start.26
  903.7 309.6 %reduce-scatter.17.cloned.1.call-start = ((), (), s32[]{:S(2)}) async-start(), calls=%async_computation.6 | async-start | bytes 2949120 | tf_op jit(solution)/shard_map/reduce_scatter | solution.py:1742
  1165.8 49.5 %collective-permute-start.27 = (bf16[48,3072]{1,0:T(8,128)(2,1)}, bf16[48,3072]{1,0:T(8,128)(2,1)}, u32[]{:S(2)}, u32[]{:S(2)}) collective-permute-start(bf16[48,3072]{1,0:T(8,128)(2,1)} %dynamic-slice_bitcast_fusion.4), channel_id=1, source_target_pairs={{0,4},{4,0},{1,5},{5,1},{2,6},{6,2},{3,7},{7,3},{8,12},{12,8},{9,1... | collective-permute-start | bytes 884744 | tf_op jit(solution)/shard_map/ppermute | solution.py:677
  1167.7 47.6 %collective-permute-start.28 = (bf16[48,3072]{1,0:T(8,128)(2,1)}, bf16[48,3072]{1,0:T(8,128)(2,1)}, u32[]{:S(2)}, u32[]{:S(2)}) collective-permute-start(bf16[48,3072]{1,0:T(8,128)(2,1)} %dynamic-slice_bitcast_fusion.2), channel_id=1, source_target_pairs={{0,4},{4,0},{1,5},{5,1},{2,6},{6,2},{3,7},{7,3},{8,12},{12,8},{9,1... | collective-permute-start | bytes 884744 | tf_op jit(solution)/shard_map/ppermute | solution.py:677
  1226.0 4.4 collective-permute-start.31
  (147 other events, 2883.1 us)
Sparse Core Ops, SparseCore 0:
  12.8 187.6 all-gather.4
  203.8 152.1 all-gather.6
  359.4 122.0 all-gather.8
  616.9 94.6 reduce-scatter.18
  714.5 95.0 reduce-scatter.20
  812.6 94.9 reduce-scatter.22
  910.0 253.8 all-reduce.10
  1166.2 47.0 reduce-scatter.16

commit v4 on v3

--- a/solution.py
+++ b/solution.py
@@ -204,19 +204,20 @@
     return (first_moment, second_moment, weight)
 
 
-def shampoo_update(slots_now, gradient, left_stat, right_stat, left_root, right_root):
-    left_stat = STAT_DECAY * left_stat + (1.0 - STAT_DECAY) * jnp.einsum(
-        "sij,skj->sik", gradient, gradient, precision=BEST_PRECISION
-    )
-    right_stat = STAT_DECAY * right_stat + (1.0 - STAT_DECAY) * jnp.einsum(
-        "sji,sjk->sik", gradient, gradient, precision=BEST_PRECISION
-    )
-    inner = jnp.einsum("sij,sjk->sik", gradient, right_root, precision=BEST_PRECISION)
-    direction = jnp.einsum("sij,sjk->sik", left_root, inner, precision=BEST_PRECISION)
+def shampoo_update(slots_now, gradient, rest, left_stat, right_stat, left_root, right_root):
+    share_now = (1.0 - STAT_DECAY) * rest * rest
+    left_stat = STAT_DECAY * left_stat + share_now * jnp.einsum(
+        "sij,skj->sik", gradient, gradient, precision=lax.Precision.HIGH
+    )
+    right_stat = STAT_DECAY * right_stat + share_now * jnp.einsum(
+        "sji,sjk->sik", gradient, gradient, precision=lax.Precision.HIGH
+    )
+    inner = jnp.einsum("sij,sjk->sik", gradient, right_root, precision=lax.Precision.HIGH)
+    direction = jnp.einsum("sij,sjk->sik", left_root, inner, precision=lax.Precision.HIGH)
     return (
         left_stat,
         right_stat,
-        slots_now - SHAMPOO_RATE * (direction + WEIGHT_DECAY * slots_now),
+        slots_now - SHAMPOO_RATE * (rest * direction + WEIGHT_DECAY * slots_now),
     )
 
 
@@ -681,24 +682,6 @@
     return lax.dynamic_index_in_dim(values, position, axis, keepdims=False)
 
 
-def grow(values, axis):
-    bit = 1
-    while bit < lax.axis_size(axis):
-        values = jnp.concatenate([values, swap(values, axis, bit)], 0)
-        bit *= 2
-    return values
-
-
-def own_quarters(values, core, line):
-    pair = jnp.concatenate([values, swap(values, "c")], 0)
-    pieces = []
-    for offset in range(4):
-        target = line ^ offset
-        piece = pick(pair, ((target // 2) ^ core) * 2 + target % 2)
-        pieces.append(swap(piece, "z", offset) if offset else piece)
-    return jnp.concatenate(pieces, 0)
-
-
 def low_sum(*terms):
     total = terms[0].astype(jnp.float32)
     for term in terms[1:]:
@@ -764,13 +747,17 @@
 def gather_kernel(arrays, groups, *refs):
     count = len(arrays)
     inputs = sum(2 if kind == "cols" else 1 for kind, _, _ in arrays)
-    sources, bufs = list(refs[:inputs]), refs[inputs : inputs + count]
-    send_sem, recv_sem, core_send, core_recv, local_sem = refs[inputs + count :]
+    sources = list(refs[:inputs])
+    send_sem, recv_sem, core_send, core_recv, local_sem, *item_sems = refs[inputs + 4 + count :]
+    item_refs = refs[inputs : inputs + 2] + refs[inputs + 2 + count : inputs + 4 + count]
+    bufs = refs[inputs + 2 : inputs + 2 + count]
     me = coordinates()
     row, column, core, line = me
     plane = 2 * row + column
     peers = chip_peers(me)
-    greet(peers)
+    others = {offset + 4: (row, column, 1 - core, line ^ offset) for offset in (1, 2, 3)}
+    greet({**peers, **others})
+    finish_items = move_items(me, item_refs, item_sems)
     local, cross = [], []
     for index_value, (kind, _, _) in enumerate(arrays):
         spot = bufs[index_value].at[plane, 0 if kind == "one" else core, line]
@@ -864,9 +851,71 @@
         last = core_copy(number)
         if last is not None:
             last.wait()
-
-
-def gather_weights(arrays, groups, sources, collective_id):
+    finish_items()
+
+
+def move_items(me, refs, sems):
+    row, column, core, line = me
+    send_sem, recv_sem, local_sem = sems
+
+    def outgoing(kind, inner, side):
+        return send(
+            refs[kind].at[inner],
+            refs[2 + kind].at[line],
+            send_sem.at[kind, inner, side],
+            recv_sem.at[kind, line],
+            (row, column, side, 2 * core + inner),
+        )
+
+    def kept(kind, inner):
+        return pltpu.make_async_copy(
+            refs[kind].at[inner], refs[2 + kind].at[line], local_sem.at[kind]
+        )
+
+    def incoming(kind, origin):
+        return send(
+            refs[kind].at[0],
+            refs[2 + kind].at[origin],
+            send_sem.at[kind, 0, 0],
+            recv_sem.at[kind, origin],
+            (row, column, 1 - core, line),
+        )
+
+    def each_target(act, keep):
+        for kind in range(2):
+            for inner in range(2):
+                for side in range(2):
+                    own = (2 * core + inner == line) & (core == side)
+
+                    @pl.when(own)
+                    def stay():
+                        keep(kind, inner)
+
+                    @pl.when(jnp.logical_not(own))
+                    def leave():
+                        act(kind, inner, side)
+
+    each_target(
+        lambda kind, inner, side: outgoing(kind, inner, side).start(),
+        lambda kind, inner: kept(kind, inner).start(),
+    )
+
+    def finish_items():
+        each_target(
+            lambda kind, inner, side: outgoing(kind, inner, side).wait_send(),
+            lambda kind, inner: kept(kind, inner).wait(),
+        )
+        for kind in range(2):
+            for origin in range(4):
+
+                @pl.when(jnp.logical_not((line == origin) & (core == line // 2)))
+                def arrive():
+                    incoming(kind, origin).wait_recv()
+
+    return finish_items
+
+
+def gather_weights(arrays, groups, sources, items, collective_id):
     units = sum(len(group) for group in groups)
     dma = pltpu.SemaphoreType.DMA
     return pl.pallas_call(
@@ -874,18 +923,185 @@
         out_shape=[
             jax.ShapeDtypeStruct((4, 1 if kind == "one" else 2, 4) + shape, dtype)
             for kind, shape, dtype in arrays
-        ],
-        in_specs=anywhere(len(sources)),
-        out_specs=anywhere(len(arrays)),
+        ]
+        + [jax.ShapeDtypeStruct((4,) + item.shape[1:], item.dtype) for item in items],
+        in_specs=anywhere(len(sources) + 2),
+        out_specs=anywhere(len(arrays) + 2),
         scratch_shapes=[
             dma((units, 7)),
             dma((units, 7)),
             dma((len(arrays),)),
             dma((len(arrays),)),
             dma((len(arrays),)),
+            dma((2, 2, 2)),
+            dma((2, 4)),
+            dma((2,)),
         ],
         compiler_params=pltpu.CompilerParams(collective_id=collective_id, has_side_effects=True),
-    )(*sources)
+    )(*sources, *items)
+
+
+def share_kernel(values, shared, send_sem, recv_sem):
+    row, column, core, line = coordinates()
+    own = 8 * row + 4 * column + line
+
+    def peer(offset):
+        return (row ^ (offset // 8), column ^ (offset // 4 % 2), core, line ^ (offset % 4))
+
+    greet({offset: peer(offset) for offset in range(1, 16)})
+    copies = [
+        send(
+            values, shared.at[own], send_sem.at[offset], recv_sem.at[offset], peer(offset)
+        )
+        for offset in range(1, 16)
+    ]
+    for copy in copies:
+        copy.start()
+    shared[own] = values[...]
+    for copy in copies:
+        copy.wait()
+
+
+def share(values, collective_id):
+    dma = pltpu.SemaphoreType.DMA
+    return pl.pallas_call(
+        share_kernel,
+        out_shape=jax.ShapeDtypeStruct((16,) + values.shape, values.dtype),
+        in_specs=[pl.BlockSpec(memory_space=pltpu.VMEM)],
+        out_specs=pl.BlockSpec(memory_space=pltpu.VMEM),
+        scratch_shapes=[dma((16,)), dma((16,))],
+        compiler_params=pltpu.CompilerParams(collective_id=collective_id, has_side_effects=True),
+    )(values)
+
+
+FEED_TILE = 256
+FEED_ROWS = 512
+
+
+def chunks(size, body):
+    for start in range(0, size, FEED_ROWS):
+        body(pl.ds(start, FEED_ROWS))
+
+
+def feed_kernel(rows, gate_tile, up_tile, gate, up, hidden):
+    def body(at):
+        gate_part = jnp.dot(rows[at, :], gate_tile[...], preferred_element_type=jnp.float32)
+        up_part = jnp.dot(rows[at, :], up_tile[...], preferred_element_type=jnp.float32)
+        gate[at, :] = gate_part.astype(gate.dtype)
+        up[at, :] = up_part.astype(up.dtype)
+        hidden[at, :] = (gate_part * jax.nn.sigmoid(gate_part) * up_part).astype(hidden.dtype)
+
+    chunks(rows.shape[0], body)
+
+
+def hidden_back_kernel(grad, down_tile, gate, up, hidden, grad_gate, grad_up, grad_down):
+    def body(at):
+        back = dot_back(grad[at, :], down_tile[...])
+        gate_part = gate[at, :].astype(jnp.float32)
+        sigmoid = jax.nn.sigmoid(gate_part)
+        grad_gate[at, :] = (
+            back * up[at, :].astype(jnp.float32) * sigmoid * (1.0 + gate_part * (1.0 - sigmoid))
+        ).astype(grad_gate.dtype)
+        grad_up[at, :] = (back * gate_part * sigmoid).astype(grad_up.dtype)
+
+    chunks(grad.shape[0], body)
+
+    def weight(at):
+        grad_down[:, at] = tdot(hidden[...], grad[:, at]).astype(grad_down.dtype)
+
+    chunks(grad.shape[1], weight)
+
+
+def rows_back_kernel(
+    turned_rows, grad_gate, grad_up, gate_tile, up_tile, gate_out, up_out, rows_out, total
+):
+    @pl.when(pl.program_id(0) == 0)
+    def clear():
+        total[...] = jnp.zeros_like(total)
+
+    def body(at):
+        gate_out[at, :] = jnp.dot(
+            turned_rows[at, :], grad_gate[...], preferred_element_type=jnp.float32
+        ).astype(gate_out.dtype)
+        up_out[at, :] = jnp.dot(
+            turned_rows[at, :], grad_up[...], preferred_element_type=jnp.float32
+        ).astype(up_out.dtype)
+        total[:, at] += dot_back(grad_gate[...], gate_tile[at, :]) + dot_back(
+            grad_up[...], up_tile[at, :]
+        )
+
+    chunks(turned_rows.shape[0], body)
+
+    @pl.when(pl.program_id(0) == pl.num_programs(0) - 1)
+    def store():
+        rows_out[...] = total[...].astype(rows_out.dtype)
+
+
+def feed_call(kernel, operands, outputs, flops, scratch=()):
+    units = FF // 2
+
+    def spec(shape, kind):
+        height, width = shape
+        if kind == "columns":
+            return pl.BlockSpec((height, FEED_TILE), lambda step: (0, step))
+        if kind == "rows":
+            return pl.BlockSpec((FEED_TILE, width), lambda step: (step, 0))
+        return pl.BlockSpec(shape, lambda step: (0, 0))
+
+    low = jnp.bfloat16
+    moved = sum(value.size for value, _ in operands) + sum(h * w for (h, w), _ in outputs)
+    return pl.pallas_call(
+        kernel,
+        grid=(units // FEED_TILE,),
+        in_specs=[spec(value.shape, kind) for value, kind in operands],
+        out_specs=[spec(shape, kind) for shape, kind in outputs],
+        out_shape=[jax.ShapeDtypeStruct(shape, low) for shape, _ in outputs],
+        scratch_shapes=list(scratch),
+        compiler_params=pltpu.CompilerParams(vmem_limit_bytes=56 * 2**20),
+        cost_estimate=pl.CostEstimate(flops=flops, bytes_accessed=2 * moved, transcendentals=0),
+    )(*[value for value, _ in operands])
+
+
+def feed(rows, gate_weight, up_weight):
+    shape = (rows.shape[0], FF // 2)
+    return feed_call(
+        feed_kernel,
+        [(rows, "whole"), (gate_weight, "columns"), (up_weight, "columns")],
+        [(shape, "columns")] * 3,
+        4 * rows.size * (FF // 2),
+    )
+
+
+def hidden_back(grad, down, gate, up, hidden):
+    shape = hidden.shape
+    return feed_call(
+        hidden_back_kernel,
+        [
+            (grad, "whole"),
+            (down, "rows"),
+            (gate, "columns"),
+            (up, "columns"),
+            (hidden, "columns"),
+        ],
+        [(shape, "columns"), (shape, "columns"), (down.shape, "rows")],
+        4 * grad.size * (FF // 2),
+    )
+
+
+def rows_back(rows, grad_gate, grad_up, gate_weight, up_weight):
+    return feed_call(
+        rows_back_kernel,
+        [
+            (rows.T, "whole"),
+            (grad_gate, "columns"),
+            (grad_up, "columns"),
+            (gate_weight, "columns"),
+            (up_weight, "columns"),
+        ],
+        [(gate_weight.shape, "columns"), (up_weight.shape, "columns"), (rows.shape, "whole")],
+        8 * rows.size * (FF // 2),
+        [pltpu.VMEM(rows.shape, jnp.float32)],
+    )
 
 
 def reduce_kernel(arrays, groups, *refs):
@@ -1219,7 +1435,7 @@
         ],
         compiler_params=pltpu.CompilerParams(vmem_limit_bytes=48 * 2**20),
         cost_estimate=pl.CostEstimate(
-            flops=pairs * 2 * rows * count * 128 * 4,
+            flops=3 * pairs * 2 * rows * count * 128 * 4,
             bytes_accessed=pairs * 128 * (rows * 10 + count * 4),
             transcendentals=pairs * 2 * rows * count,
         ),
@@ -1339,7 +1555,7 @@
         scratch_shapes=[pltpu.VMEM((count, 128), jnp.float32)] * 2,
         compiler_params=pltpu.CompilerParams(vmem_limit_bytes=48 * 2**20),
         cost_estimate=pl.CostEstimate(
-            flops=pairs * 2 * rows * count * 128 * 10,
+            flops=3 * pairs * 2 * rows * count * 128 * 10,
             bytes_accessed=pairs * 128 * (rows * 16 + count * 8),
             transcendentals=pairs * 2 * rows * count,
         ),
@@ -1401,32 +1617,37 @@
 SLOTS_STEP = 8
 
 
-def collect_kernel(rows_at, columns_at, sides, joined, mix, target):
+def collect_kernel(rows_at, columns_at, sides, joined, mix, near, far):
     step = pl.program_id(0)
     lane = lax.broadcasted_iota(jnp.int32, (BLK, 2 * BLK), 1)
-    target[...] = jnp.zeros_like(target)
-    for inner in range(SLOTS_STEP):
-        slot, pair, right = step * SLOTS_STEP + inner, inner // 2, inner % 2
-        code = sides[slot]
-        rows = pl.ds(pl.multiple_of(rows_at[slot] * BLK, BLK), BLK)
-        columns = pl.ds(pl.multiple_of(columns_at[slot] * 2 * BLK, 128), 2 * BLK)
-
-        def put(source):
-            tile = shifted(source[rows, columns], code % 2 != right).astype(target.dtype)
+
+    def fill(target):
+        target[...] = jnp.zeros_like(target)
+        for inner in range(SLOTS_STEP):
+            slot, pair, right = step * SLOTS_STEP + inner, inner // 2, inner % 2
+            code = sides[slot]
+            rows = pl.ds(pl.multiple_of(rows_at[slot] * BLK, BLK), BLK)
+            columns = pl.ds(pl.multiple_of(columns_at[slot] * 2 * BLK, 128), 2 * BLK)
             own = lane // BLK == right
-            target[pair] = jnp.where(own, tile, target[pair])
-
-        @pl.when(code // 2 == 0)
-        def from_joined():
-            put(joined)
-
-        @pl.when(code // 2 == 1)
-        def from_mix():
-            put(mix)
+
+            def put(source, is_shifted):
+                tile = source[rows, columns]
+                if is_shifted:
+                    tile = pltpu.roll(tile.astype(jnp.float32), BLK, 1).astype(tile.dtype)
+                target[pair] = jnp.where(own, tile, target[pair])
+
+            for which, source in enumerate((joined, mix)):
+                for side in range(2):
+                    pl.when(code == 2 * which + side)(partial(put, source, side != right))
+
+    near_steps = pl.num_programs(0) // 2
+    pl.when(step < near_steps)(partial(fill, near))
+    pl.when(step >= near_steps)(partial(fill, far))
 
 
 def collect(joined, mix, rows_at, columns_at, sides):
     steps = sides.shape[0] // SLOTS_STEP
+    block = (SLOTS_STEP // 2, BLK, 2 * BLK)
 
     def resident(array):
         return pl.BlockSpec(array.shape, lambda step, *_: (0, 0), pipeline_mode=pl.Buffered(1))
@@ -1437,15 +1658,16 @@
             num_scalar_prefetch=3,
             grid=(steps,),
             in_specs=[resident(joined), resident(mix)],
-            out_specs=pl.BlockSpec(
-                (SLOTS_STEP // 2, BLK, 2 * BLK), lambda step, *_: (step, 0, 0)
-            ),
+            out_specs=[
+                pl.BlockSpec(block, lambda step, *_: (jnp.minimum(step, steps // 2 - 1), 0, 0)),
+                pl.BlockSpec(block, lambda step, *_: (jnp.maximum(step - steps // 2, 0), 0, 0)),
+            ],
         ),
-        out_shape=jax.ShapeDtypeStruct((sides.shape[0] // 2, BLK, 2 * BLK), joined.dtype),
+        out_shape=[jax.ShapeDtypeStruct((sides.shape[0] // 4, BLK, 2 * BLK), joined.dtype)] * 2,
         compiler_params=pltpu.CompilerParams(vmem_limit_bytes=48 * 2**20),
         cost_estimate=pl.CostEstimate(
             flops=0,
-            bytes_accessed=2 * (joined.size + mix.size) + 2 * sides.shape[0] * BLK * BLK,
+            bytes_accessed=4 * (joined.size + mix.size) + 4 * sides.shape[0] * BLK * BLK,
             transcendentals=0,
         ),
     )(rows_at, columns_at, sides, joined, mix)
@@ -1496,14 +1718,16 @@
     items_total = 16
     mse_scale = 1.0 / (items_total * FRAMES * DIN)
 
+    meta = jnp.concatenate([timesteps, text_lengths, negatives.reshape(-1)])[None]
     pack = jnp.concatenate(
         [
-            end_weights.reshape(4, D),
             time_table,
-            jnp.pad(norm_gains.reshape(1, 144), ((0, 3), (0, D - 144))),
+            jnp.pad(norm_gains.T.reshape(1, 144), ((0, 0), (0, D - 144))),
+            jnp.pad(meta.astype(f32), ((0, 6), (0, D - 34))),
         ],
         0,
     ).astype(bf16)
+    low_ends = end_weights.reshape(48, 2 * DIN).astype(bf16)
     low_slots = square_slots.astype(bf16).reshape(4, 2, BLK, BLK)
     low_pairs = jnp.concatenate([low_slots[:, 0], low_slots[:, 1]], 2).reshape(4 * BLK, 2 * BLK)
     low_cross = cross_weights.astype(bf16)
@@ -1537,10 +1761,7 @@
         feed_blocks.append(
             jnp.where(core == 0, jnp.stack([kept, received]), jnp.stack([received, kept]))
         )
-    gate_weight, up_weight = (
-        gathered(block).reshape(4, 4, 2, 48, FF // 2).transpose(0, 2, 1, 3, 4).reshape(D, FF // 2)
-        for block in feed_blocks
-    )
+    gate_weight, up_weight = (gathered(block).reshape(D, FF // 2) for block in feed_blocks)
     down = gathered(low_down).reshape(FF // 2, D)
     arrays = (
         ("cols", (16, D), bf16),
@@ -1549,9 +1770,10 @@
         ("half", (48, D), bf16),
         ("cols", (16, 1152), bf16),
         ("cols", (16, 1152), bf16),
+        ("cols", (48, 2 * DIN), bf16),
     )
     whole = slice(None)
-    groups = [((0, 0, whole, whole), (5, 1, whole, whole))]
+    groups = [((0, 0, whole, whole), (5, 1, whole, whole), (6, 1, whole, whole))]
     groups += [
         ((1, 0, pl.ds(step * 96, 96), whole), (1, 1, pl.ds(384 + step * 96, 96), whole))
         for step in range(4)
@@ -1561,7 +1783,17 @@
         for step in range(2)
     ]
     groups += [((4, 0, whole, whole),)]
-    packs, all_pairs, cross_query, cross_out, keys_own, values_own = gather_weights(
+    (
+        packs,
+        all_pairs,
+        cross_query,
+        cross_out,
+        keys_own,
+        values_own,
+        ends_full,
+        frames,
+        tokens,
+    ) = gather_weights(
         arrays,
         groups,
         (
@@ -1575,14 +1807,17 @@
             kv_block(0, 1 - core),
             kv_block(1, core),
             kv_block(1, 1 - core),
+            low_ends,
+            low_ends,
         ),
+        (jnp.concatenate([latents, noise_field], 2), text_tokens),
         1,
     )
     packs = packs.reshape(32, 16, D)
-    ends_full = packs[:, :4].reshape(D, 2, DIN)
-    table_full = packs[:, 4:12].reshape(NTIME, D)
-    gain_values = packs[:, 12, :144].reshape(D, 3).astype(f32)
-    weight_in, weight_out = ends_full[:, 0, :], ends_full[:, 1, :]
+    table_full = packs[:, :8].reshape(NTIME, D)
+    gain_values = packs[:, 8, :144].reshape(32, 3, 48).transpose(1, 0, 2).reshape(3, D).astype(f32)
+    ends_full = ends_full.reshape(D, 2 * DIN)
+    weight_in, weight_out = ends_full[:, :DIN], ends_full[:, DIN:]
     all_pairs = all_pairs.reshape(128, BLK, 2 * BLK)
     inverse_order = (
         jnp.zeros_like(assignment)
@@ -1609,25 +1844,15 @@
         [keys_own.reshape(DT, half), values_own.reshape(DT, half)], 1
     )
 
-    meta = jnp.concatenate([timesteps[:, None], text_lengths[:, None], negatives], 1)
-    metas = meta
-    for axis in ("c", "x", "y"):
-        metas = grow(metas, axis)
-    base = 4 * plane + 2 * core
-    relative = jnp.arange(items_total, dtype=jnp.int32)
-    metas = metas[(item ^ base) ^ relative]
-    timestep, text_length = metas[0, 0], metas[0, 1]
-    negative_rows = metas[:, 2:]
-    frames = own_quarters(jnp.concatenate([latents, noise_field], 2), core, line)
+    metas = packs.reshape(8, 4, 16, D)[:, 0, 9, :34].astype(jnp.int32)
+    timestep = pick(metas[:, :2].reshape(-1), item)
+    text_length = pick(metas[:, 2:4].reshape(-1), item)
+    negative_rows = metas[:, 4:].reshape(items_total, -1)
+    frames = frames.reshape(FRAMES, 2 * DIN)
     clean, noise = frames[:, :DIN], frames[:, DIN:]
-    tokens = own_quarters(text_tokens, core, line)
-    quarter = line ^ four
-    frame_positions = (
-        (quarter[:, None] * 256 + jnp.arange(256, dtype=jnp.int32)[None, :]).reshape(-1) + 1
-    )
-    token_slots = (
-        quarter[:, None] * 32 + jnp.arange(32, dtype=jnp.int32)[None, :]
-    ).reshape(-1)
+    tokens = tokens.reshape(-1, DT)
+    frame_positions = jnp.arange(FRAMES, dtype=jnp.int32) + 1
+    token_slots = jnp.arange(tokens.shape[0], dtype=jnp.int32)
     halfway = HD // 2
     frequency = jnp.exp(jnp.arange(halfway, dtype=f32) * (-2.0 * math.log(10000.0) / HD))
     turn = frame_positions.astype(f32)[:, None] * frequency[None, :]
@@ -1640,11 +1865,11 @@
 
     residual = dot_back(noised, weight_in)
     normed_one, inverse_one = layer_stats(residual)
-    input_one = (normed_one * gain_values[:, 0]).astype(bf16)
+    input_one = (normed_one * gain_values[0]).astype(bf16)
     features = time_features(timestep[None]).astype(bf16)
     embeds = jnp.dot(features, table_full, preferred_element_type=f32)
     normed_time, inverse_time = layer_stats(embeds)
-    input_time = (normed_time * gain_values[:, 0]).astype(bf16)
+    input_time = (normed_time * gain_values[0]).astype(bf16)
     time_block = jnp.pad(input_time, ((0, 15), (0, 0)))
     joined, joined_time = join(input_one, time_block, projection, cosine_table, sine_table)
     pairs = half // 128
@@ -1654,7 +1879,7 @@
     )
     after_self = residual + on_both(jnp.dot(mixed_flat, weight_mix, preferred_element_type=f32))
     normed_two, inverse_two = layer_stats(after_self)
-    input_two = (normed_two * gain_values[:, 1]).astype(bf16)
+    input_two = (normed_two * gain_values[1]).astype(bf16)
     cross_queries = jnp.dot(input_two, cross_query, preferred_element_type=f32).astype(bf16)
     projected = jnp.dot(tokens, kv_own, preferred_element_type=f32).astype(bf16)
     valid = token_slots < text_length
@@ -1669,12 +1894,12 @@
     )
     after_cross = after_self + on_both(jnp.dot(cross_flat, cross_out, preferred_element_type=f32))
     normed_three, inverse_three = layer_stats(after_cross)
-    input_three = (normed_three * gain_values[:, 2]).astype(bf16)
-    gate_part = jnp.dot(input_three, gate_weight, preferred_element_type=f32)
-    up_part = jnp.dot(input_three, up_weight, preferred_element_type=f32)
-    sigmoid = jax.nn.sigmoid(gate_part)
-    silu_value = gate_part * sigmoid
-    hidden = (silu_value * up_part).astype(bf16)
+    input_three = (normed_three * gain_values[2]).astype(bf16)
+    feature = jnp.arange(D, dtype=jnp.int32)
+    gathered_at = (feature // 384 * 4 + feature // 48 % 4) * 96 + feature // 192 % 2 * 48 + feature % 48
+    reorder = (gathered_at[:, None] == feature[None, :]).astype(bf16)
+    feed_rows = jnp.dot(input_three, reorder, preferred_element_type=f32).astype(bf16)
+    gate_part, up_part, hidden = feed(feed_rows, gate_weight, up_weight)
     down_out = on_both(jnp.dot(hidden, down, preferred_element_type=f32))
     output_rows = after_cross + down_out
     output_low = output_rows.astype(bf16)
@@ -1690,9 +1915,8 @@
         jnp.concatenate([text_half, text_rest]),
         jnp.concatenate([text_rest, text_half]),
     )
-    pools = jnp.stack([jnp.sum(output_rows, 0) / FRAMES, text_pool], 0)[None]
-    for axis in ("z", "x", "y"):
-        pools = grow(pools, axis)
+    pools = jnp.stack([jnp.sum(output_rows, 0) / FRAMES, text_pool], 0)
+    pools = share(pools.reshape(8, D // 4), 3).reshape(items_total, 2, D)
     inverse_pools = lax.rsqrt(jnp.sum(pools * pools, -1, keepdims=True) + POOL_EPS)
     units = pools * inverse_pools
     audio_units, text_units = units[:, 0], units[:, 1]
@@ -1704,47 +1928,54 @@
     )
     same = jnp.eye(items_total, dtype=f32)
     counts = same + jnp.sum(
-        (negative_rows[:, None, :] == (item ^ relative)[None, :, None]).astype(f32), -1
+        (negative_rows[:, None, :] == jnp.arange(items_total, dtype=jnp.int32)[None, :, None]).astype(f32), -1
     )
     peak = jnp.max(jnp.where(counts > 0, similar, -jnp.inf), -1, keepdims=True)
     powers = jnp.where(counts > 0, counts * jnp.exp(similar - peak), 0.0)
     totals_row = jnp.sum(powers, -1, keepdims=True)
-    contrast_own = peak[0, 0] + jnp.log(totals_row[0, 0]) - similar[0, 0]
+    contrast_own = pick(
+        peak[:, 0] + jnp.log(totals_row[:, 0]) - jnp.sum(same * similar, -1), item
+    )
     grad_similar = (powers / totals_row - same) * (
         CONTRAST_WEIGHT / items_total / CONTRAST_TEMP
     )
-    grad_audio_unit = jnp.sum(grad_similar[0][:, None] * text_units, 0)
-    grad_text_unit = jnp.sum(grad_similar[:, 0][:, None] * audio_units, 0)
+    grad_audio_unit = jnp.sum(pick(grad_similar, item)[:, None] * text_units, 0)
+    grad_text_unit = jnp.sum(pick(grad_similar, item, 1)[:, None] * audio_units, 0)
 
     def unit_back(gradient, unit, inverse):
         return inverse * (gradient - unit * jnp.sum(unit * gradient))
 
-    grad_audio = unit_back(grad_audio_unit, audio_units[0], inverse_pools[0, 0])
-    grad_text = unit_back(grad_text_unit, text_units[0], inverse_pools[0, 1])
+    grad_audio = unit_back(grad_audio_unit, pick(audio_units, item), pick(inverse_pools, item)[0])
+    grad_text = unit_back(grad_text_unit, pick(text_units, item), pick(inverse_pools, item)[1])
 
     grad_predicted = (2.0 * mse_scale * errors).astype(bf16)
     grad_out_weight = tdot(output_low, grad_predicted)
     grad_output = dot_back(grad_predicted, weight_out) + grad_audio[None, :] / FRAMES
     grad_low = grad_output.astype(bf16)
-    grad_down = tdot(hidden, grad_low).astype(bf16)
-    grad_hidden = dot_back(grad_low, down)
-    grad_gate = (grad_hidden * up_part * sigmoid * (1.0 + gate_part * (1.0 - sigmoid))).astype(bf16)
-    grad_up = (grad_hidden * silu_value).astype(bf16)
-    grad_gate_weight = tdot(input_three, grad_gate).astype(bf16)
-    grad_up_weight = tdot(input_three, grad_up).astype(bf16)
-    def scattered(gradient, width):
-        total = lax.psum_scatter(
-            gradient.reshape(4, -1, 4, width, gradient.shape[1]),
+    grad_gate, grad_up, grad_down = hidden_back(grad_low, down, gate_part, up_part, hidden)
+    grad_gate_weight, grad_up_weight, grad_feed_rows = rows_back(
+        feed_rows, grad_gate, grad_up, gate_weight, up_weight
+    )
+
+    def over_plane(gradient, width):
+        return lax.psum_scatter(
+            gradient.reshape(4, 4, -1, width, gradient.shape[1]),
             ("y", "x"),
             scatter_dimension=0,
             tiled=True,
         )
-        return lax.psum_scatter(total, "z", scatter_dimension=2, tiled=True)[0, :, 0]
-
-    feed_sums = []
-    for gradient in (grad_gate_weight, grad_up_weight):
-        both_rows = scattered(gradient, 48)
-        feed_sums.append((pick(both_rows, core), swap(pick(both_rows, 1 - core), "c")))
+
+    def over_line(total):
+        return lax.psum_scatter(total, "z", scatter_dimension=1, tiled=True)[0, 0]
+
+    totals = [
+        over_plane(gradient, width)
+        for gradient, width in ((grad_down, 192), (grad_gate_weight, 48), (grad_up_weight, 48))
+    ]
+    down_total, *gate_totals = [over_line(total) for total in totals]
+    feed_sums = [
+        (pick(both_rows, core), swap(pick(both_rows, 1 - core), "c")) for both_rows in gate_totals
+    ]
     gate_columns = []
     for mine, other in feed_sums:
         sides = (jnp.where(core == 0, mine, other), jnp.where(core == 0, other, mine))
@@ -1752,10 +1983,10 @@
             for side in sides:
                 gate_columns.append(side[:, quadrant * 768 : (quadrant + 1) * 768])
     grad_gate_up = jnp.concatenate(gate_columns, 1).astype(f32)
-    grad_down = scattered(grad_down, 192)[0].astype(f32)
-    grad_input_three = on_both(dot_back(grad_gate, gate_weight) + dot_back(grad_up, up_weight))
+    grad_down = down_total[0].astype(f32)
+    grad_input_three = on_both(dot_back(grad_feed_rows, reorder))
     grad_after_cross, gain_three = layer_back(
-        grad_input_three, normed_three, inverse_three, gain_values[:, 2]
+        grad_input_three, normed_three, inverse_three, gain_values[2]
     )
     grad_after_cross = grad_after_cross + grad_output
     grad_cross_in = grad_after_cross.astype(bf16)
@@ -1787,7 +2018,7 @@
         for gradient in (grad_pair_keys, grad_text_values)
     ]
     grad_after_self, gain_two = layer_back(
-        grad_input_two, normed_two, inverse_two, gain_values[:, 1]
+        grad_input_two, normed_two, inverse_two, gain_values[1]
     )
     grad_after_self = grad_after_self + grad_after_cross
     grad_self_in = grad_after_self.astype(bf16)
@@ -1819,14 +2050,15 @@
     is_out = matrix == 3
     side = jnp.where(is_out, block_row // 4, block_column // 4)
     code = jnp.where(side == core, 2 * is_out + block_column % 2, 4)
-    collected = collect(
+    near_slots, far_slots = collect(
         grad_projection,
         grad_mix,
         jnp.where(is_out, block_row % 4, block_row),
         jnp.where(is_out, block_column // 2, matrix * 2 + (block_column % 4) // 2),
         code.astype(jnp.int32),
-    ).reshape(2, 4, 1, 4, 4 * BLK, 2 * BLK)
-    slot_sums = low_sum(collected[0], swap(collected[1], "c")).astype(bf16)
+    )
+    slot_sums = low_sum(near_slots, swap(far_slots, "c")).astype(bf16)
+    slot_sums = slot_sums.reshape(4, 1, 4, 4 * BLK, 2 * BLK)
 
     partial_one = dot_back(grad_joined, projection)
     partial_time = jnp.dot(
@@ -1834,29 +2066,30 @@
     )
     grad_input_one = on_both(partial_one)
     grad_input_time = partial_time + swap(partial_time, "c")
-    grad_residual, gain_one = layer_back(grad_input_one, normed_one, inverse_one, gain_values[:, 0])
+    grad_residual, gain_one = layer_back(grad_input_one, normed_one, inverse_one, gain_values[0])
     grad_residual = (grad_residual + grad_after_self).astype(bf16)
     grad_embeds, gain_time = layer_back(
-        grad_input_time, normed_time, inverse_time, gain_values[:, 0]
+        grad_input_time, normed_time, inverse_time, gain_values[0]
     )
     grad_in_weight = tdot(grad_residual, noised)
     grad_table = features.astype(f32).reshape(NTIME, 1) * grad_embeds
-    grad_gains = jnp.stack([gain_one + gain_time, gain_two, gain_three], 1)
-    grad_ends = jnp.stack([grad_in_weight, grad_out_weight], 1)
-
-    def own_rows(values, width):
-        return pick(values.reshape(2, 2, 2, 4, -1, width), core, 2)
+    grad_gains = jnp.stack([gain_one + gain_time, gain_two, gain_three], 0)
+
+    def own_rows(values):
+        return pick(values.reshape((4, 2, 4) + values.shape[1:]), core, 1)
 
     small = jnp.concatenate(
         [
-            own_rows(grad_ends.reshape(-1, D), D),
-            own_rows(grad_table, D),
+            own_rows(grad_table.reshape(32, 8, D)),
             jnp.pad(
-                own_rows(grad_gains.reshape(32, 144), 144),
-                ((0, 0), (0, 0), (0, 0), (0, 3), (0, D - 144)),
+                own_rows(grad_gains.reshape(3, 32, 48).transpose(1, 0, 2).reshape(32, 1, 144)),
+                ((0, 0), (0, 0), (0, 7), (0, D - 144)),
             ),
         ],
-        3,
+        2,
+    )
+    grad_ends = own_rows(
+        jnp.concatenate([grad_in_weight, grad_out_weight], 1).astype(bf16).reshape(32, 48, 2 * DIN)
     )
     rest_arrays = (
         ("one", (4 * BLK, 2 * BLK)),
@@ -1865,6 +2098,7 @@
         ("cols", (16, 1152)),
         ("cols", (16, 1152)),
         ("one", (16, D)),
+        ("one", (48, 2 * DIN)),
     )
     rest_groups = [((3, 0, whole, whole), (4, 1, whole, whole))]
     rest_groups += [
@@ -1875,7 +2109,7 @@
         ((0, 0, pl.ds(step * 96, 96), whole), (0, 1, pl.ds(384 + step * 96, 96), whole))
         for step in range(4)
     ]
-    rest_groups += [((5, 0, whole, whole),)]
+    rest_groups += [((5, 0, whole, whole), (6, 1, whole, whole))]
     rest_sums = reduce_gradients(
         rest_arrays,
         rest_groups,
@@ -1886,10 +2120,11 @@
             kv_sources[0],
             kv_sources[1],
             small.astype(bf16).reshape(4, 1, 4, 16, D),
+            grad_ends.reshape(4, 1, 4, 48, 2 * DIN),
         ),
         2,
     )
-    slot_rows, query_mine, query_other, grad_cross_out, *kv_sums, small = (
+    slot_rows, query_mine, query_other, grad_cross_out, *kv_sums, small, grad_ends = (
         value.astype(f32) for value in rest_sums
     )
     slot_rows = slot_rows.reshape(4, BLK, 2 * BLK)
@@ -1906,9 +2141,9 @@
         kv_columns.append(jnp.where(core == 0, mine, other))
         kv_columns.append(jnp.where(core == 0, other, mine))
     grad_key_value = jnp.concatenate(kv_columns, 1)
-    grad_ends = small[:4].reshape(48, 2, DIN)
-    grad_table = small[4:12]
-    grad_gains = small[12, :144].reshape(48, 3)
+    grad_ends = grad_ends.reshape(48, 2, DIN)
+    grad_table = small[:8]
+    grad_gains = small[8, :144].reshape(3, 48).T
 
     reduced = (
         grad_ends,
@@ -1968,13 +2203,9 @@
 
 
 def all_sum(*values):
-    total = jnp.stack(values)
-    for axis in ("c", "z", "x", "y"):
-        bit = 1
-        while bit < lax.axis_size(axis):
-            total = total + swap(total, axis, bit)
-            bit *= 2
-    return total[0], total[1]
+    total = jnp.pad(jnp.stack(values)[None], ((0, 7), (0, 128 - len(values))))
+    total = jnp.sum(share(total + swap(total, "c"), 4), 0)
+    return total[0, 0], total[0, 1]
 
 
 def finish(loss_total, gradient_norm, reduced, masters, firsts, seconds, statistics):
@@ -1990,9 +2221,12 @@
                 ADAM_RATES[index_value],
             )
         )
-    clipped_slots = factor * reduced[2]
-    left_new, right_new, slots_new = shampoo_update(masters[2], clipped_slots, *statistics)
-    results.extend([clipped_slots, left_new, right_new, slots_new])
+    slot_norm = jnp.sqrt(jnp.sum(reduced[2] * reduced[2]))
+    slot_factor = CLIP_NORM / jnp.maximum(slot_norm, CLIP_NORM)
+    left_new, right_new, slots_new = shampoo_update(
+        masters[2], slot_factor * reduced[2], factor / slot_factor, *statistics
+    )
+    results.extend([factor * reduced[2], left_new, right_new, slots_new])
     return tuple(results)
 
 

time: 1300 us -> 1230 us (0.946)
  Pallas kernels: 634 us -> 765 us
  matrix products: 261 us -> 136 us
  starting transfers between devices: 33.1 us -> 4.75 us
  local copies, waits for them, and re-layouts: 112 us -> 88.1 us
  waiting for transfers between devices: 84 us -> 67 us
    pallas_call x0 -> x5, Pallas kernels: none -> 124 us  [the longest x3 103 us: feed_call(): pl.pallas_call(kernel, grid=(units // FEED_TILE,), in_specs=[spec(value.s...]
    unnamed x12, waiting for transfers between devices: 0.2 us -> 48.5 us
    dot_general x9 -> x7, matrix products: 84.2 us -> 37.6 us  [dot_back(): lax.dot_general(left, right, (((1,), (1,)), ((), ())), preferred_element_...]
    dot_general x11 -> x8, matrix products: 83.6 us -> 39.8 us  [tdot(): lax.dot_general(left, right, (((0,), (0,)), ((), ())), preferred_element_...]
    reduce_scatter x1 -> x3, waiting for transfers between devices: 38.7 us -> 0.01 us  [over_line(): return lax.psum_scatter(total, 'z', scatter_dimension=1, tiled=True)[0, 0]]
    dot_general x6 -> x5, matrix products: 51.9 us -> 18.6 us  [the longest x1 7.91 us: item_per_chip(): jnp.dot(input_three, reorder, preferred_element_type=f32).astype(bf16)]
    ppermute x34 -> x15, starting transfers between devices: 32.8 us -> 4.39 us  [swap(): lax.ppermute(values, axis, [(i, i ^ bit) for i in range(lax.axis_size(axi...]
    ppermute x34 -> x15, waiting for transfers between devices: 45.1 us -> 16.9 us  [swap(): lax.ppermute(values, axis, [(i, i ^ bit) for i in range(lax.axis_size(axi...]
  transfers between devices with their start and end apart: 42 -> 24, of which waited for: 20 -> 8; matrix products, arithmetic and copies ran while one was open for 29% -> 22% of each run, Pallas kernels for 49% -> 54%
where the time goes in v4:
time: 1230 us
  Pallas kernels  765 us (62%)
  other arithmetic  137 us (11%)
  matrix products  136 us (11%)
  local copies, waits for them, and re-layouts  88.1 us (7%)
  waiting for transfers between devices  67 us (5%)
  between operations  29.6 us (2%)
    pallas_call x1, Pallas kernels, gather_weights(): pl.pallas_call(partial(gather_kernel, arrays, groups), out_shape=[jax.Sha...  270 us
    pallas_call x1, Pallas kernels, reduce_gradients(): pl.pallas_call(partial(reduce_kernel, arrays, groups), out_shape=out_shap...  208 us
    pallas_call x3, Pallas kernels, feed_call(): pl.pallas_call(kernel, grid=(units // FEED_TILE,), in_specs=[spec(value.s...  103 us
    pallas_call x2, Pallas kernels, attend_back(): pl.pallas_call(partial(attend_back_kernel, timed), grid=(pairs,), in_spec...  58.9 us
    unnamed x12, waiting for transfers between devices  48.5 us
    pallas_call x2, Pallas kernels, attend(): pl.pallas_call(partial(attend_kernel, timed), grid=(pairs,), in_specs=[la...  41 us
    dot_general x8, matrix products, tdot(): lax.dot_general(left, right, (((0,), (0,)), ((), ())), preferred_element_...  39.8 us
    dot_general x7, matrix products, dot_back(): lax.dot_general(left, right, (((1,), (1,)), ((), ())), preferred_element_...  37.6 us
  transfers between devices with their start and end apart: 24, of which 8 were waited for; matrix products, arithmetic and copies ran while one was open for 22% of the time, Pallas kernels for 54%

profile of v4, /device:TPU:0, one launch (start us, length us, event | category | flops | bytes accessed | tf_op | source)
XLA Modules:
  0.0 1227.0 jit_solution(11577749109686182725)
XLA Ops:
  32.0 269.5 %shard_map.520 = (bf16[4,2,4,16,1536]{4,3,2,1,0:T(8,128)(2,1)}, bf16[4,2,4,768,384]{4,3,2,1,0:T(8,128)(2,1)}, bf16[4,2,4,48,768]{4,3,2,1,0:T(8,128)(2,1)}, bf16[...) custom-call(bf16[16,1536]{1,0:T(8,128)(2,1)} %fusion.72.refs_0_.refs, ...), custom_call_target="tpu_custom_call" | custom-call | tf_op jit(solution)/shard_map/pallas_call | solution.py:921
  325.3 16.6 %shard_map.521 = (bf16[1536,2304]{1,0:T(8,128)(2,1)}, bf16[768,1536]{1,0:T(8,128)(2,1)S(1)}) custom-call(s32[96]{0:T(128)S(1)} %gather_fusion, s32[32]{0:T(128)S(1)} %gather_fusion.1, bf16[128,192,384]{2,1,0:T(8,128)(2,1)} %bitcast.211), custom_call_target="tpu_custom_call" | custom-call | bytes 28311552 | tf_op jit(solution)/shard_map/pallas_call | solution.py:1591
  342.4 19.0 %shard_map.522 = (bf16[1024,2304]{1,0:T(8,128)(2,1)}, bf16[16,2304]{1,0:T(8,128)(2,1)S(1)}) custom-call(bf16[1024,1536]{1,0:T(8,128)(2,1)S(1)} %multiply_convert_fusion.2.rows, bf16[16,1536]{1,0:T(8,128)(2,1)S(1)} %pad.25.times, bf16[1536,2304]{1,0:T(8,128)(2,1)} %get-tuple-element.77.weights, f32[1024,128]{1,0:T(8,128)S(1)} %pad_maximum_fusion.5.cosine.refs_8_, ...), custom_call_target="tpu_custom_call" | custom-call | flops 7247757312 | bytes 14942208 | tf_op jit(solution)/shard_map/pallas_call | solution.py:1337
  361.4 30.9 %shard_map.523 = (bf16[1024,768]{1,0:T(8,128)(2,1)S(1)}, f32[1024,768]{1,0:T(8,128)S(1)}) custom-call(bf16[1024,2304]{1,0:T(8,128)(2,1)} %get-tuple-element.78.queries.keys.values.refs_0_.refs_1_.refs_2_, bf16[1024,2304]{1,0:T(8,128)(2,1)} %get-tuple-element.78.queries.keys.values.refs_0_.refs_1_.refs_2_, ...), custom_call_target="tpu_custom_call" | custom-call | flops 19327352832 | bytes 11010048 | tf_op jit(solution)/shard_map/pallas_call | solution.py:1422
  419.0 10.2 shard_map.524
  439.8 5.8 fusion.151
  448.3 7.9 fusion.12
  460.8 26.2 %shard_map.525 = (bf16[1024,3072]{1,0:T(8,128)(2,1)}, bf16[1024,3072]{1,0:T(8,128)(2,1)}, bf16[1024,3072]{1,0:T(8,128)(2,1)}) custom-call(bf16[1024,1536]{1,0:T(8,128)(2,1)} %copy.224.rows, bf16[1536,3072]{1,0:T(8,128)(2,1)} %bitcast.246, bf16[1536,3072]{1,0:T(8,128)(2,1)} %bitcast.248), custom_call_target="tpu_custom_call" | custom-call | flops 19327352832 | bytes 40894464 | tf_op jit(solution)/shard_map/pallas_call | solution.py:1053
  488.7 15.6 %convolution_convert_fusion = bf16[1024,1536]{1,0:T(8,128)(2,1)} fusion(bf16[1024,3072]{1,0:T(8,128)(2,1)} %get-tuple-element.88.hidden, bf16[3072,1536]{1,0:T(8,128)(2,1)} %all-gather.9.cloned.1.call-done.down_tile), kind=kOutput, calls=%fused_computation.44 | convolution fusion | flops 9665249280 | bytes 18874368 | tf_op jit(solution)/shard_map/dot_general | solution.py:1903
  510.4 7.6 fusion.19
  518.6 11.5 shard_map.526
  546.2 28.8 %shard_map.527 = (bf16[1024,3072]{1,0:T(8,128)(2,1)}, bf16[1024,3072]{1,0:T(8,128)(2,1)}, bf16[3072,1536]{1,0:T(8,128)(2,1)}) custom-call(bf16[1024,1536]{1,0:T(8,128)(2,1)} %get-tuple-element.391.grad, bf16[3072,1536]{1,0:T(8,128)(2,1)} %all-gather.9.cloned.1.call-done.down_tile, bf16[1024,3072]{1,0:T(8,128)(2,1)} %get-tuple-element.91.gate, ...), custom_call_target="tpu_custom_call" | custom-call | flops 19327352832 | bytes 53477376 | tf_op jit(solution)/shard_map/pallas_call | solution.py:1053
  575.0 47.5 %shard_map.528 = (bf16[1536,3072]{1,0:T(8,128)(2,1)}, bf16[1536,3072]{1,0:T(8,128)(2,1)}, bf16[1024,1536]{1,0:T(8,128)(2,1)}) custom-call(bf16[1536,1024]{1,0:T(8,128)(2,1)} %bitcast.219, bf16[1024,3072]{1,0:T(8,128)(2,1)} %get-tuple-element.93.grad_gate, bf16[1024,3072]{1,0:T(8,128)(2,1)} %get-tuple-element.94.grad_up, bf16[1536,3072]{1,0:T(8,128)(2,1)} %bitcast.247, ...), custom_call_target="tpu_custom_call" | custom-call | flops 38654705664 | bytes 56623104 | tf_op jit(solution)/shard_map/pallas_call | solution.py:1053
  623.4 8.8 fusion.13
  632.3 5.9 collective-permute-done.6
  638.2 7.4 multiply_reduce_fusion.1
  645.6 8.6 multiply_add_fusion.1
  658.8 12.5 %shard_map.529 = (bf16[1024,768]{1,0:T(8,128)(2,1)S(1)}, f32[128,768]{1,0:T(8,128)S(1)}, f32[128,768]{1,0:T(8,128)S(1)}) custom-call(bf16[1024,768]{1,0:T(8,128)(2,1)S(1)} %copy-done.16, bf16[128,1536]{1,0:T(8,128)(2,1)S(1)} %convolution_convert_fusion.8.keys.values.refs_1_.refs_2_, ...), custom_call_target="tpu_custom_call" | custom-call | flops 6039797760 | bytes 13369344 | tf_op jit(solution)/shard_map/pallas_call | solution.py:1549
  683.0 7.1 multiply_reduce_fusion.2
  699.4 46.3 %shard_map.530 = (bf16[1024,768]{1,0:T(8,128)(2,1)S(1)}, bf16[1024,768]{1,0:T(8,128)(2,1)S(1)}, bf16[1024,768]{1,0:T(8,128)(2,1)S(1)}, f32[8,768]{1,0:T(8,128)S(1)}, f32[8,768]{1,0:T(8,128)S(1)}) custom-call(bf16[1024,2304]{1,0:T(8,128)(2,1)} %get-tuple-element.78.queries.keys.values.refs_0_.refs_1_.refs_2_, ...), custom_call_target="tpu_custom_call" | custom-call | flops 48318382080 | bytes 18874368 | tf_op jit(solution)/shard_map/pallas_call | solution.py:1549
  749.6 9.6 add_convert_fusion.1.joined
  759.3 6.2 convolution_convert_fusion.7.mix
  765.5 27.6 %shard_map.531 = (bf16[64,192,384]{2,1,0:T(8,128)(2,1)}, bf16[64,192,384]{2,1,0:T(8,128)(2,1)}) custom-call(s32[256]{0:T(256)S(1)} %get-tuple-element.384.rows_at, s32[256]{0:T(256)S(1)} %get-tuple-element.383.columns_at, s32[256]{0:T(256)S(1)} %get-tuple-element.326.sides, bf16[1536,2304]{1,0:T(8,128)(2,1)} %add_convert_fusion.1.joined, ...), custom_call_target="tpu_custom_call" | custom-call | bytes 56623104 | tf_op jit(solution)/shard_map/pallas_call | solution.py:1655
  793.3 11.3 convolution_convert_fusion.1
  823.3 6.6 convolution_convert_fusion.6
  837.6 6.2 fusion.8
  844.3 6.5 multiply_reduce_fusion
  853.1 8.6 fusion.27
  863.9 47.8 %reduce-scatter.23.cloned.1.call-done = bf16[1,4,1,192,1536]{4,3,2,1,0:T(8,128)(2,1)} async-done(((bf16[4,4,1,192,1536]{4,3,2,1,0:T(8,128)(2,1)}), bf16[1,4,1,192,1536]{4,3,2,1,0:T(8,128)(2,1)}) %reduce-scatter.23.cloned.1.call-update) | async-done | bytes 2359312
  911.8 12.1 add_convert_fusion
  923.9 208.0 %shard_map.532 = (bf16[768,384]{1,0:T(8,128)(2,1)}, bf16[48,768]{1,0:T(8,128)(2,1)}, bf16[48,768]{1,0:T(8,128)(2,1)}, bf16[48,1536]{1,0:T(8,128)(2,1)}, bf16[16,...) custom-call(bf16[4,1,4,768,384]{4,3,2,1,0:T(8,128)(2,1)} %bitcast.20, ...), custom_call_target="tpu_custom_call" | custom-call | tf_op jit(solution)/shard_map/pallas_call | solution.py:1281
  1171.9 10.0 shard_map.533
  (597 shorter events, 243.1 us)
Async XLA Ops:
  7.2 1186.6 %copy-start = (f32[8,192,192]{2,1,0:T(8,128)S(1)}, f32[8,192,192]{2,1,0:T(8,128)}, u32[]{:S(2)}) copy-start(f32[8,192,192]{2,1,0:T(8,128)} %param.65) | copy-start | bytes 3538948
  7.2 453.6 %all-gather.5.cloned.1.call-start = ((), (), s32[]{:S(2)}) async-start(), calls=%async_computation.6 | async-start | bytes 10027008 | tf_op jit(solution)/shard_map/all_gather | solution.py:1756
  10.0 1.7 collective-permute-start.2
  12.7 448.2 %all-gather.7.cloned.1.call-start = ((), (), s32[]{:S(2)}) async-start(), calls=%async_computation.7 | async-start | bytes 10027008 | tf_op jit(solution)/shard_map/all_gather | solution.py:1756
  13.7 1.6 collective-permute-start.3
  16.3 472.4 %all-gather.9.cloned.1.call-start = ((), (), s32[]{:S(2)}) async-start(), calls=%async_computation.11 | async-start | bytes 10027008 | tf_op jit(solution)/shard_map/all_gather | solution.py:1756
  18.6 740.6 %reduce-scatter.19.cloned.1.call-start = ((), (), s32[]{:S(2)}) async-start(), calls=%async_computation.12 | async-start | bytes 11796480
  28.7 275.3 %copy-start.21 = (s32[256]{0:T(256)S(1)}, s32[256]{0:T(256)}, u32[]{:S(2)}) copy-start(s32[256]{0:T(256)} %param.39) | copy-start | bytes 3076
  325.3 17.1 %copy-start.1 = (bf16[1024,1536]{1,0:T(8,128)(2,1)}, bf16[1024,1536]{1,0:T(8,128)(2,1)S(1)}, u32[]{:S(2)}) copy-start(bf16[1024,1536]{1,0:T(8,128)(2,1)S(1)} %multiply_convert_fusion.2.rows) | copy-start | bytes 9437188
  341.9 50.4 %copy-start.9 = (bf16[768,1536]{1,0:T(8,128)(2,1)}, bf16[768,1536]{1,0:T(8,128)(2,1)S(1)}, u32[]{:S(2)}) copy-start(bf16[768,1536]{1,0:T(8,128)(2,1)S(1)} %get-tuple-element.81) | copy-start | bytes 7077892
  342.3 19.0 %copy-start.3 = (f32[1024,128]{1,0:T(8,128)}, f32[1024,128]{1,0:T(8,128)S(1)}, u32[]{:S(2)}) copy-start(f32[1024,128]{1,0:T(8,128)S(1)} %pad_maximum_fusion.6.sine.refs_9_) | copy-start | bytes 1572868
  361.4 30.9 %copy-start.19 = (bf16[16,2304]{1,0:T(8,128)(2,1)}, bf16[16,2304]{1,0:T(8,128)(2,1)S(1)}, u32[]{:S(2)}) copy-start(bf16[16,2304]{1,0:T(8,128)(2,1)S(1)} %get-tuple-element.79.first.second.refs_3_.refs_4_) | copy-start | bytes 221188
  396.3 10.0 collective-permute-start
  433.7 6.2 collective-permute-start.1
  504.3 6.0 collective-permute-start.4
  506.3 3.7 collective-permute-start.5
  622.6 210.3 %reduce-scatter.21.cloned.1.call-start = ((), (), s32[]{:S(2)}) async-start(), calls=%async_computation.13 | async-start | bytes 11796480
  623.2 288.5 %reduce-scatter.23.cloned.1.call-start = ((), (), s32[]{:S(2)}) async-start(), calls=%async_computation.14 | async-start | bytes 11796480
  632.2 6.0 collective-permute-start.6
  632.2 521.5 %reduce-scatter.13.cloned.1.call-start = ((), (), s32[]{:S(2)}) async-start(), calls=%async_computation.8 | async-start | bytes 2949120 | tf_op jit(solution)/shard_map/reduce_scatter | solution.py:1969
  675.6 7.4 collective-permute-start.7
  759.2 396.1 %reduce-scatter.15.cloned.1.call-start = ((), (), s32[]{:S(2)}) async-start(), calls=%async_computation.9 | async-start | bytes 2949120 | tf_op jit(solution)/shard_map/reduce_scatter | solution.py:1969
  765.5 27.7 %copy-start.66 = (bf16[1024,2304]{1,0:T(8,128)(2,1)S(1)}, bf16[1024,2304]{1,0:T(8,128)(2,1)}, u32[]{:S(2)}) copy-start(bf16[1024,2304]{1,0:T(8,128)(2,1)} %copy-done.65) | copy-start | bytes 14155780
  793.2 118.6 %collective-permute-start.8 = (bf16[64,192,384]{2,1,0:T(8,128)(2,1)}, bf16[64,192,384]{2,1,0:T(8,128)(2,1)}, u32[]{:S(2)}, u32[]{:S(2)}) collective-permute-start(bf16[64,192,384]{2,1,0:T(8,128)(2,1)} %get-tuple-element.103), channel_id=1, source_target_pairs={{0,4},{4,0},{1,5},{5,1},{2,6},{6,2},{3,7},{7,3},{8,12},{12,8},{9,1... | collective-permute-start | bytes 28311560 | tf_op jit(solution)/shard_map/ppermute | solution.py:678
  804.6 39.7 %collective-permute-start.11 = (bf16[1024,1536]{1,0:T(8,128)(2,1)}, bf16[1024,1536]{1,0:T(8,128)(2,1)}, u32[]{:S(2)}, u32[]{:S(2)}) collective-permute-start(bf16[1024,1536]{1,0:T(8,128)(2,1)} %convolution_convert_fusion.1), channel_id=1, source_target_pairs={{0,4},{4,0},{1,5},{5,1},{2,6},{6,2},{3,7},{7,3},{8,12},{12,8},{9,1... | collective-permute-start | bytes 9437192 | tf_op jit(solution)/shard_map/ppermute | solution.py:678
  810.3 19.6 %collective-permute-start.9 = (bf16[2,192,1536]{2,1,0:T(8,128)(2,1)}, bf16[2,192,1536]{2,1,0:T(8,128)(2,1)}, u32[]{:S(2)}, u32[]{:S(2)}) collective-permute-start(bf16[2,192,1536]{2,1,0:T(8,128)(2,1)} %get-tuple-element.332), channel_id=1, source_target_pairs={{0,4},{4,0},{1,5},{5,1},{2,6},{6,2},{3,7},{7,3},{8,12},{12,8},{9,1... | collective-permute-start | bytes 3538952 | tf_op jit(solution)/shard_map/ppermute | solution.py:678
  832.9 324.6 %reduce-scatter.17.cloned.1.call-start = ((), (), s32[]{:S(2)}) async-start(), calls=%async_computation.10 | async-start | bytes 2949120 | tf_op jit(solution)/shard_map/reduce_scatter | solution.py:1969
  843.8 7.0 collective-permute-start.10
  1155.4 4.2 collective-permute-start.12
  1157.1 3.8 collective-permute-start.13
  1160.8 23.4 %copy-start.94 = (bf16[48,128]{1,0:T(8,128)(2,1)S(1)}, bf16[48,128]{1,0:T(8,128)(2,1)}, u32[]{:S(2)}) copy-start(bf16[48,128]{1,0:T(8,128)(2,1)} %get-tuple-element.106) | copy-start | bytes 36868
  1166.8 3.9 collective-permute-start.14
  (124 other events, 742.2 us)
Sparse Core Ops, SparseCore 0:
  12.8 207.2 all-gather.4
  223.4 141.2 all-gather.6
  368.1 120.6 all-gather.8
  622.7 92.9 reduce-scatter.18
  718.7 95.0 reduce-scatter.20
  816.7 94.9 reduce-scatter.22
  914.0 48.0 reduce-scatter.12
  964.4 75.8 reduce-scatter.14
  1042.6 83.6 reduce-scatter.16

commit v5 on v4

--- a/solution.py
+++ b/solution.py
@@ -204,20 +204,19 @@
     return (first_moment, second_moment, weight)
 
 
-def shampoo_update(slots_now, gradient, rest, left_stat, right_stat, left_root, right_root):
-    share_now = (1.0 - STAT_DECAY) * rest * rest
-    left_stat = STAT_DECAY * left_stat + share_now * jnp.einsum(
-        "sij,skj->sik", gradient, gradient, precision=lax.Precision.HIGH
-    )
-    right_stat = STAT_DECAY * right_stat + share_now * jnp.einsum(
-        "sji,sjk->sik", gradient, gradient, precision=lax.Precision.HIGH
-    )
-    inner = jnp.einsum("sij,sjk->sik", gradient, right_root, precision=lax.Precision.HIGH)
-    direction = jnp.einsum("sij,sjk->sik", left_root, inner, precision=lax.Precision.HIGH)
+def shampoo_update(slots_now, gradient, left_stat, right_stat, left_root, right_root):
+    left_stat = STAT_DECAY * left_stat + (1.0 - STAT_DECAY) * jnp.einsum(
+        "sij,skj->sik", gradient, gradient, precision=BEST_PRECISION
+    )
+    right_stat = STAT_DECAY * right_stat + (1.0 - STAT_DECAY) * jnp.einsum(
+        "sji,sjk->sik", gradient, gradient, precision=BEST_PRECISION
+    )
+    inner = jnp.einsum("sij,sjk->sik", gradient, right_root, precision=BEST_PRECISION)
+    direction = jnp.einsum("sij,sjk->sik", left_root, inner, precision=BEST_PRECISION)
     return (
         left_stat,
         right_stat,
-        slots_now - SHAMPOO_RATE * (rest * direction + WEIGHT_DECAY * slots_now),
+        slots_now - SHAMPOO_RATE * (direction + WEIGHT_DECAY * slots_now),
     )
 
 
@@ -974,7 +973,161 @@
     )(values)
 
 
+def total_kernel(count, loss, *refs):
+    pieces, result = refs[:count], refs[count]
+    own_part, core_part, shared, send_sem, recv_sem = refs[count + 1 :]
+    row, column, core, line = coordinates()
+    own = 8 * row + 4 * column + line
+
+    def peer(offset):
+        return (row ^ (offset // 8), column ^ (offset // 4 % 2), core, line ^ (offset % 4))
+
+    peers = {offset: peer(offset) for offset in range(1, 16)}
+    peers[0] = (row, column, 1 - core, line)
+    greet(peers)
+    squares = jnp.zeros((1, 1), jnp.float32)
+    for piece in pieces:
+        value = piece[...].astype(jnp.float32)
+        value = jnp.sum(value * value, 0, keepdims=True)
+        squares = squares + jnp.sum(value, 1, keepdims=True)
+    lane = lax.broadcasted_iota(jnp.int32, (8, 128), 1)
+    own_part[...] = jnp.where(lane == 0, loss[0:1, 0:1], jnp.where(lane == 1, squares, 0.0))
+    across = send(own_part, core_part, send_sem.at[0], recv_sem.at[0], peers[0])
+    across.start()
+    across.wait()
+    own_part[...] = own_part[...] + core_part[...]
+    copies = [
+        send(own_part, shared.at[own], send_sem.at[offset], recv_sem.at[offset], peers[offset])
+        for offset in range(1, 16)
+    ]
+    for copy in copies:
+        copy.start()
+    shared[own] = own_part[...]
+    for copy in copies:
+        copy.wait()
+    total = shared[0]
+    for index_value in range(1, 16):
+        total = total + shared[index_value]
+    result[...] = total
+
+
+def total_squares(loss, pieces, collective_id):
+    vmem, dma = pltpu.VMEM, pltpu.SemaphoreType.DMA
+    tile = (8, 128)
+    return pl.pallas_call(
+        partial(total_kernel, len(pieces)),
+        out_shape=jax.ShapeDtypeStruct(tile, jnp.float32),
+        in_specs=[pl.BlockSpec(memory_space=vmem)] * (len(pieces) + 1),
+        out_specs=pl.BlockSpec(memory_space=vmem),
+        scratch_shapes=[
+            vmem(tile, jnp.float32),
+            vmem(tile, jnp.float32),
+            vmem((16,) + tile, jnp.float32),
+            dma((16,)),
+            dma((16,)),
+        ],
+        compiler_params=pltpu.CompilerParams(
+            collective_id=collective_id, has_side_effects=True, vmem_limit_bytes=48 * 2**20
+        ),
+    )(jnp.broadcast_to(loss, tile), *pieces)
+
+
+def exact_dot(left, right, dims):
+    return lax.dot_general(
+        left,
+        right,
+        (dims, ((), ())),
+        precision=BEST_PRECISION,
+        preferred_element_type=jnp.float32,
+    )
+
+
+def shampoo_kernel(factor, pair, slots, left, right, left_root, right_root, *outs):
+    clipped, new_left, new_right, new_slots = outs
+    both = pair[0].astype(jnp.float32) * factor[0, 0]
+    for side in range(2):
+        grad = (pltpu.roll(both, BLK, 1) if side else both)[:, :BLK]
+        clipped[side] = grad
+        new_left[side] = STAT_DECAY * left[side] + (1.0 - STAT_DECAY) * exact_dot(
+            grad, grad, ((1,), (1,))
+        )
+        new_right[side] = STAT_DECAY * right[side] + (1.0 - STAT_DECAY) * exact_dot(
+            grad, grad, ((0,), (0,))
+        )
+        inner = exact_dot(grad, right_root[side], ((1,), (0,)))
+        direction = exact_dot(left_root[side], inner, ((1,), (0,)))
+        new_slots[side] = slots[side] - SHAMPOO_RATE * (direction + WEIGHT_DECAY * slots[side])
+
+
+def shampoo_pairs(factor, pairs, slots, *statistics):
+    steps = pairs.shape[0]
+    block = pl.BlockSpec((2, BLK, BLK), lambda step: (step, 0, 0))
+    return pl.pallas_call(
+        shampoo_kernel,
+        grid=(steps,),
+        in_specs=[
+            pl.BlockSpec(memory_space=pltpu.SMEM),
+            pl.BlockSpec((1, BLK, 2 * BLK), lambda step: (step, 0, 0)),
+        ]
+        + [block] * 5,
+        out_specs=[block] * 4,
+        out_shape=[jax.ShapeDtypeStruct(slots.shape, jnp.float32)] * 4,
+        cost_estimate=pl.CostEstimate(
+            flops=96 * steps * BLK**3, bytes_accessed=40 * slots.size, transcendentals=0
+        ),
+    )(factor.reshape(1, 1), pairs, slots, *statistics)
+
+
+NORM_ROWS = 128
+
+
+def norm_back_kernel(mine, other, normed, inverse, gain, rest, *outs):
+    grad_low, gain_out = outs[-2:]
+    total = mine[...].astype(jnp.float32) + other[...].astype(jnp.float32)
+    row = normed[...]
+
+    @pl.when(pl.program_id(0) == 0)
+    def clear():
+        gain_out[...] = jnp.zeros_like(gain_out)
+
+    gain_out[0:1, :] += jnp.sum(total * row, 0, keepdims=True)
+    scaled = total * gain[0:1, :]
+    grad = scaled - jnp.mean(scaled, -1, keepdims=True)
+    grad = inverse[...] * (grad - row * jnp.mean(scaled * row, -1, keepdims=True))
+    grad = grad + rest[...]
+    grad_low[...] = grad.astype(grad_low.dtype)
+    if len(outs) == 3:
+        outs[0][...] = grad
+
+
+def norm_back(partial_sum, normed, inverse, gain, rest, keep):
+    low = partial_sum.astype(jnp.bfloat16)
+    rows, width = rest.shape
+
+    def block(columns):
+        return pl.BlockSpec((NORM_ROWS, columns), lambda step: (step, 0))
+
+    fixed = pl.BlockSpec((8, width), lambda step: (0, 0))
+    wide = [jax.ShapeDtypeStruct((rows, width), jnp.float32)] if keep else []
+    outs = pl.pallas_call(
+        norm_back_kernel,
+        grid=(rows // NORM_ROWS,),
+        in_specs=[block(width)] * 3 + [block(1), fixed, block(width)],
+        out_specs=[block(width)] * (len(wide) + 1) + [fixed],
+        out_shape=wide
+        + [
+            jax.ShapeDtypeStruct((rows, width), jnp.bfloat16),
+            jax.ShapeDtypeStruct((8, width), jnp.float32),
+        ],
+        cost_estimate=pl.CostEstimate(
+            flops=16 * rows * width, bytes_accessed=18 * rows * width, transcendentals=0
+        ),
+    )(low, swap(low, "c"), normed, inverse, jnp.broadcast_to(gain, (8, width)), rest)
+    return (*outs[:-1], outs[-1][0])
+
+
 FEED_TILE = 256
+UP_LOW = 768
 FEED_ROWS = 512
 
 
@@ -1013,19 +1166,30 @@
 
 
 def rows_back_kernel(
-    turned_rows, grad_gate, grad_up, gate_tile, up_tile, gate_out, up_out, rows_out, total
+    turned_rows, grad_gate, grad_up, gate_tile, up_tile, gate_out, up_low, up_high, rows_out, total
 ):
     @pl.when(pl.program_id(0) == 0)
     def clear():
         total[...] = jnp.zeros_like(total)
 
+    is_low = pl.program_id(0) < UP_LOW // FEED_TILE
+
     def body(at):
         gate_out[at, :] = jnp.dot(
             turned_rows[at, :], grad_gate[...], preferred_element_type=jnp.float32
         ).astype(gate_out.dtype)
-        up_out[at, :] = jnp.dot(
+        up_part = jnp.dot(
             turned_rows[at, :], grad_up[...], preferred_element_type=jnp.float32
-        ).astype(up_out.dtype)
+        ).astype(up_low.dtype)
+
+        @pl.when(is_low)
+        def store_low():
+            up_low[at, :] = up_part
+
+        @pl.when(jnp.logical_not(is_low))
+        def store_high():
+            up_high[at, :] = up_part
+
         total[:, at] += dot_back(grad_gate[...], gate_tile[at, :]) + dot_back(
             grad_up[...], up_tile[at, :]
         )
@@ -1046,6 +1210,14 @@
             return pl.BlockSpec((height, FEED_TILE), lambda step: (0, step))
         if kind == "rows":
             return pl.BlockSpec((FEED_TILE, width), lambda step: (step, 0))
+        if kind == "low":
+            last = width // FEED_TILE - 1
+            return pl.BlockSpec((height, FEED_TILE), lambda step: (0, jnp.minimum(step, last)))
+        if kind == "high":
+            first = (units - width) // FEED_TILE
+            return pl.BlockSpec(
+                (height, FEED_TILE), lambda step: (0, jnp.maximum(step - first, 0))
+            )
         return pl.BlockSpec(shape, lambda step: (0, 0))
 
     low = jnp.bfloat16
@@ -1098,7 +1270,12 @@
             (gate_weight, "columns"),
             (up_weight, "columns"),
         ],
-        [(gate_weight.shape, "columns"), (up_weight.shape, "columns"), (rows.shape, "whole")],
+        [
+            (gate_weight.shape, "columns"),
+            ((D, UP_LOW), "low"),
+            ((D, FF // 2 - UP_LOW), "high"),
+            (rows.shape, "whole"),
+        ],
         8 * rows.size * (FF // 2),
         [pltpu.VMEM(rows.shape, jnp.float32)],
     )
@@ -1109,13 +1286,7 @@
     flat = [unit for group in groups for unit in group]
     total = len(flat)
     sources = refs[:count]
-    outputs = sum(2 if kind == "cols" else 1 for kind, _ in arrays)
-    targets, at = [], count
-    for kind, _ in arrays:
-        width = 2 if kind == "cols" else 1
-        targets.append(refs[at : at + width])
-        at += width
-    scratch = refs[at:]
+    targets, scratch = refs[count : 2 * count], refs[2 * count :]
     sides, onwards, mines, from_ons, from_lines, from_cores = (
         scratch[index_value * total : (index_value + 1) * total] for index_value in range(6)
     )
@@ -1180,6 +1351,13 @@
             recv_sem.at[number, 6],
             peers["c"],
         )
+
+    def side_columns(number, side):
+        array, _, _, columns = flat[number]
+        width = arrays[array][1][1]
+        start = 0 if isinstance(columns, slice) else columns.start
+        at = pl.multiple_of(side * width + start, 128)
+        return pl.ds(at, extent(columns, width))
 
     def is_cols(number):
         return arrays[flat[number][0]][0] == "cols"
@@ -1232,15 +1410,15 @@
             mine[side, line] = value.astype(mine.dtype)
         if is_cols(number):
             core_copy(number).start()
-            targets[array][0][rows, columns] = mine[core, line]
+            targets[array][rows, side_columns(number, core)] = mine[core, line]
         else:
-            targets[array][0][rows, columns] = mine[0, line]
+            targets[array][rows, columns] = mine[0, line]
 
     def stage_five(number):
         if is_cols(number):
             core_copy(number).wait()
-            array, _, rows, columns = flat[number]
-            targets[array][1][rows, columns] = from_cores[number][...]
+            array, _, rows, _ = flat[number]
+            targets[array][rows, side_columns(number, 1 - core)] = from_cores[number][...]
         first_copy(number, 0).wait_send()
         first_copy(number, 1).wait_send()
         onward_copy(number).wait_send()
@@ -1275,9 +1453,10 @@
         scratch += [vmem((c, 4, h, w), low) for c, h, w in shapes]
     scratch += [vmem((3, c, h, w), low) for c, h, w in shapes]
     scratch += [vmem((h, w) if c == 2 else (16, 128), low) for c, h, w in shapes]
-    out_shape = []
-    for kind, shape in arrays:
-        out_shape += [jax.ShapeDtypeStruct(shape, low)] * (2 if kind == "cols" else 1)
+    out_shape = [
+        jax.ShapeDtypeStruct((height, width * (2 if kind == "cols" else 1)), low)
+        for kind, (height, width) in arrays
+    ]
     return pl.pallas_call(
         partial(reduce_kernel, arrays, groups),
         out_shape=out_shape,
@@ -1764,13 +1943,13 @@
     gate_weight, up_weight = (gathered(block).reshape(D, FF // 2) for block in feed_blocks)
     down = gathered(low_down).reshape(FF // 2, D)
     arrays = (
-        ("cols", (16, D), bf16),
+        ("both", (16, D), bf16),
         ("both", (4 * BLK, 2 * BLK), bf16),
         ("cols", (48, half), bf16),
         ("half", (48, D), bf16),
         ("cols", (16, 1152), bf16),
         ("cols", (16, 1152), bf16),
-        ("cols", (48, 2 * DIN), bf16),
+        ("both", (48, 2 * DIN), bf16),
     )
     whole = slice(None)
     groups = [((0, 0, whole, whole), (5, 1, whole, whole), (6, 1, whole, whole))]
@@ -1798,7 +1977,6 @@
         groups,
         (
             pack,
-            pack,
             low_pairs,
             head_columns(low_cross[:, 0, :], 0, core),
             head_columns(low_cross[:, 0, :], 0, 1 - core),
@@ -1807,7 +1985,6 @@
             kv_block(0, 1 - core),
             kv_block(1, core),
             kv_block(1, 1 - core),
-            low_ends,
             low_ends,
         ),
         (jnp.concatenate([latents, noise_field], 2), text_tokens),
@@ -1953,7 +2130,7 @@
     grad_output = dot_back(grad_predicted, weight_out) + grad_audio[None, :] / FRAMES
     grad_low = grad_output.astype(bf16)
     grad_gate, grad_up, grad_down = hidden_back(grad_low, down, gate_part, up_part, hidden)
-    grad_gate_weight, grad_up_weight, grad_feed_rows = rows_back(
+    grad_gate_weight, grad_up_low, grad_up_high, grad_feed_rows = rows_back(
         feed_rows, grad_gate, grad_up, gate_weight, up_weight
     )
 
@@ -1968,28 +2145,15 @@
     def over_line(total):
         return lax.psum_scatter(total, "z", scatter_dimension=1, tiled=True)[0, 0]
 
-    totals = [
-        over_plane(gradient, width)
-        for gradient, width in ((grad_down, 192), (grad_gate_weight, 48), (grad_up_weight, 48))
-    ]
-    down_total, *gate_totals = [over_line(total) for total in totals]
-    feed_sums = [
-        (pick(both_rows, core), swap(pick(both_rows, 1 - core), "c")) for both_rows in gate_totals
-    ]
-    gate_columns = []
-    for mine, other in feed_sums:
-        sides = (jnp.where(core == 0, mine, other), jnp.where(core == 0, other, mine))
-        for quadrant in quads:
-            for side in sides:
-                gate_columns.append(side[:, quadrant * 768 : (quadrant + 1) * 768])
-    grad_gate_up = jnp.concatenate(gate_columns, 1).astype(f32)
-    grad_down = down_total[0].astype(f32)
-    grad_input_three = on_both(dot_back(grad_feed_rows, reorder))
-    grad_after_cross, gain_three = layer_back(
-        grad_input_three, normed_three, inverse_three, gain_values[2]
-    )
-    grad_after_cross = grad_after_cross + grad_output
-    grad_cross_in = grad_after_cross.astype(bf16)
+    down_total = over_plane(grad_down, 192)
+    grad_after_cross, grad_cross_in, gain_three = norm_back(
+        dot_back(grad_feed_rows, reorder),
+        normed_three,
+        inverse_three,
+        gain_values[2],
+        grad_output,
+        True,
+    )
     cross_rows = tdot(cross_flat, grad_cross_in).astype(bf16).reshape(2, 2, 192, D)
     cross_kept = pick(cross_rows, core, 1)
     cross_received = swap(pick(cross_rows, 1 - core, 1), "c")
@@ -2035,6 +2199,22 @@
         grad_mixed_self,
         (cosine_table, sine_table),
     )
+    grad_gate_weight, down_total, _ = lax.optimization_barrier(
+        (grad_gate_weight, down_total, grad_cross_in)
+    )
+    gate_total = over_plane(grad_gate_weight, 48)
+    grad_up_high, gate_total, _ = lax.optimization_barrier(
+        (grad_up_high, gate_total, grad_queries)
+    )
+    up_total = over_plane(grad_up_high, 48)
+    gate_total, up_total = lax.optimization_barrier((gate_total, up_total))
+    down_total, *gate_totals = [
+        over_line(total) for total in (down_total, gate_total, up_total)
+    ]
+    feed_sums = [
+        (pick(both_rows, core), swap(pick(both_rows, 1 - core), "c")) for both_rows in gate_totals
+    ]
+    grad_down_low = down_total[0]
     grad_joined = jnp.concatenate([grad_queries, grad_keys, grad_values], 1)
     grad_time_pair = jnp.concatenate([grad_time_keys[:1], grad_time_values[:1]], 1)
     time_row = jnp.concatenate([jnp.zeros((1, half), f32), grad_time_pair], 1)
@@ -2058,15 +2238,17 @@
         code.astype(jnp.int32),
     )
     slot_sums = low_sum(near_slots, swap(far_slots, "c")).astype(bf16)
+    slot_sums, grad_down_low = lax.optimization_barrier((slot_sums, grad_down_low))
     slot_sums = slot_sums.reshape(4, 1, 4, 4 * BLK, 2 * BLK)
 
     partial_one = dot_back(grad_joined, projection)
     partial_time = jnp.dot(
         grad_time_pair, projection[:, half:].astype(f32).T, precision=BEST_PRECISION
     )
-    grad_input_one = on_both(partial_one)
     grad_input_time = partial_time + swap(partial_time, "c")
-    grad_residual, gain_one = layer_back(grad_input_one, normed_one, inverse_one, gain_values[0])
+    grad_residual, gain_one = layer_back(
+        on_both(partial_one), normed_one, inverse_one, gain_values[0]
+    )
     grad_residual = (grad_residual + grad_after_self).astype(bf16)
     grad_embeds, gain_time = layer_back(
         grad_input_time, normed_time, inverse_time, gain_values[0]
@@ -2099,8 +2281,12 @@
         ("cols", (16, 1152)),
         ("one", (16, D)),
         ("one", (48, 2 * DIN)),
-    )
-    rest_groups = [((3, 0, whole, whole), (4, 1, whole, whole))]
+        ("one", (96, UP_LOW)),
+    )
+    rest_groups = [
+        ((7, 0, whole, pl.ds(0, UP_LOW // 2)), (7, 1, whole, pl.ds(UP_LOW // 2, UP_LOW // 2)))
+    ]
+    rest_groups += [((3, 0, whole, whole), (4, 1, whole, whole))]
     rest_groups += [
         ((1, 0, whole, pl.ds(step * 384, 384)), (2, 1, whole, pl.ds(step * 768, 768)))
         for step in range(2)
@@ -2121,25 +2307,30 @@
             kv_sources[1],
             small.astype(bf16).reshape(4, 1, 4, 16, D),
             grad_ends.reshape(4, 1, 4, 48, 2 * DIN),
+            grad_up_low.reshape(4, 1, 4, 96, UP_LOW),
         ),
         2,
     )
-    slot_rows, query_mine, query_other, grad_cross_out, *kv_sums, small, grad_ends = (
-        value.astype(f32) for value in rest_sums
-    )
-    slot_rows = slot_rows.reshape(4, BLK, 2 * BLK)
-    grad_slots = jnp.stack([slot_rows[:, :, :BLK], slot_rows[:, :, BLK:]], 1).reshape(8, BLK, BLK)
-    grad_cross_query = jnp.where(
-        core == 0,
-        jnp.concatenate([query_mine, query_other], 1),
-        jnp.concatenate([query_other, query_mine], 1),
-    )
+    grad_down = grad_down_low.astype(f32)
+    up_sums = rest_sums[-1].reshape(2, 48, UP_LOW)
+    slot_pairs = rest_sums[0].reshape(4, BLK, 2 * BLK)
+    grad_cross_query, grad_cross_out, *kv_sums, small, grad_ends = (
+        value.astype(f32) for value in rest_sums[1:-1]
+    )
+    gate_sides, (up_own, up_other) = feed_sums
+    up_own = jnp.concatenate([pick(up_sums, core), up_own], 1)
+    up_other = jnp.concatenate([swap(pick(up_sums, 1 - core), "c"), up_other], 1)
+    gate_columns = []
+    for mine, other in (gate_sides, (up_own, up_other)):
+        sides = (jnp.where(core == 0, mine, other), jnp.where(core == 0, other, mine))
+        for quadrant in quads:
+            for side in sides:
+                gate_columns.append(side[:, quadrant * 768 : (quadrant + 1) * 768])
+    grad_gate_up = jnp.concatenate(gate_columns, 1).astype(f32)
     grad_cross = jnp.stack([grad_cross_query, grad_cross_out], 1)
     kv_columns = []
-    for mine, other in (kv_sums[:2], kv_sums[2:]):
-        mine, other = mine.reshape(24, half), other.reshape(24, half)
-        kv_columns.append(jnp.where(core == 0, mine, other))
-        kv_columns.append(jnp.where(core == 0, other, mine))
+    for pair in kv_sums:
+        kv_columns += [pair[:, :1152].reshape(24, half), pair[:, 1152:].reshape(24, half)]
     grad_key_value = jnp.concatenate(kv_columns, 1)
     grad_ends = grad_ends.reshape(48, 2, DIN)
     grad_table = small[:8]
@@ -2148,22 +2339,22 @@
     reduced = (
         grad_ends,
         grad_table,
-        grad_slots,
+        slot_pairs,
         grad_cross,
         grad_key_value,
         grad_gate_up,
         grad_down,
         grad_gains,
     )
-    square_sum = jnp.zeros((), f32)
-    for member in reduced:
-        square_sum = square_sum + jnp.sum(member * member)
     loss_part = jnp.where(
         core == 0,
         jnp.sum(errors * errors) * mse_scale + contrast_own * (CONTRAST_WEIGHT / items_total),
         0.0,
     )
-    loss_total, norm_square = all_sum(loss_part, square_sum)
+    totals = total_squares(
+        loss_part, (*rest_sums[:-1], *gate_sides, up_own, up_other, grad_down_low), 4
+    )
+    loss_total, norm_square = totals[0, 0], totals[0, 1]
     return finish(
         loss_total,
         jnp.sqrt(norm_square),
@@ -2202,12 +2393,6 @@
     )
 
 
-def all_sum(*values):
-    total = jnp.pad(jnp.stack(values)[None], ((0, 7), (0, 128 - len(values))))
-    total = jnp.sum(share(total + swap(total, "c"), 4), 0)
-    return total[0, 0], total[0, 1]
-
-
 def finish(loss_total, gradient_norm, reduced, masters, firsts, seconds, statistics):
     factor = CLIP_NORM / jnp.maximum(gradient_norm, CLIP_NORM)
     results = [loss_total, gradient_norm]
@@ -2221,12 +2406,12 @@
                 ADAM_RATES[index_value],
             )
         )
-    slot_norm = jnp.sqrt(jnp.sum(reduced[2] * reduced[2]))
-    slot_factor = CLIP_NORM / jnp.maximum(slot_norm, CLIP_NORM)
-    left_new, right_new, slots_new = shampoo_update(
-        masters[2], slot_factor * reduced[2], factor / slot_factor, *statistics
-    )
-    results.extend([factor * reduced[2], left_new, right_new, slots_new])
+    if reduced[2].dtype == jnp.bfloat16:
+        results.extend(shampoo_pairs(factor, reduced[2], masters[2], *statistics))
+    else:
+        clipped_slots = factor * reduced[2]
+        results.append(clipped_slots)
+        results.extend(shampoo_update(masters[2], clipped_slots, *statistics))
     return tuple(results)
 
 

time: 1230 us -> 1160 us (0.943)
  other arithmetic: 137 us -> 101 us
  waiting for transfers between devices: 67 us -> 48.6 us
  matrix products: 136 us -> 119 us
    unnamed x12 -> x9, waiting for transfers between devices: 48.5 us -> 0.15 us
    pallas_call x0 -> x3, Pallas kernels: none -> 33.6 us  [the longest x1 13.8 us: norm_back(): pl.pallas_call(norm_back_kernel, grid=(rows // NORM_ROWS,), in_specs=[blo...]
    pallas_call x1, Pallas kernels: 208 us -> 191 us  [reduce_gradients(): pl.pallas_call(partial(reduce_kernel, arrays, groups), out_shape=out_shap...]
    optimization_barrier x0 -> x3, waiting for transfers between devices: none -> 16.1 us  [the longest x1 9.59 us: item_per_chip(): lax.optimization_barrier((grad_gate_weight, down_total, grad_cross_in))]
    unnamed x294 -> x298, local copies, waits for them, and re-layouts: 33.2 us -> 28 us
  transfers between devices with their start and end apart: 24 -> 24, of which waited for: 8 -> 9; matrix products, arithmetic and copies ran while one was open for 22% -> 19% of each run, Pallas kernels for 54% -> 62%
where the time goes in v5:
time: 1160 us
  Pallas kernels  773 us (67%)
  matrix products  119 us (10%)
  other arithmetic  101 us (9%)
  local copies, waits for them, and re-layouts  85.7 us (7%)
  waiting for transfers between devices  48.6 us (4%)
  between operations  24.2 us (2%)
    pallas_call x1, Pallas kernels, gather_weights(): pl.pallas_call(partial(gather_kernel, arrays, groups), out_shape=[jax.Sha...  265 us
    pallas_call x1, Pallas kernels, reduce_gradients(): pl.pallas_call(partial(reduce_kernel, arrays, groups), out_shape=out_shap...  191 us
    pallas_call x3, Pallas kernels, feed_call(): pl.pallas_call(kernel, grid=(units // FEED_TILE,), in_specs=[spec(value.s...  111 us
    pallas_call x2, Pallas kernels, attend_back(): pl.pallas_call(partial(attend_back_kernel, timed), grid=(pairs,), in_spec...  58.5 us
    pallas_call x2, Pallas kernels, attend(): pl.pallas_call(partial(attend_kernel, timed), grid=(pairs,), in_specs=[la...  41 us
    dot_general x7, matrix products, dot_back(): lax.dot_general(left, right, (((1,), (1,)), ((), ())), preferred_element_...  40.8 us
    dot_general x8, matrix products, tdot(): lax.dot_general(left, right, (((0,), (0,)), ((), ())), preferred_element_...  36.9 us
    unnamed x298, local copies, waits for them, and re-layouts  28 us
  transfers between devices with their start and end apart: 24, of which 9 were waited for; matrix products, arithmetic and copies ran while one was open for 19% of the time, Pallas kernels for 62%

profile of v5, /device:TPU:0, one launch (start us, length us, event | category | flops | bytes accessed | tf_op | source)
XLA Modules:
  0.0 1155.5 jit_solution(6381800248680232520)
XLA Ops:
  26.5 264.7 %shard_map.520 = (bf16[4,2,4,16,1536]{4,3,2,1,0:T(8,128)(2,1)}, bf16[4,2,4,768,384]{4,3,2,1,0:T(8,128)(2,1)}, bf16[4,2,4,48,768]{4,3,2,1,0:T(8,128)(2,1)}, bf16[...) custom-call(bf16[16,1536]{1,0:T(8,128)(2,1)} %fusion.54.refs_0_, ...), custom_call_target="tpu_custom_call" | custom-call | tf_op jit(solution)/shard_map/pallas_call | solution.py:920
  313.2 16.2 %shard_map.521 = (bf16[1536,2304]{1,0:T(8,128)(2,1)}, bf16[768,1536]{1,0:T(8,128)(2,1)S(1)}) custom-call(s32[96]{0:T(128)S(1)} %gather_fusion, s32[32]{0:T(128)S(1)} %gather_fusion.1, bf16[128,192,384]{2,1,0:T(8,128)(2,1)} %bitcast.178), custom_call_target="tpu_custom_call" | custom-call | bytes 28311552 | tf_op jit(solution)/shard_map/pallas_call | solution.py:1770
  329.4 19.2 %shard_map.522 = (bf16[1024,2304]{1,0:T(8,128)(2,1)}, bf16[16,2304]{1,0:T(8,128)(2,1)S(1)}) custom-call(bf16[1024,1536]{1,0:T(8,128)(2,1)S(1)} %multiply_convert_fusion.2.rows, bf16[16,1536]{1,0:T(8,128)(2,1)S(1)} %pad.21.times, bf16[1536,2304]{1,0:T(8,128)(2,1)} %get-tuple-element.91.weights, f32[1024,128]{1,0:T(8,128)S(1)} %pad_maximum_fusion.3.cosine.refs_8_, ...), custom_call_target="tpu_custom_call" | custom-call | flops 7247757312 | bytes 14942208 | tf_op jit(solution)/shard_map/pallas_call | solution.py:1516
  348.7 30.9 %shard_map.523 = (bf16[1024,768]{1,0:T(8,128)(2,1)S(1)}, f32[1024,768]{1,0:T(8,128)S(1)}) custom-call(bf16[1024,2304]{1,0:T(8,128)(2,1)} %get-tuple-element.92.queries.keys.values.refs_0_.refs_1_.refs_2_, bf16[1024,2304]{1,0:T(8,128)(2,1)} %get-tuple-element.92.queries.keys.values.refs_0_.refs_1_.refs_2_, ...), custom_call_target="tpu_custom_call" | custom-call | flops 19327352832 | bytes 11010048 | tf_op jit(solution)/shard_map/pallas_call | solution.py:1601
  405.3 10.1 shard_map.524
  435.5 5.8 fusion.10
  444.6 26.2 %shard_map.525 = (bf16[1024,3072]{1,0:T(8,128)(2,1)}, bf16[1024,3072]{1,0:T(8,128)(2,1)}, bf16[1024,3072]{1,0:T(8,128)(2,1)}) custom-call(bf16[1024,1536]{1,0:T(8,128)(2,1)} %copy.197.rows, bf16[1536,3072]{1,0:T(8,128)(2,1)} %bitcast.215, bf16[1536,3072]{1,0:T(8,128)(2,1)} %bitcast.217), custom_call_target="tpu_custom_call" | custom-call | flops 19327352832 | bytes 40894464 | tf_op jit(solution)/shard_map/pallas_call | solution.py:1225
  470.9 13.1 %all-gather.9.cloned.1.call-done.down_tile = bf16[3072,1536]{1,0:T(8,128)(2,1)} async-done(((bf16[192,1536]{1,0:T(8,128)(2,1)}), bf16[3072,1536]{1,0:T(8,128)(2,1)}) %all-gather.9.cloned.1.call-update) | async-done | bytes 9437200 | tf_op jit(solution)/shard_map/all_gather | solution.py:1935
  484.0 14.0 %convolution_convert_fusion = bf16[1024,1536]{1,0:T(8,128)(2,1)S(1)} fusion(bf16[1024,3072]{1,0:T(8,128)(2,1)} %get-tuple-element.102.hidden, bf16[3072,1536]{1,0:T(8,128)(2,1)} %all-gather.9.cloned.1.call-done.down_tile), kind=kOutput, calls=%fused_computation.38 | convolution fusion | flops 9665249280 | bytes 18874368 | tf_op jit(solution)/shard_map/dot_general | solution.py:2080
  505.1 6.1 fusion.14
  513.2 11.1 shard_map.526
  545.1 29.0 %shard_map.527 = (bf16[1024,3072]{1,0:T(8,128)(2,1)}, bf16[1024,3072]{1,0:T(8,128)(2,1)}, bf16[3072,1536]{1,0:T(8,128)(2,1)}) custom-call(bf16[1024,1536]{1,0:T(8,128)(2,1)} %get-tuple-element.419.grad, bf16[3072,1536]{1,0:T(8,128)(2,1)} %all-gather.9.cloned.1.call-done.down_tile, bf16[1024,3072]{1,0:T(8,128)(2,1)} %get-tuple-element.105.gate, ...), custom_call_target="tpu_custom_call" | custom-call | flops 19327352832 | bytes 53477376 | tf_op jit(solution)/shard_map/pallas_call | solution.py:1225
  574.2 55.8 %shard_map.528 = (bf16[1536,3072]{1,0:T(8,128)(2,1)}, bf16[1536,768]{1,0:T(8,128)(2,1)}, bf16[1536,2304]{1,0:T(8,128)(2,1)}, bf16[1024,1536]{1,0:T(8,128)(2,1)}) custom-call(bf16[1536,1024]{1,0:T(8,128)(2,1)} %bitcast.186, bf16[1024,3072]{1,0:T(8,128)(2,1)} %get-tuple-element.107.grad_gate, bf16[1024,3072]{1,0:T(8,128)(2,1)} %get-tuple-element.108.grad_up, ...), custom_call_target="tpu_custom_call" | custom-call | flops 38654705664 | bytes 56623104 | tf_op jit(solution)/shard_map/pallas_call | solution.py:1225
  630.0 7.5 fusion.11.mine
  644.1 13.8 %shard_map.529 = (f32[1024,1536]{1,0:T(8,128)}, bf16[1024,1536]{1,0:T(8,128)(2,1)}, f32[8,1536]{1,0:T(8,128)}) custom-call(bf16[1024,1536]{1,0:T(8,128)(2,1)} %copy-done.54, bf16[1024,1536]{1,0:T(8,128)(2,1)} %collective-permute-done.6.other, f32[1024,1536]{1,0:T(8,128)} %copy-done.44, f32[1024,1]{1,0:T(8,128)} %copy.202.inverse, ...), custom_call_target="tpu_custom_call" | custom-call | flops 25165824 | bytes 28311552 | tf_op jit(solution)/shard_map/pallas_call | solution.py:1112
  657.9 9.6 reduce-scatter.19.cloned.1.call-done
  667.6 6.5 fusion.24.refs_7_
  674.2 12.7 %shard_map.530 = (bf16[1024,768]{1,0:T(8,128)(2,1)S(1)}, f32[128,768]{1,0:T(8,128)S(1)}, f32[128,768]{1,0:T(8,128)S(1)}) custom-call(bf16[1024,768]{1,0:T(8,128)(2,1)S(1)} %copy-done.31, bf16[128,1536]{1,0:T(8,128)(2,1)S(1)} %convolution_convert_fusion.8.keys.values.refs_1_.refs_2_, ...), custom_call_target="tpu_custom_call" | custom-call | flops 6039797760 | bytes 13369344 | tf_op jit(solution)/shard_map/pallas_call | solution.py:1728
  710.8 45.8 %shard_map.531 = (bf16[1024,768]{1,0:T(8,128)(2,1)S(1)}, bf16[1024,768]{1,0:T(8,128)(2,1)S(1)}, bf16[1024,768]{1,0:T(8,128)(2,1)S(1)}, f32[8,768]{1,0:T(8,128)S(1)}, f32[8,768]{1,0:T(8,128)S(1)}) custom-call(bf16[1024,2304]{1,0:T(8,128)(2,1)} %get-tuple-element.92.queries.keys.values.refs_0_.refs_1_.refs_2_, ...), custom_call_target="tpu_custom_call" | custom-call | flops 48318382080 | bytes 18874368 | tf_op jit(solution)/shard_map/pallas_call | solution.py:1728
  759.0 6.5 reduce-scatter.21.cloned.1.call-done
  792.9 9.6 add_convert_fusion.1.joined
  802.5 5.9 convolution_convert_fusion.7.mix
  808.4 26.3 %shard_map.532 = (bf16[64,192,384]{2,1,0:T(8,128)(2,1)}, bf16[64,192,384]{2,1,0:T(8,128)(2,1)}) custom-call(s32[256]{0:T(256)S(1)} %get-tuple-element.410.rows_at, s32[256]{0:T(256)S(1)} %get-tuple-element.409.columns_at, s32[256]{0:T(256)S(1)} %get-tuple-element.349.sides, bf16[1536,2304]{1,0:T(8,128)(2,1)} %add_convert_fusion.1.joined, ...), custom_call_target="tpu_custom_call" | custom-call | bytes 56623104 | tf_op jit(solution)/shard_map/pallas_call | solution.py:1834
  835.7 11.6 %convolution_convert_fusion.1 = bf16[1024,1536]{1,0:T(8,128)(2,1)} fusion(bf16[1024,2304]{1,0:T(8,128)(2,1)S(1)} %copy-done.74, bf16[1536,2304]{1,0:T(8,128)(2,1)} %get-tuple-element.91.weights), kind=kOutput, calls=%fused_computation.41 | convolution fusion | flops 7249330176 | bytes 14942208 | tf_op jit(solution)/shard_map/dot_general | solution.py:701
  857.6 6.1 convolution_convert_fusion.6
  867.2 6.1 fusion.6
  873.5 6.2 multiply_reduce_fusion
  880.6 8.0 fusion.20
  892.3 12.0 %add_convert_fusion = bf16[64,192,384]{2,1,0:T(8,128)(2,1)} fusion(bf16[64,192,384]{2,1,0:T(8,128)(2,1)} %collective-permute-done.8, bf16[64,192,384]{2,1,0:T(8,128)(2,1)} %get-tuple-element.118), kind=kLoop, calls=%fused_computation.4 | loop fusion | flops 18874368 | bytes 28311552 | tf_op jit(solution)/shard_map/convert_element_type | solution.py:2240
  904.3 190.9 %shard_map.533 = (bf16[768,384]{1,0:T(8,128)(2,1)}, bf16[48,1536]{1,0:T(8,128)(2,1)}, bf16[48,1536]{1,0:T(8,128)(2,1)}, bf16[16,2304]{1,0:T(8,128)(2,1)}, bf16[1...) custom-call(bf16[4,1,4,768,384]{4,3,2,1,0:T(8,128)(2,1)} %bitcast.177, ...), custom_call_target="tpu_custom_call" | custom-call | tf_op jit(solution)/shard_map/pallas_call | solution.py:1460
  1104.7 9.9 shard_map.534
  1137.6 9.8 shard_map.535
  (578 shorter events, 224.1 us)
Async XLA Ops:
  7.2 437.4 %all-gather.5.cloned.1.call-start = ((), (), s32[]{:S(2)}) async-start(), calls=%async_computation.6 | async-start | bytes 10027008 | tf_op jit(solution)/shard_map/all_gather | solution.py:1935
  9.3 1.7 collective-permute-start.2
  11.9 432.7 %all-gather.7.cloned.1.call-start = ((), (), s32[]{:S(2)}) async-start(), calls=%async_computation.7 | async-start | bytes 10027008 | tf_op jit(solution)/shard_map/all_gather | solution.py:1935
  12.0 1.6 collective-permute-start.3
  14.6 469.4 %all-gather.9.cloned.1.call-start = ((), (), s32[]{:S(2)}) async-start(), calls=%async_computation.11 | async-start | bytes 10027008 | tf_op jit(solution)/shard_map/all_gather | solution.py:1935
  15.5 651.9 %reduce-scatter.19.cloned.1.call-start = ((), (), s32[]{:S(2)}) async-start(), calls=%async_computation.12 | async-start | bytes 11796480
  23.2 271.1 %copy-start.37 = (s32[256]{0:T(256)S(1)}, s32[256]{0:T(256)}, u32[]{:S(2)}) copy-start(s32[256]{0:T(256)} %param.39) | copy-start | bytes 3076
  300.7 28.7 %copy-start.11 = (f32[1024,128]{1,0:T(8,128)}, f32[1024,128]{1,0:T(8,128)S(1)}, u32[]{:S(2)}) copy-start(f32[1024,128]{1,0:T(8,128)S(1)} %pad_maximum_fusion.3.cosine.refs_8_) | copy-start | bytes 1572868
  311.2 18.3 %copy-start.9 = (f32[1024,128]{1,0:T(8,128)}, f32[1024,128]{1,0:T(8,128)S(1)}, u32[]{:S(2)}) copy-start(f32[1024,128]{1,0:T(8,128)S(1)} %pad_maximum_fusion.4.sine.refs_9_) | copy-start | bytes 1572868
  329.4 50.2 %copy-start.23 = (bf16[768,1536]{1,0:T(8,128)(2,1)}, bf16[768,1536]{1,0:T(8,128)(2,1)S(1)}, u32[]{:S(2)}) copy-start(bf16[768,1536]{1,0:T(8,128)(2,1)S(1)} %get-tuple-element.95) | copy-start | bytes 7077892
  348.7 30.9 %copy-start.35 = (bf16[16,2304]{1,0:T(8,128)(2,1)}, bf16[16,2304]{1,0:T(8,128)(2,1)S(1)}, u32[]{:S(2)}) copy-start(bf16[16,2304]{1,0:T(8,128)(2,1)S(1)} %get-tuple-element.93.first.second.refs_3_.refs_4_) | copy-start | bytes 221188
  382.5 11.0 collective-permute-start
  418.3 5.9 collective-permute-start.1
  498.1 7.0 collective-permute-start.4
  500.3 4.1 collective-permute-start.5
  511.2 25.8 %copy-start.42 = (bf16[1024,1536]{1,0:T(8,128)(2,1)}, bf16[1024,1536]{1,0:T(8,128)(2,1)S(1)}, u32[]{:S(2)}) copy-start(bf16[1024,1536]{1,0:T(8,128)(2,1)S(1)} %get-tuple-element.357) | copy-start | bytes 9437188
  574.1 191.4 %reduce-scatter.21.cloned.1.call-start = ((), (), s32[]{:S(2)}) async-start(), calls=%async_computation.13 | async-start | bytes 11796480
  574.2 55.8 %copy-start.120 = (s32[1536]{0:T(1024)S(1)}, s32[1536]{0:T(1024)}, u32[]{:S(2)}) copy-start(s32[1536]{0:T(1024)} %copy-done.119) | copy-start | bytes 18436
  637.6 5.9 collective-permute-start.6
  667.6 197.6 %reduce-scatter.23.cloned.1.call-start = ((), (), s32[]{:S(2)}) async-start(), calls=%async_computation.14 | async-start | bytes 8847360
  692.3 5.7 collective-permute-start.7
  765.5 138.8 %reduce-scatter.13.cloned.1.call-start = ((), (), s32[]{:S(2)}) async-start(), calls=%async_computation.8 | async-start | bytes 2949120 | tf_op jit(solution)/shard_map/reduce_scatter | solution.py:2146
  802.5 294.6 %reduce-scatter.17.cloned.1.call-start = ((), (), s32[]{:S(2)}) async-start(), calls=%async_computation.10 | async-start | bytes 2211840 | tf_op jit(solution)/shard_map/reduce_scatter | solution.py:2146
  808.4 27.3 %copy-start.74 = (bf16[1024,2304]{1,0:T(8,128)(2,1)S(1)}, bf16[1024,2304]{1,0:T(8,128)(2,1)}, u32[]{:S(2)}) copy-start(bf16[1024,2304]{1,0:T(8,128)(2,1)} %copy-done.73) | copy-start | bytes 14155780
  834.7 57.6 %collective-permute-start.8 = (bf16[64,192,384]{2,1,0:T(8,128)(2,1)}, bf16[64,192,384]{2,1,0:T(8,128)(2,1)}, u32[]{:S(2)}, u32[]{:S(2)}) collective-permute-start(bf16[64,192,384]{2,1,0:T(8,128)(2,1)} %get-tuple-element.119), channel_id=1, source_target_pairs={{0,4},{4,0},{1,5},{5,1},{2,6},{6,2},{3,7},{7,3},{8,12},{12,8},{9,1... | collective-permute-start | bytes 28311560 | tf_op jit(solution)/shard_map/ppermute | solution.py:677
  847.2 26.2 %collective-permute-start.11 = (bf16[1024,1536]{1,0:T(8,128)(2,1)}, bf16[1024,1536]{1,0:T(8,128)(2,1)}, u32[]{:S(2)}, u32[]{:S(2)}) collective-permute-start(bf16[1024,1536]{1,0:T(8,128)(2,1)} %convolution_convert_fusion.1), channel_id=1, source_target_pairs={{0,4},{4,0},{1,5},{5,1},{2,6},{6,2},{3,7},{7,3},{8,12},{12,8},{9,1... | collective-permute-start | bytes 9437192 | tf_op jit(solution)/shard_map/ppermute | solution.py:677
  851.8 11.8 %collective-permute-start.9 = (bf16[2,192,1536]{2,1,0:T(8,128)(2,1)}, bf16[2,192,1536]{2,1,0:T(8,128)(2,1)}, u32[]{:S(2)}, u32[]{:S(2)}) collective-permute-start(bf16[2,192,1536]{2,1,0:T(8,128)(2,1)} %get-tuple-element.359), channel_id=1, source_target_pairs={{0,4},{4,0},{1,5},{5,1},{2,6},{6,2},{3,7},{7,3},{8,12},{12,8},{9,1... | collective-permute-start | bytes 3538952 | tf_op jit(solution)/shard_map/ppermute | solution.py:677
  865.2 235.4 %reduce-scatter.15.cloned.1.call-start = ((), (), s32[]{:S(2)}) async-start(), calls=%async_computation.9 | async-start | bytes 2949120 | tf_op jit(solution)/shard_map/reduce_scatter | solution.py:2146
  873.3 6.4 collective-permute-start.10
  1096.2 4.4 collective-permute-start.13
  1098.2 2.4 collective-permute-start.14
  1101.7 1.6 collective-permute-start.12
  (128 other events, 723.1 us)
Sparse Core Ops, SparseCore 0:
  12.1 204.3 all-gather.4
  219.8 140.1 all-gather.6
  363.3 120.7 all-gather.8
  574.3 93.1 reduce-scatter.18
  670.4 95.0 reduce-scatter.20
  768.4 76.7 reduce-scatter.22
  847.5 48.0 reduce-scatter.12
  897.9 37.8 reduce-scatter.16
  938.3 80.6 reduce-scatter.14

commit v6 on v5

--- a/solution.py
+++ b/solution.py
@@ -1127,7 +1127,6 @@
 
 
 FEED_TILE = 256
-UP_LOW = 768
 FEED_ROWS = 512
 
 
@@ -1166,30 +1165,19 @@
 
 
 def rows_back_kernel(
-    turned_rows, grad_gate, grad_up, gate_tile, up_tile, gate_out, up_low, up_high, rows_out, total
+    turned_rows, grad_gate, grad_up, gate_tile, up_tile, gate_out, up_out, rows_out, total
 ):
     @pl.when(pl.program_id(0) == 0)
     def clear():
         total[...] = jnp.zeros_like(total)
 
-    is_low = pl.program_id(0) < UP_LOW // FEED_TILE
-
     def body(at):
         gate_out[at, :] = jnp.dot(
             turned_rows[at, :], grad_gate[...], preferred_element_type=jnp.float32
         ).astype(gate_out.dtype)
-        up_part = jnp.dot(
+        up_out[at, :] = jnp.dot(
             turned_rows[at, :], grad_up[...], preferred_element_type=jnp.float32
-        ).astype(up_low.dtype)
-
-        @pl.when(is_low)
-        def store_low():
-            up_low[at, :] = up_part
-
-        @pl.when(jnp.logical_not(is_low))
-        def store_high():
-            up_high[at, :] = up_part
-
+        ).astype(up_out.dtype)
         total[:, at] += dot_back(grad_gate[...], gate_tile[at, :]) + dot_back(
             grad_up[...], up_tile[at, :]
         )
@@ -1210,14 +1198,6 @@
             return pl.BlockSpec((height, FEED_TILE), lambda step: (0, step))
         if kind == "rows":
             return pl.BlockSpec((FEED_TILE, width), lambda step: (step, 0))
-        if kind == "low":
-            last = width // FEED_TILE - 1
-            return pl.BlockSpec((height, FEED_TILE), lambda step: (0, jnp.minimum(step, last)))
-        if kind == "high":
-            first = (units - width) // FEED_TILE
-            return pl.BlockSpec(
-                (height, FEED_TILE), lambda step: (0, jnp.maximum(step - first, 0))
-            )
         return pl.BlockSpec(shape, lambda step: (0, 0))
 
     low = jnp.bfloat16
@@ -1272,8 +1252,7 @@
         ],
         [
             (gate_weight.shape, "columns"),
-            ((D, UP_LOW), "low"),
-            ((D, FF // 2 - UP_LOW), "high"),
+            (up_weight.shape, "columns"),
             (rows.shape, "whole"),
         ],
         8 * rows.size * (FF // 2),
@@ -1545,7 +1524,7 @@
 
 
 def attend_kernel(timed, queries, keys, values, first, second, mixed, logsum):
-    tile = 256 if timed else 512
+    tile = 512
 
     def body(step, carry):
         at = pl.ds(pl.multiple_of(step * tile, tile), tile)
@@ -1633,7 +1612,7 @@
         out_first[...] = jnp.zeros_like(out_first)
         out_second[...] = jnp.zeros_like(out_second)
 
-    tile = 256 if timed else 512
+    tile = 512
 
     def body(step, carry):
         at = pl.ds(pl.multiple_of(step * tile, tile), tile)
@@ -2130,7 +2109,7 @@
     grad_output = dot_back(grad_predicted, weight_out) + grad_audio[None, :] / FRAMES
     grad_low = grad_output.astype(bf16)
     grad_gate, grad_up, grad_down = hidden_back(grad_low, down, gate_part, up_part, hidden)
-    grad_gate_weight, grad_up_low, grad_up_high, grad_feed_rows = rows_back(
+    grad_gate_weight, grad_up_weight, grad_feed_rows = rows_back(
         feed_rows, grad_gate, grad_up, gate_weight, up_weight
     )
 
@@ -2199,28 +2178,22 @@
         grad_mixed_self,
         (cosine_table, sine_table),
     )
-    grad_gate_weight, down_total, _ = lax.optimization_barrier(
-        (grad_gate_weight, down_total, grad_cross_in)
-    )
-    gate_total = over_plane(grad_gate_weight, 48)
-    grad_up_high, gate_total, _ = lax.optimization_barrier(
-        (grad_up_high, gate_total, grad_queries)
-    )
-    up_total = over_plane(grad_up_high, 48)
-    gate_total, up_total = lax.optimization_barrier((gate_total, up_total))
-    down_total, *gate_totals = [
-        over_line(total) for total in (down_total, gate_total, up_total)
-    ]
-    feed_sums = [
-        (pick(both_rows, core), swap(pick(both_rows, 1 - core), "c")) for both_rows in gate_totals
-    ]
-    grad_down_low = down_total[0]
     grad_joined = jnp.concatenate([grad_queries, grad_keys, grad_values], 1)
     grad_time_pair = jnp.concatenate([grad_time_keys[:1], grad_time_values[:1]], 1)
     time_row = jnp.concatenate([jnp.zeros((1, half), f32), grad_time_pair], 1)
     grad_projection = (
         tdot(input_one, grad_joined) + input_time.astype(f32).reshape(D, 1) * time_row
     ).astype(bf16)
+    grad_gate_weight, down_total, _ = lax.optimization_barrier(
+        (grad_gate_weight, down_total, grad_cq)
+    )
+    gate_total = over_plane(grad_gate_weight, 48)
+    grad_up_weight, gate_total, _ = lax.optimization_barrier(
+        (grad_up_weight, gate_total, grad_projection)
+    )
+    up_total = over_plane(grad_up_weight, 48)
+    down_total = over_line(down_total)
+    grad_down_low = down_total[0]
     position = jnp.arange(256, dtype=jnp.int32)
     owner_core = core ^ (position // 128)
     block = assignment[
@@ -2250,6 +2223,13 @@
         on_both(partial_one), normed_one, inverse_one, gain_values[0]
     )
     grad_residual = (grad_residual + grad_after_self).astype(bf16)
+    gate_total, up_total, grad_residual = lax.optimization_barrier(
+        (gate_total, up_total, grad_residual)
+    )
+    feed_sums = []
+    for total in (gate_total, up_total):
+        both_rows = over_line(total)
+        feed_sums.append((pick(both_rows, core), swap(pick(both_rows, 1 - core), "c")))
     grad_embeds, gain_time = layer_back(
         grad_input_time, normed_time, inverse_time, gain_values[0]
     )
@@ -2281,12 +2261,8 @@
         ("cols", (16, 1152)),
         ("one", (16, D)),
         ("one", (48, 2 * DIN)),
-        ("one", (96, UP_LOW)),
-    )
-    rest_groups = [
-        ((7, 0, whole, pl.ds(0, UP_LOW // 2)), (7, 1, whole, pl.ds(UP_LOW // 2, UP_LOW // 2)))
-    ]
-    rest_groups += [((3, 0, whole, whole), (4, 1, whole, whole))]
+    )
+    rest_groups = [((3, 0, whole, whole), (4, 1, whole, whole))]
     rest_groups += [
         ((1, 0, whole, pl.ds(step * 384, 384)), (2, 1, whole, pl.ds(step * 768, 768)))
         for step in range(2)
@@ -2307,19 +2283,15 @@
             kv_sources[1],
             small.astype(bf16).reshape(4, 1, 4, 16, D),
             grad_ends.reshape(4, 1, 4, 48, 2 * DIN),
-            grad_up_low.reshape(4, 1, 4, 96, UP_LOW),
         ),
         2,
     )
     grad_down = grad_down_low.astype(f32)
-    up_sums = rest_sums[-1].reshape(2, 48, UP_LOW)
     slot_pairs = rest_sums[0].reshape(4, BLK, 2 * BLK)
     grad_cross_query, grad_cross_out, *kv_sums, small, grad_ends = (
-        value.astype(f32) for value in rest_sums[1:-1]
+        value.astype(f32) for value in rest_sums[1:]
     )
     gate_sides, (up_own, up_other) = feed_sums
-    up_own = jnp.concatenate([pick(up_sums, core), up_own], 1)
-    up_other = jnp.concatenate([swap(pick(up_sums, 1 - core), "c"), up_other], 1)
     gate_columns = []
     for mine, other in (gate_sides, (up_own, up_other)):
         sides = (jnp.where(core == 0, mine, other), jnp.where(core == 0, other, mine))
@@ -2352,7 +2324,7 @@
         0.0,
     )
     totals = total_squares(
-        loss_part, (*rest_sums[:-1], *gate_sides, up_own, up_other, grad_down_low), 4
+        loss_part, (*rest_sums, *gate_sides, up_own, up_other, grad_down_low), 4
     )
     loss_total, norm_square = totals[0, 0], totals[0, 1]
     return finish(

time: 1160 us -> 1160 us (level)
  waiting for transfers between devices: 48.6 us -> 78.3 us
  Pallas kernels: 773 us -> 746 us
  local copies, waits for them, and re-layouts: 85.7 us -> 69.2 us
    optimization_barrier x3, waiting for transfers between devices: 16.1 us -> 46.4 us  [the longest x1 36.2 us: item_per_chip(): lax.optimization_barrier((gate_total, up_total, grad_residual))]
    pallas_call x1, Pallas kernels: 191 us -> 175 us  [reduce_gradients(): pl.pallas_call(partial(reduce_kernel, arrays, groups), out_shape=out_shap...]
    unnamed x298 -> x271, local copies, waits for them, and re-layouts: 28 us -> 20.7 us
  transfers between devices with their start and end apart: 24 -> 23, of which waited for: 9 -> 10; matrix products, arithmetic and copies ran while one was open for 19% -> 20% of each run, Pallas kernels for 62% -> 60%
where the time goes in v6:
time: 1160 us; the launch traced here: 1150 us
  Pallas kernels  746 us (64%)
  matrix products  124 us (11%)
  other arithmetic  104 us (9%)
  waiting for transfers between devices  78.3 us (7%)
  local copies, waits for them, and re-layouts  69.2 us (6%)
  between operations  24 us (2%)
    pallas_call x1, Pallas kernels, gather_weights(): pl.pallas_call(partial(gather_kernel, arrays, groups), out_shape=[jax.Sha...  265 us
    pallas_call x1, Pallas kernels, reduce_gradients(): pl.pallas_call(partial(reduce_kernel, arrays, groups), out_shape=out_shap...  175 us
    pallas_call x3, Pallas kernels, feed_call(): pl.pallas_call(kernel, grid=(units // FEED_TILE,), in_specs=[spec(value.s...  103 us
    pallas_call x2, Pallas kernels, attend_back(): pl.pallas_call(partial(attend_back_kernel, timed), grid=(pairs,), in_spec...  57.3 us
    dot_general x7, matrix products, dot_back(): lax.dot_general(left, right, (((1,), (1,)), ((), ())), preferred_element_...  42.1 us
    pallas_call x2, Pallas kernels, attend(): pl.pallas_call(partial(attend_kernel, timed), grid=(pairs,), in_specs=[la...  39.3 us
    optimization_barrier x1, waiting for transfers between devices, item_per_chip(): lax.optimization_barrier((gate_total, up_total, grad_residual))  36.2 us
    dot_general x8, matrix products, tdot(): lax.dot_general(left, right, (((0,), (0,)), ((), ())), preferred_element_...  35.2 us
  transfers between devices with their start and end apart: 23, of which 10 were waited for; matrix products, arithmetic and copies ran while one was open for 20% of the time, Pallas kernels for 60%

profile of v6, /device:TPU:0, one launch (start us, length us, event | category | flops | bytes accessed | tf_op | source)
XLA Modules:
  0.0 1150.8 jit_solution(4724744510950752983)
XLA Ops:
  26.5 264.7 %shard_map.520 = (bf16[4,2,4,16,1536]{4,3,2,1,0:T(8,128)(2,1)}, bf16[4,2,4,768,384]{4,3,2,1,0:T(8,128)(2,1)}, bf16[4,2,4,48,768]{4,3,2,1,0:T(8,128)(2,1)}, bf16[...) custom-call(bf16[16,1536]{1,0:T(8,128)(2,1)} %fusion.52.refs_0_, ...), custom_call_target="tpu_custom_call" | custom-call | tf_op jit(solution)/shard_map/pallas_call | solution.py:920
  312.6 16.2 %shard_map.521 = (bf16[1536,2304]{1,0:T(8,128)(2,1)}, bf16[768,1536]{1,0:T(8,128)(2,1)S(1)}) custom-call(s32[96]{0:T(128)S(1)} %gather_fusion, s32[32]{0:T(128)S(1)} %gather_fusion.1, bf16[128,192,384]{2,1,0:T(8,128)(2,1)} %bitcast.178), custom_call_target="tpu_custom_call" | custom-call | bytes 28311552 | tf_op jit(solution)/shard_map/pallas_call | solution.py:1749
  328.9 19.1 %shard_map.522 = (bf16[1024,2304]{1,0:T(8,128)(2,1)}, bf16[16,2304]{1,0:T(8,128)(2,1)S(1)}) custom-call(bf16[1024,1536]{1,0:T(8,128)(2,1)S(1)} %multiply_convert_fusion.2.rows, bf16[16,1536]{1,0:T(8,128)(2,1)S(1)} %pad.21.times, bf16[1536,2304]{1,0:T(8,128)(2,1)} %get-tuple-element.90.weights, f32[1024,128]{1,0:T(8,128)S(1)} %pad_maximum_fusion.3.cosine.refs_8_, ...), custom_call_target="tpu_custom_call" | custom-call | flops 7247757312 | bytes 14942208 | tf_op jit(solution)/shard_map/pallas_call | solution.py:1495
  348.0 29.2 %shard_map.523 = (bf16[1024,768]{1,0:T(8,128)(2,1)S(1)}, f32[1024,768]{1,0:T(8,128)S(1)}) custom-call(bf16[1024,2304]{1,0:T(8,128)(2,1)} %get-tuple-element.91.queries.keys.values.refs_0_.refs_1_.refs_2_, bf16[1024,2304]{1,0:T(8,128)(2,1)} %get-tuple-element.91.queries.keys.values.refs_0_.refs_1_.refs_2_, ...), custom_call_target="tpu_custom_call" | custom-call | flops 19327352832 | bytes 11010048 | tf_op jit(solution)/shard_map/pallas_call | solution.py:1580
  390.3 6.2 fusion.130
  403.6 10.1 shard_map.524
  423.9 6.8 fusion.129
  436.6 7.0 fusion.10
  448.3 26.3 %shard_map.525 = (bf16[1024,3072]{1,0:T(8,128)(2,1)}, bf16[1024,3072]{1,0:T(8,128)(2,1)}, bf16[1024,3072]{1,0:T(8,128)(2,1)}) custom-call(bf16[1024,1536]{1,0:T(8,128)(2,1)} %copy.197.rows, bf16[1536,3072]{1,0:T(8,128)(2,1)} %bitcast.213, bf16[1536,3072]{1,0:T(8,128)(2,1)} %bitcast.215), custom_call_target="tpu_custom_call" | custom-call | flops 19327352832 | bytes 40894464 | tf_op jit(solution)/shard_map/pallas_call | solution.py:1205
  474.6 9.5 all-gather.9.cloned.1.call-done.down_tile
  484.1 15.5 %convolution_convert_fusion = bf16[1024,1536]{1,0:T(8,128)(2,1)} fusion(bf16[1024,3072]{1,0:T(8,128)(2,1)} %get-tuple-element.101.hidden, bf16[3072,1536]{1,0:T(8,128)(2,1)} %all-gather.9.cloned.1.call-done.down_tile), kind=kOutput, calls=%fused_computation.38 | convolution fusion | flops 9665249280 | bytes 18874368 | tf_op jit(solution)/shard_map/dot_general | solution.py:2059
  505.6 7.7 fusion.13
  513.9 11.2 shard_map.526
  541.0 28.8 %shard_map.527 = (bf16[1024,3072]{1,0:T(8,128)(2,1)}, bf16[1024,3072]{1,0:T(8,128)(2,1)}, bf16[3072,1536]{1,0:T(8,128)(2,1)}) custom-call(bf16[1024,1536]{1,0:T(8,128)(2,1)} %get-tuple-element.412.grad, bf16[3072,1536]{1,0:T(8,128)(2,1)} %all-gather.9.cloned.1.call-done.down_tile, bf16[1024,3072]{1,0:T(8,128)(2,1)} %get-tuple-element.104.gate, ...), custom_call_target="tpu_custom_call" | custom-call | flops 19327352832 | bytes 53477376 | tf_op jit(solution)/shard_map/pallas_call | solution.py:1205
  569.9 47.8 %shard_map.528 = (bf16[1536,3072]{1,0:T(8,128)(2,1)}, bf16[1536,3072]{1,0:T(8,128)(2,1)}, bf16[1024,1536]{1,0:T(8,128)(2,1)}) custom-call(bf16[1536,1024]{1,0:T(8,128)(2,1)} %bitcast.186, bf16[1024,3072]{1,0:T(8,128)(2,1)} %get-tuple-element.106.grad_gate, bf16[1024,3072]{1,0:T(8,128)(2,1)} %get-tuple-element.107.grad_up, bf16[1536,3072]{1,0:T(8,128)(2,1)} %bitcast.214, ...), custom_call_target="tpu_custom_call" | custom-call | flops 38654705664 | bytes 56623104 | tf_op jit(solution)/shard_map/pallas_call | solution.py:1205
  617.7 8.7 fusion.11.mine
  633.1 14.4 %shard_map.529 = (f32[1024,1536]{1,0:T(8,128)}, bf16[1024,1536]{1,0:T(8,128)(2,1)}, f32[8,1536]{1,0:T(8,128)}) custom-call(bf16[1024,1536]{1,0:T(8,128)(2,1)} %fusion.11.mine, bf16[1024,1536]{1,0:T(8,128)(2,1)} %collective-permute-done.6.other, f32[1024,1536]{1,0:T(8,128)} %copy-done.33, f32[1024,1]{1,0:T(8,128)} %copy.202.inverse, ...), custom_call_target="tpu_custom_call" | custom-call | flops 25165824 | bytes 28311552 | tf_op jit(solution)/shard_map/pallas_call | solution.py:1112
  647.5 6.5 fusion.22.refs_7_
  654.1 12.3 %shard_map.530 = (bf16[1024,768]{1,0:T(8,128)(2,1)S(1)}, f32[128,768]{1,0:T(8,128)S(1)}, f32[128,768]{1,0:T(8,128)S(1)}) custom-call(bf16[1024,768]{1,0:T(8,128)(2,1)S(1)} %copy-done.22, bf16[128,1536]{1,0:T(8,128)(2,1)S(1)} %convolution_convert_fusion.8.keys.values.refs_1_.refs_2_, ...), custom_call_target="tpu_custom_call" | custom-call | flops 6039797760 | bytes 13369344 | tf_op jit(solution)/shard_map/pallas_call | solution.py:1707
  692.6 45.0 %shard_map.531 = (bf16[1024,768]{1,0:T(8,128)(2,1)S(1)}, bf16[1024,768]{1,0:T(8,128)(2,1)S(1)}, bf16[1024,768]{1,0:T(8,128)(2,1)S(1)}, f32[8,768]{1,0:T(8,128)S(1)}, f32[8,768]{1,0:T(8,128)S(1)}) custom-call(bf16[1024,2304]{1,0:T(8,128)(2,1)} %get-tuple-element.91.queries.keys.values.refs_0_.refs_1_.refs_2_, ...), custom_call_target="tpu_custom_call" | custom-call | flops 48318382080 | bytes 18874368 | tf_op jit(solution)/shard_map/pallas_call | solution.py:1707
  741.5 9.6 add_convert_fusion.1.joined
  751.1 10.2 reduce-scatter.21.cloned.1.call-done
  761.4 12.5 %convolution_convert_fusion.1 = bf16[1024,1536]{1,0:T(8,128)(2,1)} fusion(bf16[1024,2304]{1,0:T(8,128)(2,1)} %copy-done.61, bf16[1536,2304]{1,0:T(8,128)(2,1)} %get-tuple-element.90.weights), kind=kOutput, calls=%fused_computation.41 | convolution fusion | flops 7249330176 | bytes 14942208 | tf_op jit(solution)/shard_map/dot_general | solution.py:701
  776.0 6.4 convolution_convert_fusion.7.mix
  782.4 26.7 %shard_map.532 = (bf16[64,192,384]{2,1,0:T(8,128)(2,1)}, bf16[64,192,384]{2,1,0:T(8,128)(2,1)}) custom-call(s32[256]{0:T(256)S(1)} %get-tuple-element.403.rows_at, s32[256]{0:T(256)S(1)} %get-tuple-element.402.columns_at, s32[256]{0:T(256)S(1)} %get-tuple-element.349.sides, bf16[1536,2304]{1,0:T(8,128)(2,1)} %add_convert_fusion.1.joined, ...), custom_call_target="tpu_custom_call" | custom-call | bytes 56623104 | tf_op jit(solution)/shard_map/pallas_call | solution.py:1813
  809.8 7.4 multiply_reduce_fusion
  823.1 36.2 %reduce-scatter.23.cloned.1.call-done = bf16[1,4,2,48,3072]{4,3,2,1,0:T(8,128)(2,1)} async-done(((bf16[4,4,2,48,3072]{4,3,2,1,0:T(8,128)(2,1)}), bf16[1,4,2,48,3072]{4,3,2,1,0:T(8,128)(2,1)}) %reduce-scatter.23.cloned.1.call-update) | async-done | bytes 2359312 | tf_op jit(solution)/shard_map/optimization_barrier | solution.py:2226
  883.5 6.1 convolution_convert_fusion.6
  903.1 12.3 %add_convert_fusion = bf16[64,192,384]{2,1,0:T(8,128)(2,1)} fusion(bf16[64,192,384]{2,1,0:T(8,128)(2,1)} %collective-permute-done.8, bf16[64,192,384]{2,1,0:T(8,128)(2,1)} %get-tuple-element.117), kind=kLoop, calls=%fused_computation.4 | loop fusion | flops 18874368 | bytes 28311552 | tf_op jit(solution)/shard_map/convert_element_type | solution.py:2213
  919.6 175.1 %shard_map.533 = (bf16[768,384]{1,0:T(8,128)(2,1)}, bf16[48,1536]{1,0:T(8,128)(2,1)}, bf16[48,1536]{1,0:T(8,128)(2,1)}, bf16[16,2304]{1,0:T(8,128)(2,1)}, bf16[1...) custom-call(bf16[4,1,4,768,384]{4,3,2,1,0:T(8,128)(2,1)} %bitcast.175, ...), custom_call_target="tpu_custom_call" | custom-call | tf_op jit(solution)/shard_map/pallas_call | solution.py:1439
  1104.7 9.6 shard_map.534
  1132.8 9.8 shard_map.535
  (551 shorter events, 211.8 us)
Async XLA Ops:
  7.2 441.1 %all-gather.5.cloned.1.call-start = ((), (), s32[]{:S(2)}) async-start(), calls=%async_computation.6 | async-start | bytes 10027008 | tf_op jit(solution)/shard_map/all_gather | solution.py:1914
  9.3 1.7 collective-permute-start.2
  11.9 436.3 %all-gather.7.cloned.1.call-start = ((), (), s32[]{:S(2)}) async-start(), calls=%async_computation.7 | async-start | bytes 10027008 | tf_op jit(solution)/shard_map/all_gather | solution.py:1914
  12.0 1.6 collective-permute-start.3
  14.6 469.5 %all-gather.9.cloned.1.call-start = ((), (), s32[]{:S(2)}) async-start(), calls=%async_computation.11 | async-start | bytes 10027008 | tf_op jit(solution)/shard_map/all_gather | solution.py:1914
  15.5 652.0 %reduce-scatter.19.cloned.1.call-start = ((), (), s32[]{:S(2)}) async-start(), calls=%async_computation.12 | async-start | bytes 11796480
  23.2 270.5 %copy-start.28 = (s32[256]{0:T(256)S(1)}, s32[256]{0:T(256)}, u32[]{:S(2)}) copy-start(s32[256]{0:T(256)} %param.39) | copy-start | bytes 3076
  328.9 48.3 %copy-start.16 = (bf16[768,1536]{1,0:T(8,128)(2,1)}, bf16[768,1536]{1,0:T(8,128)(2,1)S(1)}, u32[]{:S(2)}) copy-start(bf16[768,1536]{1,0:T(8,128)(2,1)S(1)} %get-tuple-element.94) | copy-start | bytes 7077892
  348.0 29.2 %copy-start.26 = (bf16[16,2304]{1,0:T(8,128)(2,1)}, bf16[16,2304]{1,0:T(8,128)(2,1)S(1)}, u32[]{:S(2)}) copy-start(bf16[16,2304]{1,0:T(8,128)(2,1)S(1)} %get-tuple-element.92.first.second.refs_3_.refs_4_) | copy-start | bytes 221188
  381.7 8.6 collective-permute-start
  417.9 6.0 collective-permute-start.1
  499.6 6.0 collective-permute-start.4
  501.0 4.2 collective-permute-start.5
  569.9 191.4 %reduce-scatter.21.cloned.1.call-start = ((), (), s32[]{:S(2)}) async-start(), calls=%async_computation.13 | async-start | bytes 11796480
  626.5 6.0 collective-permute-start.6
  667.6 191.7 %reduce-scatter.23.cloned.1.call-start = ((), (), s32[]{:S(2)}) async-start(), calls=%async_computation.14 | async-start | bytes 11796480
  672.4 5.7 collective-permute-start.7
  761.3 154.1 %reduce-scatter.13.cloned.1.call-start = ((), (), s32[]{:S(2)}) async-start(), calls=%async_computation.8 | async-start | bytes 2949120 | tf_op jit(solution)/shard_map/reduce_scatter | solution.py:2125
  773.9 35.9 %collective-permute-start.11 = (bf16[1024,1536]{1,0:T(8,128)(2,1)}, bf16[1024,1536]{1,0:T(8,128)(2,1)}, u32[]{:S(2)}, u32[]{:S(2)}) collective-permute-start(bf16[1024,1536]{1,0:T(8,128)(2,1)} %convolution_convert_fusion.1), channel_id=1, source_target_pairs={{0,4},{4,0},{1,5},{5,1},{2,6},{6,2},{3,7},{7,3},{8,12},{12,8},{9,1... | collective-permute-start | bytes 9437192 | tf_op jit(solution)/shard_map/ppermute | solution.py:677
  773.9 326.5 %reduce-scatter.15.cloned.1.call-start = ((), (), s32[]{:S(2)}) async-start(), calls=%async_computation.9 | async-start | bytes 2949120 | tf_op jit(solution)/shard_map/reduce_scatter | solution.py:2125
  776.0 41.1 %slice-start.4 = ((s8[6291456]{0:T(1024)(128)(4,1)}), s8[4194304]{0:T(1024)(128)(4,1)S(1)}, s32[]{:S(2)}) async-start(s8[6291456]{0:T(1024)(128)(4,1)} %bitcast.176), calls=%async_computation.19 | async-start | bytes 8388608
  782.4 34.8 %slice-start.5 = ((s8[6291456]{0:T(1024)(128)(4,1)}), s8[2097152]{0:T(1024)(128)(4,1)S(1)}, s32[]{:S(2)}) async-start(s8[6291456]{0:T(1024)(128)(4,1)} %bitcast.176), calls=%async_computation.20 | async-start | bytes 4194304
  809.2 94.0 %collective-permute-start.8 = (bf16[64,192,384]{2,1,0:T(8,128)(2,1)}, bf16[64,192,384]{2,1,0:T(8,128)(2,1)}, u32[]{:S(2)}, u32[]{:S(2)}) collective-permute-start(bf16[64,192,384]{2,1,0:T(8,128)(2,1)} %get-tuple-element.118), channel_id=1, source_target_pairs={{0,4},{4,0},{1,5},{5,1},{2,6},{6,2},{3,7},{7,3},{8,12},{12,8},{9,1... | collective-permute-start | bytes 28311560 | tf_op jit(solution)/shard_map/ppermute | solution.py:677
  817.2 42.4 %copy-start.100 = (f32[16]{0:T(128)S(1)}, f32[16]{0:T(128)}, u32[]{:S(2)}) copy-start(f32[16]{0:T(128)} %copy-done.99) | copy-start | bytes 196
  817.2 42.4 %copy-start.105 = (f32[16]{0:T(128)S(1)}, f32[16]{0:T(128)}, u32[]{:S(2)}) copy-start(f32[16]{0:T(128)} %copy-done.104) | copy-start | bytes 196
  817.2 42.4 %copy-start.108 = (f32[16]{0:T(128)S(1)}, f32[16]{0:T(128)}, u32[]{:S(2)}) copy-start(f32[16]{0:T(128)} %get-tuple-element.319) | copy-start | bytes 196
  817.2 44.3 %copy-start.43 = (f32[1024,64]{0,1:T(8,128)S(1)}, f32[1024,64]{0,1:T(8,128)}, u32[]{:S(2)}) copy-start(f32[1024,64]{0,1:T(8,128)} %copy-done.42) | copy-start | bytes 786436
  859.3 242.1 %reduce-scatter.17.cloned.1.call-start = ((), (), s32[]{:S(2)}) async-start(), calls=%async_computation.10 | async-start | bytes 2949120 | tf_op jit(solution)/shard_map/reduce_scatter | solution.py:2125
  873.2 16.4 %collective-permute-start.9 = (bf16[2,192,1536]{2,1,0:T(8,128)(2,1)}, bf16[2,192,1536]{2,1,0:T(8,128)(2,1)}, u32[]{:S(2)}, u32[]{:S(2)}) collective-permute-start(bf16[2,192,1536]{2,1,0:T(8,128)(2,1)} %get-tuple-element.359), channel_id=1, source_target_pairs={{0,4},{4,0},{1,5},{5,1},{2,6},{6,2},{3,7},{7,3},{8,12},{12,8},{9,1... | collective-permute-start | bytes 3538952 | tf_op jit(solution)/shard_map/ppermute | solution.py:677
  897.2 2.5 collective-permute-start.10
  1101.3 1.8 collective-permute-start.12
  1102.6 1.7 collective-permute-start.13
  (114 other events, 740.1 us)
Sparse Core Ops, SparseCore 0:
  12.1 204.3 all-gather.4
  219.8 140.0 all-gather.6
  363.3 120.7 all-gather.8
  570.0 93.2 reduce-scatter.18
  667.7 93.5 reduce-scatter.20
  764.2 95.0 reduce-scatter.22
  861.6 48.0 reduce-scatter.12
  912.0 47.8 reduce-scatter.14
  962.1 79.5 reduce-scatter.16
